TPU v7x, 32 devices: a whole 2x2x4 slice. The times are simulated.
32 devices in a mesh: dp: 4 (over y, core), point: 8 (over z, x).
Axes of the slice: x: 2, y: 2, z: 4, core: 2. Of those that a mesh axis runs over, the one named last changes fastest.
Arguments:
- inputs: float32 [4, 4096, 256], P('dp', 'point'), may hold values from -6 to 6
- cotangent: float32 [4, 4096, 256], P('dp', 'point'), may hold values from -6 to 6
- gain_one: float32 [256], replicated, may hold values from 0.5 to 1.5
- fx_weight: float32 [256, 256], replicated, may hold values from -0.375 to 0.375
- x_weight: float32 [256, 256], replicated, may hold values from -0.375 to 0.375
- slice_logit_weight: float32 [32, 64], replicated, may hold values from -2 to 2
- temper: float32 [8], replicated, may hold values from 0.5 to 2
- slice_query_matrix: float32 [32, 32], replicated, may hold values from -1.5 to 1.5
- slice_key_matrix: float32 [32, 32], replicated, may hold values from -1.5 to 1.5
- slice_value_matrix: float32 [32, 32], replicated, may hold values from -1 to 1
- out_weight: float32 [256, 256], replicated, may hold values from -0.375 to 0.375
- gain_two: float32 [256], replicated, may hold values from 0.5 to 1.5
- expand_weight: float32 [256, 256], replicated, may hold values from -0.375 to 0.375
- down_weight: float32 [256, 256], replicated, may hold values from -0.375 to 0.375
Outputs:
- input_grad: float32 [4, 4096, 256], P('dp', 'point')
- matrix_grads: float32 [5, 256, 256], replicated
- attention_gradient_set: float32 [3, 32, 32], replicated
- slice_grad: float32 [32, 64], replicated
- gain_grads: float32 [2, 256], replicated
All inputs are finite; a program needn't handle non-finite values.
Results may differ from a plain program's by a relative error of at most 0.00016.
Values sent between devices are 32-bit elements; how exact they have to be, the bound alone decides.
No kernel may reach another device: no remote copies, remote signals or barrier semaphores. Data moves between devices by JAX's collectives and lax.ppermute only.
A program may use at most 64 MiB of HBM per device.

v0:
```python
import jax
import jax.numpy as jnp
from jax import lax
from jax.sharding import PartitionSpec as P


def matmul(left, right):
    return jnp.dot(left, right, precision=lax.Precision.HIGHEST)


def normed(value_rows, gain):
    centre = value_rows - jnp.mean(value_rows, axis=-1, keepdims=True)
    spread_back = jnp.mean(centre * centre, axis=-1, keepdims=True)
    return centre * lax.rsqrt(spread_back + 1e-05) * gain


def front(rows, gain_one, fx_weight, x_weight, slice_logit_weight, temper):
    count = rows.shape[0]
    heads = temper.shape[0]
    normal = normed(rows, gain_one)
    feature_columns = jnp.einsum(
        "pc,ce->ep", normal, fx_weight, precision=lax.Precision.HIGHEST
    ).reshape(heads, -1, count)
    assign_cols = jnp.einsum(
        "pc,ce->ep", normal, x_weight, precision=lax.Precision.HIGHEST
    ).reshape(heads, -1, count)
    slice_logit_rows = jnp.einsum(
        "hdp,dm->hmp", assign_cols, slice_logit_weight, precision=lax.Precision.HIGHEST
    )
    slice_membership_weights = jax.nn.softmax(slice_logit_rows / temper[:, None, None], axis=1)
    total = jnp.sum(slice_membership_weights, axis=2)
    summed_tokens = jnp.einsum(
        "fiz,flz->fil", slice_membership_weights, feature_columns, precision=lax.Precision.HIGHEST
    )
    return (slice_membership_weights, summed_tokens, total)


def middle(summed_tokens, total, slice_query_matrix, slice_key_matrix, slice_value_matrix):
    slice_tokens = summed_tokens / (total[:, :, None] + 1e-05)
    query_rows = jnp.einsum(
        "plq,qz->plz", slice_tokens, slice_query_matrix, precision=lax.Precision.HIGHEST
    )
    key_rows = jnp.einsum(
        "plq,qz->plz", slice_tokens, slice_key_matrix, precision=lax.Precision.HIGHEST
    )
    value_rows = jnp.einsum(
        "plq,qz->plz", slice_tokens, slice_value_matrix, precision=lax.Precision.HIGHEST
    )
    score_logits = jnp.einsum("aot,azt->aoz", query_rows, key_rows, precision=lax.Precision.HIGHEST)
    score_logits = score_logits * query_rows.shape[-1] ** (-0.5)
    attention_probs = jax.nn.softmax(score_logits, axis=-1)
    return jnp.einsum("ecg,ego->eco", attention_probs, value_rows, precision=lax.Precision.HIGHEST)


def back(
    rows,
    slice_membership_weights,
    slice_result_rows,
    out_weight,
    gain_two,
    expand_weight,
    down_weight,
):
    spread_cols = jnp.einsum(
        "azc,azb->abc", slice_membership_weights, slice_result_rows, precision=lax.Precision.HIGHEST
    )
    spread_cols = spread_cols.reshape(-1, rows.shape[0])
    mixed = rows + jnp.einsum("cp,ce->pe", spread_cols, out_weight, precision=lax.Precision.HIGHEST)
    hidden = jax.nn.gelu(matmul(normed(mixed, gain_two), expand_weight))
    return mixed + matmul(hidden, down_weight)


def shards(
    inputs,
    cotangent,
    gain_one,
    fx_weight,
    x_weight,
    slice_logit_weight,
    temper,
    slice_query_matrix,
    slice_key_matrix,
    slice_value_matrix,
    out_weight,
    gain_two,
    expand_weight,
    down_weight,
):
    rows = inputs[0]
    width = rows.shape[1]
    head_size = slice_logit_weight.shape[0]
    slices = slice_logit_weight.shape[1]

    def front_local(local_rows, g_one, w_fx, w_x, w_slice):
        return front(local_rows, g_one, w_fx, w_x, w_slice, temper)

    (slice_membership_weights, partial_summed_block, total_part), front_pull = jax.vjp(
        front_local, rows, gain_one, fx_weight, x_weight, slice_logit_weight
    )
    summed_tokens, total = lax.psum((partial_summed_block, total_part), "point")
    slice_result_rows, middle_pull = jax.vjp(
        middle, summed_tokens, total, slice_query_matrix, slice_key_matrix, slice_value_matrix
    )
    output, back_pull = jax.vjp(
        back,
        rows,
        slice_membership_weights,
        slice_result_rows,
        out_weight,
        gain_two,
        expand_weight,
        down_weight,
    )
    grad_rows_b, grad_weights, grad_out_part, w_out, g_two, w_up, w_down = back_pull(cotangent[0])
    grad_out = lax.psum(grad_out_part, "point")
    grad_summed, grad_total, w_query, w_key, w_value = middle_pull(grad_out)
    grad_rows_a, g_one, w_fx, w_x, w_slice = front_pull((grad_weights, grad_summed, grad_total))
    input_grad = (grad_rows_a + grad_rows_b)[None]
    keep = (lax.axis_index("point") == 0).astype(jnp.float32)
    factor = 1.0 / jnp.sqrt(
        jnp.float32(rows.shape[0] * lax.axis_size("point") * lax.axis_size("dp"))
    )
    flat = (
        jnp.concatenate(
            [
                jnp.stack([w_fx, w_x, w_out, w_up, w_down]).ravel(),
                jnp.stack([w_query, w_key, w_value]).ravel() * keep,
                w_slice.ravel(),
                jnp.stack([g_one, g_two]).ravel(),
            ]
        )
        * factor
    )
    summed_all = lax.psum(flat, ("dp", "point"))
    first = 5 * width * width
    second = first + 3 * head_size * head_size
    third = second + head_size * slices
    matrix_grads = summed_all[:first].reshape(5, width, width)
    attention_gradient_set = summed_all[first:second].reshape(3, head_size, head_size)
    slice_grad = summed_all[second:third].reshape(head_size, slices)
    gain_grads = summed_all[third:].reshape(2, width)
    return (input_grad, matrix_grads, attention_gradient_set, slice_grad, gain_grads)


def solution(mesh):
    placed = (
        P("dp", "point", None),
        P("dp", "point", None),
        P(),
        P(),
        P(),
        P(),
        P(),
        P(),
        P(),
        P(),
        P(),
        P(),
        P(),
        P(),
    )
    return jax.shard_map(
        shards,
        mesh=mesh,
        in_specs=placed,
        out_specs=(P("dp", "point", None), P(), P(), P(), P()),
        check_vma=False,
    )
```

profile of v0, /device:TPU:0, one launch (start us, length us, event | category | flops | bytes accessed | tf_op | source)
XLA Modules:
  0.0 336.3 jit_solution(13277153155570920731)
XLA Ops:
  7.3 1.3 copy.19
  10.5 1.1 bitcast_reduce_fusion
  11.8 1.8 fusion.100
  14.0 23.3 %psum.29 = f32[8,64]{1,0:T(8,128)S(1)} all-reduce(f32[8,64]{1,0:T(8,128)S(1)} %fusion.99), channel_id=1, replica_groups=mesh['dp'=4,'point'=8] {'point'}, use_global_device_ids=true, to_apply=%region_6.0 | all-reduce | flops 512 | bytes 4096 | tf_op jit(solution)/shard_map/psum | solution.py:100
  38.4 47.9 %all-reduce.4.cloned.1.call-done = f32[8,64,32]{1,2,0:T(8,128)} async-done(((f32[8,64,32]{1,2,0:T(8,128)}), f32[8,64,32]{1,2,0:T(8,128)}) %all-reduce.4.cloned.1.call-update) | async-done | bytes 65552 | tf_op jit(solution)/shard_map/psum | solution.py:100
  86.3 1.3 fusion.76
  87.6 1.3 fusion.79
  92.4 1.1 fusion.29
  98.1 1.8 fusion.95
  99.9 3.1 fusion.105
  103.3 68.8 %all-reduce.6.cloned.1.call-done = f32[8,64,32]{1,2,0:T(8,128)} async-done(((f32[8,64,32]{1,2,0:T(8,128)}), f32[8,64,32]{1,2,0:T(8,128)}) %all-reduce.6.cloned.1.call-update) | async-done | bytes 65552 | tf_op jit(solution)/shard_map/psum | solution.py:115
  172.2 1.8 multiply_reduce_fusion.7
  173.9 1.4 fusion.92
  177.5 1.6 fusion.70
  179.0 1.3 multiply_reduce_fusion
  184.0 1.7 fusion.106
  185.7 1.2 fusion.4
  187.8 1.1 fusion.3
  190.6 1.1 fusion
  192.4 1.2 maximum_multiply_fusion
  193.6 1.0 copy-done.3
  195.8 127.8 %all-reduce.8.cloned.1.call-done = f32[333312]{0:T(1024)} async-done(((f32[333312]{0:T(1024)}), f32[333312]{0:T(1024)}) %all-reduce.8.cloned.1.call-update) | async-done | bytes 1333264 | tf_op jit(solution)/shard_map/psum | solution.py:134
  326.3 1.3 slice-done
  327.6 1.4 reshape.211
  (159 shorter events, 24.9 us)
Async XLA Ops:
  7.2 85.3 %copy-start = (f32[256,256]{1,0:T(8,128)S(1)}, f32[256,256]{1,0:T(8,128)}, u32[]{:S(2)}) copy-start(f32[256,256]{1,0:T(8,128)} %param.26) | copy-start | bytes 786436
  7.2 1.7 copy-start.35
  7.2 79.1 %all-reduce.4.cloned.1.call-start = ((), (), s32[]{:S(2)}) async-start(), calls=%async_computation | async-start | bytes 262144 | tf_op jit(solution)/shard_map/psum | solution.py:100
  9.7 2.1 copy-start.17
  13.6 23.7 %copy-start.23 = (f32[1,512,256]{2,1,0:T(8,128)S(1)}, f32[1,512,256]{2,1,0:T(8,128)}, u32[]{:S(2)}) copy-start(f32[1,512,256]{2,1,0:T(8,128)} %param.15) | copy-start | bytes 1572868
  13.6 72.6 %copy-start.39 = (f32[32,32]{1,0:T(8,128)S(1)}, f32[32,32]{1,0:T(8,128)}, u32[]{:S(2)}) copy-start(f32[32,32]{1,0:T(8,128)} %param.22) | copy-start | bytes 12292
  13.7 73.9 %copy-start.41 = (f32[32,32]{1,0:T(8,128)S(1)}, f32[32,32]{1,0:T(8,128)}, u32[]{:S(2)}) copy-start(f32[32,32]{1,0:T(8,128)} %param.21) | copy-start | bytes 12292
  13.7 158.5 %all-reduce.6.cloned.1.call-start = ((), (), s32[]{:S(2)}) async-start(), calls=%async_computation.1 | async-start | bytes 262144 | tf_op jit(solution)/shard_map/psum | solution.py:115
  37.4 52.2 %copy-start.38 = (f32[32,32]{1,0:T(8,128)S(1)}, f32[32,32]{1,0:T(8,128)}, u32[]{:S(2)}) copy-start(f32[32,32]{1,0:T(8,128)} %param.23) | copy-start | bytes 12292
  86.3 3.3 copy-start.29
  87.6 3.0 copy-start.33
  91.4 2.1 copy-start.12
  92.3 2.0 copy-start.44
  103.0 220.6 %all-reduce.8.cloned.1.call-start = ((), (), s32[]{:S(2)}) async-start(), calls=%async_computation.2 | async-start | bytes 2670592 | tf_op jit(solution)/shard_map/psum | solution.py:134
  172.1 3.2 copy-start.6
  172.2 3.2 copy-start.32
  173.9 2.1 copy-start.28
  175.4 1.7 copy-start.30
  175.4 1.7 copy-start.42
  183.3 2.4 copy-start.14
  184.0 2.8 copy-start.15
  184.0 2.9 copy-start.22
  187.6 2.1 copy-start.2
  187.8 1.8 copy-start.10
  (26 other events, 31.9 us)
Sparse Core Ops, SparseCore 0:
  13.8 72.4 all-reduce.3
  103.1 68.9 all-reduce.5
  193.7 129.8 all-reduce.7
where the time goes:
time: 337 us; the launch traced here: 336 us
  waiting for transfers between devices  245 us (73%)
  matrix products  35.7 us (11%)
  blocking collectives  23.3 us (7%)
  between operations  14.7 us (4%)
  local copies, waits for them, and re-layouts  14.3 us (4%)
    psum x1, waiting for transfers between devices, shards(): summed_all = lax.psum(flat, ('dp', 'point'))  128 us
    psum x1, waiting for transfers between devices, shards(): grad_out = lax.psum(grad_out_part, 'point')  68.8 us
    psum x1, waiting for transfers between devices, shards(): summed_tokens, total = lax.psum((partial_summed_block, total_part), 'point')  47.9 us
    psum x1, blocking collectives, shards(): summed_tokens, total = lax.psum((partial_summed_block, total_part), 'point')  23.3 us
    unnamed x95, local copies, waits for them, and re-layouts  8.09 us
  transfers between devices with their start and end apart: 3, of which 3 were waited for; matrix products, arithmetic and copies ran while one was open for 1% of the time, Pallas kernels for 0%

commit v1 on v0

v1 whole, which is shorter than its diff:
```python
import functools
import math

import jax
import jax.numpy as jnp
from jax import lax
from jax.experimental import pallas as pl
from jax.experimental.pallas import tpu as pltpu
from jax.sharding import PartitionSpec as P

F32 = jnp.float32
BF16 = jnp.bfloat16
GROUP = 4
EPS = 1e-05
GELU_A = math.sqrt(2.0 / math.pi)
GELU_B = 0.044715
VMEM_LIMIT = 50 * 1024 * 1024


def split(value):
    high = value.astype(BF16)
    return high, (value - high.astype(F32)).astype(BF16)


def product(left, right, left_dim, right_dim):
    def one(a, b):
        return lax.dot_general(
            a, b, (((left_dim,), (right_dim,)), ((), ())), preferred_element_type=F32
        )

    return one(left[0], right[0]) + (one(left[0], right[1]) + one(left[1], right[0]))


def rows_of(pair, start, size):
    return pair[0][start : start + size], pair[1][start : start + size]


def stacked(first, second, axis=0):
    return tuple(jnp.concatenate([a, b], axis=axis) for a, b in zip(first, second))


def column(row):
    wide = jnp.broadcast_to(row, (8, row.shape[1]))
    return wide.T[:, 0:1]


def head_mask(head_size, slices):
    shape = (GROUP * head_size, GROUP * slices)
    row = lax.broadcasted_iota(jnp.int32, shape, 0) // head_size
    lane = lax.broadcasted_iota(jnp.int32, shape, 1) // slices
    return row == lane


def spread_blocks(value, mask):
    return jnp.where(mask, jnp.concatenate([value] * GROUP, axis=0), 0.0)


def fold_blocks(value, mask, head_size):
    kept = jnp.where(mask, value, 0.0)
    total = kept[:head_size]
    for i in range(1, GROUP):
        total = total + kept[i * head_size : (i + 1) * head_size]
    return total


def standardise(columns):
    centre = columns - jnp.mean(columns, axis=0, keepdims=True)
    rstd = lax.rsqrt(jnp.mean(centre * centre, axis=0, keepdims=True) + EPS)
    return centre * rstd, rstd


def standardise_pull(grad, hat, rstd):
    first = jnp.mean(grad, axis=0, keepdims=True)
    second = jnp.mean(grad * hat, axis=0, keepdims=True)
    return rstd * (grad - first - hat * second)


def front_kernel(
    x, gain, fx_weight, x_weight, logit_weight, temper,
    weight_h, weight_l, fx_h, fx_l, assign_h, assign_l, normal_h, normal_l, x_t, sums,
):
    head_size, slices = logit_weight.shape
    heads = temper.shape[0]
    points = x.shape[1]
    width = x.shape[2]
    columns = x[0].T
    x_t[...] = columns
    hat, _ = standardise(columns)
    normal = split(hat * column(gain[...]))
    normal_h[...], normal_l[...] = normal
    both = split(jnp.concatenate([fx_weight[...], x_weight[...]], axis=1))
    projected = split(product(both, normal, 0, 0))
    fx = rows_of(projected, 0, width)
    assign = rows_of(projected, width, width)
    fx_h[...], fx_l[...] = fx
    assign_h[...], assign_l[...] = assign
    mask = head_mask(head_size, slices)
    wide = jnp.concatenate([logit_weight[...]] * GROUP, axis=1)
    logit_blocks = split(spread_blocks(wide, mask))
    ones = jnp.ones((16, points), BF16)
    nums, dens = [], []
    for g in range(heads // GROUP):
        rows = GROUP * head_size
        logits = product(logit_blocks, rows_of(assign, g * rows, rows), 0, 0)
        parts = []
        for i in range(GROUP):
            scale = jnp.full((1, points), temper[g * GROUP + i], F32)
            scaled = logits[i * slices : (i + 1) * slices] / scale
            scaled = scaled - jnp.max(scaled, axis=0, keepdims=True)
            grown = jnp.exp(scaled)
            parts.append(grown / jnp.sum(grown, axis=0, keepdims=True))
        weights = split(jnp.concatenate(parts, axis=0))
        span = slice(g * GROUP * slices, (g + 1) * GROUP * slices)
        weight_h[span], weight_l[span] = weights
        num = product(rows_of(fx, g * rows, rows), weights, 1, 1)
        nums.append(fold_blocks(num, mask, head_size))
        nt = (((1,), (1,)), ((), ()))
        den = lax.dot_general(ones, weights[0], nt, preferred_element_type=F32)
        den = den + lax.dot_general(ones, weights[1], nt, preferred_element_type=F32)
        dens.append(den[:8])
    sums[0:head_size] = jnp.concatenate(nums, axis=1)
    sums[head_size : head_size + 8] = jnp.concatenate(dens, axis=1)


def back_kernel(
    factor,
    sums, x_t, weight_h, weight_l, cotangent, query, key, value, out_weight, gain,
    expand_weight, down_weight,
    out_sum, mixed_grad, spread_grad_h, spread_grad_l, middle, attn, early,
):
    head_size = query.shape[0]
    slices = attn.shape[0] // 2
    heads = weight_h.shape[0] // slices
    rows, lanes = GROUP * head_size, GROUP * slices
    denom = sums[head_size : head_size + 1] + EPS
    tokens = sums[0:head_size] / denom
    token_pair = split(tokens)
    maps = split(jnp.concatenate([query[...], key[...], value[...]], axis=1).T)
    qkv = product(maps, token_pair, 1, 0)
    qkv_pair = split(qkv)
    wide = 2 * slices
    same = (lax.broadcasted_iota(jnp.int32, (wide, wide), 0) // slices) == (
        lax.broadcasted_iota(jnp.int32, (wide, wide), 1) // slices
    )
    results = []
    for pair in range(heads // 2):
        span = slice(pair * wide, (pair + 1) * wide)
        q = tuple(a[0:head_size, span] for a in qkv_pair)
        k = tuple(a[head_size : 2 * head_size, span] for a in qkv_pair)
        v = tuple(a[2 * head_size :, span] for a in qkv_pair)
        scores = product(k, q, 0, 0) * head_size ** (-0.5)
        scores = jnp.where(same, scores, -1e30)
        scores = scores - jnp.max(scores, axis=0, keepdims=True)
        grown = jnp.where(same, jnp.exp(scores), 0.0)
        probs = grown / jnp.sum(grown, axis=0, keepdims=True)
        attn[:, span] = probs
        results.append(product(v, split(probs), 1, 0))
    result = jnp.concatenate(results, axis=1)
    middle[0:head_size] = tokens
    middle[head_size : 4 * head_size] = qkv
    middle[4 * head_size : 5 * head_size] = result
    mask = head_mask(head_size, slices)
    spread = []
    for g in range(heads // GROUP):
        span = slice(g * lanes, (g + 1) * lanes)
        blocks = split(spread_blocks(result[:, span], mask))
        spread.append(product(blocks, (weight_h[span], weight_l[span]), 1, 0))
    spread = split(jnp.concatenate(spread, axis=0))
    out_pair = split(out_weight[...])
    mixed = x_t[...] + product(out_pair, spread, 0, 0)
    hat, rstd = standardise(mixed)
    gain_column = column(gain[...])
    normal = split(hat * gain_column)
    expand = split(expand_weight[...])
    before = product(expand, normal, 0, 0)
    square = before * before
    bent = jnp.tanh(GELU_A * (before + GELU_B * before * square))
    half = 0.5 * (1.0 + bent)
    hidden = split(before * half)
    slope = half + 0.5 * before * (1.0 - bent * bent) * (GELU_A * (1.0 + 3.0 * GELU_B * square))
    cot = cotangent[0]
    cot_t = cot.T
    hidden_grad = product(split(down_weight[...]), split(cot_t), 1, 0)
    before_grad = split(hidden_grad * slope)
    normal_grad = product(expand, before_grad, 1, 0)
    grad = cot_t + standardise_pull(normal_grad * gain_column, hat, rstd)
    mixed_grad[...] = grad
    grad_pair = split(grad)
    spread_grad = split(product(out_pair, grad_pair, 1, 0))
    spread_grad_h[...], spread_grad_l[...] = spread_grad
    sums_out = []
    for g in range(heads // GROUP):
        span = slice(g * lanes, (g + 1) * lanes)
        full = product(
            rows_of(spread_grad, g * rows, rows), (weight_h[span], weight_l[span]), 1, 1
        )
        sums_out.append(fold_blocks(full, mask, head_size))
    out_sum[...] = jnp.concatenate(sums_out, axis=1)
    width = out_weight.shape[0]
    early[0:width] = product(spread, grad_pair, 1, 1) * factor
    early[width : 2 * width] = product(normal, before_grad, 1, 1) * factor
    early[2 * width : 3 * width] = product(hidden, split(cot), 1, 0) * factor
    ones = jnp.ones((16, hat.shape[1]), BF16)
    nt = (((1,), (1,)), ((), ()))
    gains = split(normal_grad * hat)
    gain_row = lax.dot_general(ones, gains[0], nt, preferred_element_type=F32)
    gain_row = gain_row + lax.dot_general(ones, gains[1], nt, preferred_element_type=F32)
    early[3 * width :] = jnp.zeros((early.shape[0] - 3 * width, width), F32)
    early[3 * width : 3 * width + 8] = gain_row[:8] * factor


def end_kernel(
    factor, middle_factor,
    out_sum, sums, middle, attn, weight_h, weight_l, fx_h, fx_l, assign_h, assign_l, normal_h,
    normal_l, x_t, mixed_grad, spread_grad_h, spread_grad_l, query, key, value, fx_weight,
    x_weight, logit_weight, temper, gain,
    x_grad, late,
):
    head_size, slices = logit_weight.shape
    heads = temper.shape[0]
    rows, lanes = GROUP * head_size, GROUP * slices
    points = x_t.shape[1]
    width = x_t.shape[0]
    tokens = middle[0:head_size]
    qkv_pair = split(middle[head_size : 4 * head_size])
    result = middle[4 * head_size : 5 * head_size]
    result_grad = split(out_sum[...])
    wide = 2 * slices
    parts = []
    for pair in range(heads // 2):
        span = slice(pair * wide, (pair + 1) * wide)
        q = tuple(a[0:head_size, span] for a in qkv_pair)
        k = tuple(a[head_size : 2 * head_size, span] for a in qkv_pair)
        v = tuple(a[2 * head_size :, span] for a in qkv_pair)
        probs = attn[:, span]
        grad = tuple(a[:, span] for a in result_grad)
        value_grad = product(grad, split(probs), 1, 1)
        probs_grad = product(v, grad, 0, 0)
        weighted = probs * probs_grad
        total = jnp.sum(weighted, axis=0, keepdims=True)
        score_grad = split((weighted - probs * total) * head_size ** (-0.5))
        query_grad = product(k, score_grad, 1, 0)
        key_grad = product(q, score_grad, 1, 1)
        parts.append(jnp.concatenate([query_grad, key_grad, value_grad], axis=0))
    qkv_grad = split(jnp.concatenate(parts, axis=1))
    maps = split(jnp.concatenate([query[...], key[...], value[...]], axis=1))
    map_grad = product(split(tokens), qkv_grad, 1, 1)
    denom = sums[head_size : head_size + 1] + EPS
    num_grad = product(maps, qkv_grad, 1, 0) / denom
    den_grad = column(-jnp.sum(num_grad * tokens, axis=0, keepdims=True))
    mask = head_mask(head_size, slices)
    logit_wide = jnp.concatenate([logit_weight[...]] * GROUP, axis=1)
    logit_blocks = split(spread_blocks(logit_wide, mask))
    fx_grads, assign_grads = [], []
    logit_grad = jnp.zeros((head_size, lanes), F32)
    for g in range(heads // GROUP):
        span = slice(g * lanes, (g + 1) * lanes)
        piece = slice(g * rows, (g + 1) * rows)
        num_blocks = split(spread_blocks(num_grad[:, span], mask))
        result_blocks = split(spread_blocks(result[:, span], mask))
        weights = (weight_h[span], weight_l[span])
        fx_grads.append(product(num_blocks, weights, 1, 0))
        weight_grad = product(
            stacked(num_blocks, result_blocks),
            stacked(
                (fx_h[piece], fx_l[piece]), (spread_grad_h[piece], spread_grad_l[piece])
            ),
            0,
            0,
        )
        weight_grad = weight_grad + den_grad[span]
        grads = []
        for i in range(GROUP):
            block = slice(i * slices, (i + 1) * slices)
            scale = jnp.full((1, points), temper[g * GROUP + i], F32)
            w = weights[0][block].astype(F32) + weights[1][block].astype(F32)
            weighted = w * weight_grad[block]
            total = jnp.sum(weighted, axis=0, keepdims=True)
            grads.append((weighted - w * total) / scale)
        grads = split(jnp.concatenate(grads, axis=0))
        assign_grads.append(product(logit_blocks, grads, 1, 0))
        full = product((assign_h[piece], assign_l[piece]), grads, 1, 1)
        logit_grad = logit_grad + fold_blocks(full, mask, head_size)
    both_grad = split(jnp.concatenate(fx_grads + assign_grads, axis=0))
    both = split(jnp.concatenate([fx_weight[...], x_weight[...]], axis=1))
    normal_grad = product(both, both_grad, 1, 0)
    hat, rstd = standardise(x_t[...])
    columns = mixed_grad[...] + standardise_pull(normal_grad * column(gain[...]), hat, rstd)
    x_grad[0] = columns.T
    normal = (normal_h[...], normal_l[...])
    matrix = product(normal, both_grad, 1, 1) * factor
    late[0:width] = matrix[:, :width]
    late[width : 2 * width] = matrix[:, width:]
    logit_grad = logit_grad[:, : 2 * slices] + logit_grad[:, 2 * slices :]
    logit_grad = logit_grad[:, :slices] + logit_grad[:, slices:]
    base = 2 * width
    late[base:] = jnp.zeros((late.shape[0] - base, width), F32)
    late[base : base + head_size, 0 : 3 * head_size] = map_grad * middle_factor
    late[base : base + head_size, 128 : 128 + slices] = logit_grad * factor
    ones = jnp.ones((16, points), BF16)
    nt = (((1,), (1,)), ((), ()))
    gains = split(normal_grad * hat)
    gain_row = lax.dot_general(ones, gains[0], nt, preferred_element_type=F32)
    gain_row = gain_row + lax.dot_general(ones, gains[1], nt, preferred_element_type=F32)
    late[base + head_size : base + head_size + 8] = gain_row[:8] * factor


VMEM = pl.BlockSpec(memory_space=pltpu.VMEM)
SMEM = pl.BlockSpec(memory_space=pltpu.SMEM)


def call(body, name, in_specs, out_shape, args, flops):
    return pl.pallas_call(
        body,
        name=name,
        in_specs=in_specs,
        out_specs=[VMEM] * len(out_shape),
        out_shape=out_shape,
        compiler_params=pltpu.CompilerParams(vmem_limit_bytes=VMEM_LIMIT),
        cost_estimate=pl.CostEstimate(flops=flops, bytes_accessed=4 << 20, transcendentals=0),
    )(*args)


def swap(value, moves, sizes):
    dp, point = sizes
    pairs = []
    for d in range(dp):
        for p in range(point):
            other_d, other_p = moves(d, p)
            pairs.append((d * point + p, other_d * point + other_p))
    return lax.ppermute(value, ("dp", "point"), pairs)


def flip(axis, bit):
    if axis == 0:
        return lambda d, p: (d ^ bit, p)
    return lambda d, p: (d, p ^ bit)


def bits(count):
    return [1 << i for i in range(count.bit_length() - 1)]


def power(count):
    return count & (count - 1) == 0


def sum_points(value, sizes):
    if not power(sizes[1]):
        return lax.psum(value, "point")
    for bit in bits(sizes[1]):
        value = value + swap(value, flip(1, bit), sizes)
    return value


def halve(value, upper):
    half = value.shape[0] // 2
    mine = lax.dynamic_slice_in_dim(value, upper * half, half, 0)
    other = lax.dynamic_slice_in_dim(value, (1 - upper) * half, half, 0)
    return mine, other


def join(mine, other, upper):
    low = jnp.where(upper == 0, mine, other)
    high = jnp.where(upper == 0, other, mine)
    return jnp.concatenate([low, high], axis=0)


def sum_all(value, sizes):
    dp, point = sizes
    if not (power(dp) and power(point)) or dp < 2 or point < 2:
        return lax.psum(value, ("dp", "point"))
    d, p = lax.axis_index("dp"), lax.axis_index("point")
    steps = [(1, 1)] + [(0, b) for b in bits(dp)[1:]] + [(1, b) for b in bits(point)[1:]]
    turn = len(steps) // 2
    orders = [steps, steps[turn:] + steps[:turn]]

    def move(i):
        choices = [flip(*order[i]) for order in orders]
        return lambda d, p: choices[d & 1](d, p)

    core = d & 1
    mine, other = halve(value, core)
    value = mine + swap(other, flip(0, 1), sizes)
    axis_bits = [order[0] for order in orders]
    places = [((d if a == 0 else p) // b) & 1 for a, b in axis_bits]
    upper = jnp.where(core == 0, places[0], places[1])
    mine, other = halve(value, upper)
    value = mine + swap(other, move(0), sizes)
    for i in range(1, len(steps)):
        value = value + swap(value, move(i), sizes)
    value = join(value, swap(value, move(0), sizes), upper)
    return join(value, swap(value, flip(0, 1), sizes), core)


def shards(
    sizes,
    inputs, cotangent, gain_one, fx_weight, x_weight, slice_logit_weight, temper,
    slice_query_matrix, slice_key_matrix, slice_value_matrix, out_weight, gain_two,
    expand_weight, down_weight,
):
    points, width = inputs.shape[1:]
    head_size, slices = slice_logit_weight.shape
    heads = temper.shape[0]
    total = heads * slices
    gain_one, gain_two = gain_one[None], gain_two[None]
    factor = 1.0 / math.sqrt(points * sizes[0] * sizes[1])

    def shape(*dims, dtype=F32):
        return jax.ShapeDtypeStruct(dims, dtype)

    half = functools.partial(shape, dtype=BF16)
    pair = [half(width, points)] * 2
    dense = 6 * points * width * width
    (w_h, w_l, fx_h, fx_l, as_h, as_l, n_h, n_l, x_t, sums) = call(
        front_kernel, "front", [VMEM] * 5 + [SMEM],
        [half(total, points)] * 2 + pair * 3 + [shape(width, points), shape(head_size + 8, total)],
        (inputs, gain_one, fx_weight, x_weight, slice_logit_weight, temper),
        4 * dense,
    )
    sums = sum_points(sums, sizes)
    out_sum, mixed_grad, sg_h, sg_l, middle, attn, early = call(
        functools.partial(back_kernel, factor), "back", [VMEM] * 12,
        [shape(head_size, total), shape(width, points)] + pair
        + [shape(5 * head_size, total), shape(2 * slices, total), shape(3 * width + 32, width)],
        (sums, x_t, w_h, w_l, cotangent, slice_query_matrix, slice_key_matrix,
         slice_value_matrix, out_weight, gain_two, expand_weight, down_weight),
        10 * dense,
    )
    out_sum = sum_points(out_sum, sizes)
    input_grad, late = call(
        functools.partial(end_kernel, factor, factor / sizes[1]), "end",
        [VMEM] * 22 + [SMEM] + [VMEM],
        [shape(1, points, width), shape(2 * width + head_size + 32, width)],
        (out_sum, sums, middle, attn, w_h, w_l, fx_h, fx_l, as_h, as_l, n_h, n_l, x_t,
         mixed_grad, sg_h, sg_l, slice_query_matrix, slice_key_matrix, slice_value_matrix,
         fx_weight, x_weight, slice_logit_weight, temper, gain_one),
        10 * dense,
    )
    early = sum_all(early, sizes)
    late = sum_all(late, sizes)
    matrix_grads = jnp.concatenate([late[: 2 * width], early[: 3 * width]], axis=0)
    small = late[2 * width : 2 * width + head_size]
    maps = jnp.stack([small[:, i * head_size : (i + 1) * head_size] for i in range(3)])
    gains = jnp.stack([late[2 * width + head_size], early[3 * width]])
    return (
        input_grad,
        matrix_grads.reshape(5, width, width),
        maps,
        small[:, 128 : 128 + slices],
        gains,
    )


def solution(mesh):
    sizes = (mesh.shape["dp"], mesh.shape["point"])
    placed = (P("dp", "point", None),) * 2 + (P(),) * 12
    return jax.shard_map(
        functools.partial(shards, sizes),
        mesh=mesh,
        in_specs=placed,
        out_specs=(P("dp", "point", None), P(), P(), P(), P()),
        check_vma=False,
    )
```

time: 337 us -> 101 us (0.30)
  waiting for transfers between devices: 245 us -> 33.3 us
  matrix products: 35.7 us -> 0 us
  starting transfers between devices: 0.34 us -> 31.6 us
  blocking collectives: 23.3 us -> 0 us
  Pallas kernels: 0 us -> 17.8 us
  between operations: 14.7 us -> 1.03 us
    psum x3 -> x0, waiting for transfers between devices: 245 us -> none  [the longest x1 128 us: shards(): summed_all = lax.psum(flat, ('dp', 'point'))]
    dot_general x38 -> x0, matrix products: 35.7 us -> none  [the longest x3 5.7 us: back(): jnp.einsum('azc,azb->abc', slice_membership_weights, slice_result_rows, p...]
    ppermute x0 -> x20, waiting for transfers between devices: none -> 33.3 us  [swap(): return lax.ppermute(value, ('dp', 'point'), pairs)]
    ppermute x0 -> x20, starting transfers between devices: none -> 31.6 us  [swap(): return lax.ppermute(value, ('dp', 'point'), pairs)]
    psum x1 -> x0, blocking collectives: 23.3 us -> none  [shards(): summed_tokens, total = lax.psum((partial_summed_block, total_part), 'point')]
    pallas_call x0 -> x3, Pallas kernels: none -> 17.8 us  [call(): pl.pallas_call(body, name=name, in_specs=in_specs, out_specs=[VMEM] * len...]
    unnamed x95 -> x60, local copies, waits for them, and re-layouts: 8.09 us -> 9.54 us
  transfers between devices with their start and end apart: 3 -> 20, of which waited for: 3 -> 13; matrix products, arithmetic and copies ran while one was open for 1% -> 6% of each run, Pallas kernels for 0% -> 7%
where the time goes in v1:
time: 101 us
  waiting for transfers between devices  33.3 us (33%)
  starting transfers between devices  31.6 us (31%)
  Pallas kernels  17.8 us (18%)
  local copies, waits for them, and re-layouts  13.1 us (13%)
  other arithmetic  3.97 us (4%)
  between operations  1.03 us (1%)
    ppermute x20, waiting for transfers between devices, swap(): return lax.ppermute(value, ('dp', 'point'), pairs)  33.3 us
    ppermute x20, starting transfers between devices, swap(): return lax.ppermute(value, ('dp', 'point'), pairs)  31.6 us
    pallas_call x3, Pallas kernels, call(): pl.pallas_call(body, name=name, in_specs=in_specs, out_specs=[VMEM] * len...  17.8 us
    unnamed x60, local copies, waits for them, and re-layouts  9.54 us
    dynamic_slice x4, local copies, waits for them, and re-layouts, halve(): other = lax.dynamic_slice_in_dim(value, (1 - upper) * half, half, 0)  2.87 us
  transfers between devices with their start and end apart: 20, of which 13 were waited for; matrix products, arithmetic and copies ran while one was open for 6% of the time, Pallas kernels for 7%

profile of v1, /device:TPU:0, one launch (start us, length us, event | category | flops | bytes accessed | tf_op | source)
XLA Modules:
  0.0 100.8 jit_solution(14751248530097310321)
XLA Ops:
  4.6 3.8 %front.1 = (bf16[512,512]{1,0:T(8,128)(2,1)S(1)}, bf16[512,512]{1,0:T(8,128)(2,1)S(1)}, bf16[256,512]{1,0:T(8,128)(2,1)S(1)}, bf16[256,512]{1,0:T(8,128)(2,1)S(1...) custom-call(f32[1,512,256]{2,1,0:T(8,128)} %x.1, ...), custom_call_target="tpu_custom_call" | custom-call | flops 805306368 | bytes 4194304 | tf_op jit(solution)/shard_map/front/pallas_call | solution.py:313
  9.2 2.9 %collective-permute-start = (f32[40,512]{1,0:T(8,128)S(1)}, f32[40,512]{1,0:T(8,128)S(1)}, u32[]{:S(2)}, u32[]{:S(2)}) collective-permute-start(f32[40,512]{1,0:T(8,128)S(1)} %get-tuple-element.24), channel_id=1, source_target_pairs={{0,1},{1,0},{2,3},{3,2},{4,5},{5,4},{6,7},{7,6},{8,9},{9,8},{10,11... | collective-permute-start | bytes 245768 | tf_op jit(solution)/shard_map/ppermute | solution.py:331
  12.1 2.4 %collective-permute-done = f32[40,512]{1,0:T(8,128)S(1)} collective-permute-done((f32[40,512]{1,0:T(8,128)S(1)}, f32[40,512]{1,0:T(8,128)S(1)}, u32[]{:S(2)}, u32[]{:S(2)}) %collective-permute-start) | collective-permute-done | bytes 81952 | tf_op jit(solution)/shard_map/ppermute | solution.py:331
  14.5 2.2 %collective-permute-start.1 = (f32[40,512]{1,0:T(8,128)S(1)}, f32[40,512]{1,0:T(8,128)S(1)}, u32[]{:S(2)}, u32[]{:S(2)}) collective-permute-start(f32[40,512]{1,0:T(8,128)S(1)} %add.74), channel_id=1, source_target_pairs={{0,2},{1,3},{2,0},{3,1},{4,6},{5,7},{6,4},{7,5},{8,10},{9,11},{10,... | collective-permute-start | bytes 245768 | tf_op jit(solution)/shard_map/ppermute | solution.py:331
  16.7 2.4 %collective-permute-done.1 = f32[40,512]{1,0:T(8,128)S(1)} collective-permute-done((f32[40,512]{1,0:T(8,128)S(1)}, f32[40,512]{1,0:T(8,128)S(1)}, u32[]{:S(2)}, u32[]{:S(2)}) %collective-permute-start.1) | collective-permute-done | bytes 81952 | tf_op jit(solution)/shard_map/ppermute | solution.py:331
  19.1 3.1 %collective-permute-start.2 = (f32[40,512]{1,0:T(8,128)S(1)}, f32[40,512]{1,0:T(8,128)S(1)}, u32[]{:S(2)}, u32[]{:S(2)}) collective-permute-start(f32[40,512]{1,0:T(8,128)S(1)} %add.75), channel_id=1, source_target_pairs={{0,4},{1,5},{2,6},{3,7},{4,0},{5,1},{6,2},{7,3},{8,12},{9,13},{10,... | collective-permute-start | bytes 245768 | tf_op jit(solution)/shard_map/ppermute | solution.py:331
  22.2 2.4 %collective-permute-done.2 = f32[40,512]{1,0:T(8,128)S(1)} collective-permute-done((f32[40,512]{1,0:T(8,128)S(1)}, f32[40,512]{1,0:T(8,128)S(1)}, u32[]{:S(2)}, u32[]{:S(2)}) %collective-permute-start.2) | collective-permute-done | bytes 81952 | tf_op jit(solution)/shard_map/ppermute | solution.py:331
  24.8 7.1 %back.1 = (f32[32,512]{1,0:T(8,128)S(1)}, f32[256,512]{1,0:T(8,128)S(1)}, bf16[256,512]{1,0:T(8,128)(2,1)S(1)}, bf16[256,512]{1,0:T(8,128)(2,1)S(1)}, f32[160,51...) custom-call(f32[40,512]{1,0:T(8,128)S(1)} %add.76.sums, f32[256,512]{1,0:T(8,128)S(1)} %get-tuple-element.25.x_t, ...), custom_call_target="tpu_custom_call" | custom-call | flops 2013265920 | bytes 4194304 | tf_op jit(solution)/shard_map/back/pallas_call | solution.py:313
  34.8 1.9 %collective-permute-start.3 = (f32[32,512]{1,0:T(8,128)S(1)}, f32[32,512]{1,0:T(8,128)S(1)}, u32[]{:S(2)}, u32[]{:S(2)}) collective-permute-start(f32[32,512]{1,0:T(8,128)S(1)} %get-tuple-element.28), channel_id=1, source_target_pairs={{0,1},{1,0},{2,3},{3,2},{4,5},{5,4},{6,7},{7,6},{8,9},{9,8},{10,11... | collective-permute-start | bytes 196616 | tf_op jit(solution)/shard_map/ppermute | solution.py:331
  36.7 2.4 %collective-permute-done.3 = f32[32,512]{1,0:T(8,128)S(1)} collective-permute-done((f32[32,512]{1,0:T(8,128)S(1)}, f32[32,512]{1,0:T(8,128)S(1)}, u32[]{:S(2)}, u32[]{:S(2)}) %collective-permute-start.3) | collective-permute-done | bytes 65568 | tf_op jit(solution)/shard_map/ppermute | solution.py:331
  39.2 2.0 %collective-permute-start.4 = (f32[32,512]{1,0:T(8,128)S(1)}, f32[32,512]{1,0:T(8,128)S(1)}, u32[]{:S(2)}, u32[]{:S(2)}) collective-permute-start(f32[32,512]{1,0:T(8,128)S(1)} %add.77), channel_id=1, source_target_pairs={{0,2},{1,3},{2,0},{3,1},{4,6},{5,7},{6,4},{7,5},{8,10},{9,11},{10,... | collective-permute-start | bytes 196616 | tf_op jit(solution)/shard_map/ppermute | solution.py:331
  41.2 1.8 %constant_dynamic-slice_fusion.1 = f32[400,256]{1,0:T(8,128)} fusion(f32[800,256]{1,0:T(8,128)} %get-tuple-element.42, s32[]{:T(128)S(6)} %select_n.99), kind=kLoop, calls=%fused_computation.24 | loop fusion | bytes 819204 | tf_op jit(solution)/shard_map/dynamic_slice | solution.py:359
  43.5 3.3 %collective-permute-start.5 = (f32[32,512]{1,0:T(8,128)S(1)}, f32[32,512]{1,0:T(8,128)S(1)}, u32[]{:S(2)}, u32[]{:S(2)}) collective-permute-start(f32[32,512]{1,0:T(8,128)S(1)} %add.78), channel_id=1, source_target_pairs={{0,4},{1,5},{2,6},{3,7},{4,0},{5,1},{6,2},{7,3},{8,12},{9,13},{10,... | collective-permute-start | bytes 196616 | tf_op jit(solution)/shard_map/ppermute | solution.py:331
  46.8 2.5 %collective-permute-done.5 = f32[32,512]{1,0:T(8,128)S(1)} collective-permute-done((f32[32,512]{1,0:T(8,128)S(1)}, f32[32,512]{1,0:T(8,128)S(1)}, u32[]{:S(2)}, u32[]{:S(2)}) %collective-permute-start.5) | collective-permute-done | bytes 65568 | tf_op jit(solution)/shard_map/ppermute | solution.py:331
  51.3 6.9 %end.1 = (f32[1,512,256]{2,1,0:T(8,128)}, f32[576,256]{1,0:T(8,128)}) custom-call(f32[32,512]{1,0:T(8,128)S(1)} %add.79.out_sum, f32[40,512]{1,0:T(8,128)S(1)} %add.76.sums, f32[160,512]{1,0:T(8,128)S(1)} %get-tuple-element.29.middle, f32[128,512]{1,0:T(8,128)S(1)} %copy-done.27, bf16[512,512]{1,0:T(8,128)(2,1)S(1)} %get-tuple-element.26.weight_h, ...), custom_call_target="tpu_custom_call" | custom-call | flops 2013265920 | bytes 4194304 | tf_op jit(solution)/shard_map/end/pallas_call | solution.py:313
  62.7 3.6 %collective-permute-done.14 = f32[200,256]{1,0:T(8,128)S(1)} collective-permute-done((f32[200,256]{1,0:T(8,128)S(1)}, f32[200,256]{1,0:T(8,128)S(1)}, u32[]{:S(2)}, u32[]{:S(2)}) %collective-permute-start.14) | collective-permute-done | bytes 204832 | tf_op jit(solution)/shard_map/ppermute | solution.py:331
  69.5 4.2 %collective-permute-done.8 = f32[144,256]{1,0:T(8,128)S(1)} collective-permute-done((f32[144,256]{1,0:T(8,128)S(1)}, f32[144,256]{1,0:T(8,128)S(1)}, u32[]{:S(2)}, u32[]{:S(2)}) %collective-permute-start.8) | collective-permute-done | bytes 147488 | tf_op jit(solution)/shard_map/ppermute | solution.py:331
  73.7 1.9 %collective-permute-start.9 = (f32[144,256]{1,0:T(8,128)S(1)}, f32[144,256]{1,0:T(8,128)S(1)}, u32[]{:S(2)}, u32[]{:S(2)}) collective-permute-start(f32[144,256]{1,0:T(8,128)S(1)} %add.86), channel_id=1, source_target_pairs={{0,2},{1,3},{2,0},{3,1},{4,6},{5,7},{6,4},{7,5},{8,9},{9,8},{10,11... | collective-permute-start | bytes 442376 | tf_op jit(solution)/shard_map/ppermute | solution.py:331
  75.9 3.2 %collective-permute-done.9 = f32[144,256]{1,0:T(8,128)S(1)} collective-permute-done((f32[144,256]{1,0:T(8,128)S(1)}, f32[144,256]{1,0:T(8,128)S(1)}, u32[]{:S(2)}, u32[]{:S(2)}) %collective-permute-start.9) | collective-permute-done | bytes 147488 | tf_op jit(solution)/shard_map/ppermute | solution.py:331
  79.1 2.7 %collective-permute-start.10 = (f32[144,256]{1,0:T(8,128)S(1)}, f32[144,256]{1,0:T(8,128)S(1)}, u32[]{:S(2)}, u32[]{:S(2)}) collective-permute-start(f32[144,256]{1,0:T(8,128)S(1)} %add.87), channel_id=1, source_target_pairs={{0,4},{1,5},{2,6},{3,7},{4,0},{5,1},{6,2},{7,3},{8,24},{9,25},{10,... | collective-permute-start | bytes 442376 | tf_op jit(solution)/shard_map/ppermute | solution.py:331
  81.9 2.7 %collective-permute-start.17 = (f32[200,256]{1,0:T(8,128)S(1)}, f32[200,256]{1,0:T(8,128)S(1)}, u32[]{:S(2)}, u32[]{:S(2)}) collective-permute-start(f32[200,256]{1,0:T(8,128)S(1)} %add.96), channel_id=1, source_target_pairs={{0,4},{1,5},{2,6},{3,7},{4,0},{5,1},{6,2},{7,3},{8,24},{9,25},{10,... | collective-permute-start | bytes 614408 | tf_op jit(solution)/shard_map/ppermute | solution.py:331
  84.6 2.2 %collective-permute-done.10 = f32[144,256]{1,0:T(8,128)S(1)} collective-permute-done((f32[144,256]{1,0:T(8,128)S(1)}, f32[144,256]{1,0:T(8,128)S(1)}, u32[]{:S(2)}, u32[]{:S(2)}) %collective-permute-start.10) | collective-permute-done | bytes 147488 | tf_op jit(solution)/shard_map/ppermute | solution.py:331
  88.4 2.8 %collective-permute-done.17 = f32[200,256]{1,0:T(8,128)S(1)} collective-permute-done((f32[200,256]{1,0:T(8,128)S(1)}, f32[200,256]{1,0:T(8,128)S(1)}, u32[]{:S(2)}, u32[]{:S(2)}) %collective-permute-start.17) | collective-permute-done | bytes 204832 | tf_op jit(solution)/shard_map/ppermute | solution.py:331
  92.9 4.1 %collective-permute-done.18 = f32[200,256]{1,0:T(8,128)S(1)} collective-permute-done((f32[200,256]{1,0:T(8,128)S(1)}, f32[200,256]{1,0:T(8,128)S(1)}, u32[]{:S(2)}, u32[]{:S(2)}) %collective-permute-start.18) | collective-permute-done | bytes 204832 | tf_op jit(solution)/shard_map/ppermute | solution.py:331
  (112 shorter events, 25.1 us)
Async XLA Ops:
  4.6 20.1 %copy-start.10 = (f32[32,32]{1,0:T(8,128)S(1)}, f32[32,32]{1,0:T(8,128)}, u32[]{:S(2)}) copy-start(f32[32,32]{1,0:T(8,128)} %key.3) | copy-start | bytes 12292
  4.6 20.1 %copy-start.11 = (f32[32,32]{1,0:T(8,128)S(1)}, f32[32,32]{1,0:T(8,128)}, u32[]{:S(2)}) copy-start(f32[32,32]{1,0:T(8,128)} %value.3) | copy-start | bytes 12292
  4.6 20.1 %copy-start.12 = (f32[256]{0:T(256)S(1)}, f32[256]{0:T(256)}, u32[]{:S(2)}) copy-start(f32[256]{0:T(256)} %param.25) | copy-start | bytes 3076
  9.1 22.7 %copy-start.18 = (f32[256,512]{1,0:T(8,128)}, f32[256,512]{1,0:T(8,128)S(1)}, u32[]{:S(2)}) copy-start(f32[256,512]{1,0:T(8,128)S(1)} %get-tuple-element.25.x_t) | copy-start | bytes 1572868
  9.2 5.4 %collective-permute-start = (f32[40,512]{1,0:T(8,128)S(1)}, f32[40,512]{1,0:T(8,128)S(1)}, u32[]{:S(2)}, u32[]{:S(2)}) collective-permute-start(f32[40,512]{1,0:T(8,128)S(1)} %get-tuple-element.24), channel_id=1, source_target_pairs={{0,1},{1,0},{2,3},{3,2},{4,5},{5,4},{6,7},{7,6},{8,9},{9,8},{10,11... | collective-permute-start | bytes 245768 | tf_op jit(solution)/shard_map/ppermute | solution.py:331
  14.5 4.6 %collective-permute-start.1 = (f32[40,512]{1,0:T(8,128)S(1)}, f32[40,512]{1,0:T(8,128)S(1)}, u32[]{:S(2)}, u32[]{:S(2)}) collective-permute-start(f32[40,512]{1,0:T(8,128)S(1)} %add.74), channel_id=1, source_target_pairs={{0,2},{1,3},{2,0},{3,1},{4,6},{5,7},{6,4},{7,5},{8,10},{9,11},{10,... | collective-permute-start | bytes 245768 | tf_op jit(solution)/shard_map/ppermute | solution.py:331
  19.1 5.5 %collective-permute-start.2 = (f32[40,512]{1,0:T(8,128)S(1)}, f32[40,512]{1,0:T(8,128)S(1)}, u32[]{:S(2)}, u32[]{:S(2)}) collective-permute-start(f32[40,512]{1,0:T(8,128)S(1)} %add.75), channel_id=1, source_target_pairs={{0,4},{1,5},{2,6},{3,7},{4,0},{5,1},{6,2},{7,3},{8,12},{9,13},{10,... | collective-permute-start | bytes 245768 | tf_op jit(solution)/shard_map/ppermute | solution.py:331
  34.8 4.3 %collective-permute-start.3 = (f32[32,512]{1,0:T(8,128)S(1)}, f32[32,512]{1,0:T(8,128)S(1)}, u32[]{:S(2)}, u32[]{:S(2)}) collective-permute-start(f32[32,512]{1,0:T(8,128)S(1)} %get-tuple-element.28), channel_id=1, source_target_pairs={{0,1},{1,0},{2,3},{3,2},{4,5},{5,4},{6,7},{7,6},{8,9},{9,8},{10,11... | collective-permute-start | bytes 196616 | tf_op jit(solution)/shard_map/ppermute | solution.py:331
  39.2 4.3 %collective-permute-start.4 = (f32[32,512]{1,0:T(8,128)S(1)}, f32[32,512]{1,0:T(8,128)S(1)}, u32[]{:S(2)}, u32[]{:S(2)}) collective-permute-start(f32[32,512]{1,0:T(8,128)S(1)} %add.77), channel_id=1, source_target_pairs={{0,2},{1,3},{2,0},{3,1},{4,6},{5,7},{6,4},{7,5},{8,10},{9,11},{10,... | collective-permute-start | bytes 196616 | tf_op jit(solution)/shard_map/ppermute | solution.py:331
  42.9 16.4 %collective-permute-start.13 = (f32[400,256]{1,0:T(8,128)}, f32[400,256]{1,0:T(8,128)}, u32[]{:S(2)}, u32[]{:S(2)}) collective-permute-start(f32[400,256]{1,0:T(8,128)} %constant_dynamic-slice_fusion.1), channel_id=1, source_target_pairs={{0,8},{1,9},{2,10},{3,11},{4,12},{5,13},{6,14},{7,15},{8,0},{9,1},... | collective-permute-start | bytes 1228808 | tf_op jit(solution)/shard_map/ppermute | solution.py:331
  43.5 5.8 %collective-permute-start.5 = (f32[32,512]{1,0:T(8,128)S(1)}, f32[32,512]{1,0:T(8,128)S(1)}, u32[]{:S(2)}, u32[]{:S(2)}) collective-permute-start(f32[32,512]{1,0:T(8,128)S(1)} %add.78), channel_id=1, source_target_pairs={{0,4},{1,5},{2,6},{3,7},{4,0},{5,1},{6,2},{7,3},{8,12},{9,13},{10,... | collective-permute-start | bytes 196616 | tf_op jit(solution)/shard_map/ppermute | solution.py:331
  59.3 2.8 %collective-permute-start.6 = (f32[288,256]{1,0:T(8,128)S(1)}, f32[288,256]{1,0:T(8,128)S(1)}, u32[]{:S(2)}, u32[]{:S(2)}) collective-permute-start(f32[288,256]{1,0:T(8,128)S(1)} %constant_dynamic-slice_fusion.3), channel_id=1, source_target_pairs={{0,8},{1,9},{2,10},{3,11},{4,12},{5,13},{6,14},{7,15},{8,0},{9,1},... | collective-permute-start | bytes 884744 | tf_op jit(solution)/shard_map/ppermute | solution.py:331
  60.4 5.8 %collective-permute-start.14 = (f32[200,256]{1,0:T(8,128)S(1)}, f32[200,256]{1,0:T(8,128)S(1)}, u32[]{:S(2)}, u32[]{:S(2)}) collective-permute-start(f32[200,256]{1,0:T(8,128)S(1)} %constant_dynamic-slice_fusion), channel_id=1, source_target_pairs={{0,1},{1,0},{2,3},{3,2},{4,5},{5,4},{6,7},{7,6},{8,10},{9,11},{10,... | collective-permute-start | bytes 614408 | tf_op jit(solution)/shard_map/ppermute | solution.py:331
  62.1 5.8 %collective-permute-start.7 = (f32[144,256]{1,0:T(8,128)S(1)}, f32[144,256]{1,0:T(8,128)S(1)}, u32[]{:S(2)}, u32[]{:S(2)}) collective-permute-start(f32[144,256]{1,0:T(8,128)S(1)} %constant_dynamic-slice_fusion.2), channel_id=1, source_target_pairs={{0,1},{1,0},{2,3},{3,2},{4,5},{5,4},{6,7},{7,6},{8,10},{9,11},{10,... | collective-permute-start | bytes 442376 | tf_op jit(solution)/shard_map/ppermute | solution.py:331
  66.3 9.3 %collective-permute-start.15 = (f32[200,256]{1,0:T(8,128)S(1)}, f32[200,256]{1,0:T(8,128)S(1)}, u32[]{:S(2)}, u32[]{:S(2)}) collective-permute-start(f32[200,256]{1,0:T(8,128)S(1)} %dynamic-slice_add_fusion.2), channel_id=1, source_target_pairs={{0,16},{1,17},{2,18},{3,19},{4,20},{5,21},{6,22},{7,23},{8,12},{9,... | collective-permute-start | bytes 614408 | tf_op jit(solution)/shard_map/ppermute | solution.py:331
  67.9 5.8 %collective-permute-start.8 = (f32[144,256]{1,0:T(8,128)S(1)}, f32[144,256]{1,0:T(8,128)S(1)}, u32[]{:S(2)}, u32[]{:S(2)}) collective-permute-start(f32[144,256]{1,0:T(8,128)S(1)} %dynamic-slice_add_fusion.3), channel_id=1, source_target_pairs={{0,16},{1,17},{2,18},{3,19},{4,20},{5,21},{6,22},{7,23},{8,12},{9,... | collective-permute-start | bytes 442376 | tf_op jit(solution)/shard_map/ppermute | solution.py:331
  73.7 5.4 %collective-permute-start.9 = (f32[144,256]{1,0:T(8,128)S(1)}, f32[144,256]{1,0:T(8,128)S(1)}, u32[]{:S(2)}, u32[]{:S(2)}) collective-permute-start(f32[144,256]{1,0:T(8,128)S(1)} %add.86), channel_id=1, source_target_pairs={{0,2},{1,3},{2,0},{3,1},{4,6},{5,7},{6,4},{7,5},{8,9},{9,8},{10,11... | collective-permute-start | bytes 442376 | tf_op jit(solution)/shard_map/ppermute | solution.py:331
  75.6 6.2 %collective-permute-start.16 = (f32[200,256]{1,0:T(8,128)S(1)}, f32[200,256]{1,0:T(8,128)S(1)}, u32[]{:S(2)}, u32[]{:S(2)}) collective-permute-start(f32[200,256]{1,0:T(8,128)S(1)} %add.95), channel_id=1, source_target_pairs={{0,2},{1,3},{2,0},{3,1},{4,6},{5,7},{6,4},{7,5},{8,9},{9,8},{10,11... | collective-permute-start | bytes 614408 | tf_op jit(solution)/shard_map/ppermute | solution.py:331
  79.1 7.7 %collective-permute-start.10 = (f32[144,256]{1,0:T(8,128)S(1)}, f32[144,256]{1,0:T(8,128)S(1)}, u32[]{:S(2)}, u32[]{:S(2)}) collective-permute-start(f32[144,256]{1,0:T(8,128)S(1)} %add.87), channel_id=1, source_target_pairs={{0,4},{1,5},{2,6},{3,7},{4,0},{5,1},{6,2},{7,3},{8,24},{9,25},{10,... | collective-permute-start | bytes 442376 | tf_op jit(solution)/shard_map/ppermute | solution.py:331
  81.9 9.3 %collective-permute-start.17 = (f32[200,256]{1,0:T(8,128)S(1)}, f32[200,256]{1,0:T(8,128)S(1)}, u32[]{:S(2)}, u32[]{:S(2)}) collective-permute-start(f32[200,256]{1,0:T(8,128)S(1)} %add.96), channel_id=1, source_target_pairs={{0,4},{1,5},{2,6},{3,7},{4,0},{5,1},{6,2},{7,3},{8,24},{9,25},{10,... | collective-permute-start | bytes 614408 | tf_op jit(solution)/shard_map/ppermute | solution.py:331
  86.8 6.0 %collective-permute-start.11 = (f32[144,256]{1,0:T(8,128)S(1)}, f32[144,256]{1,0:T(8,128)S(1)}, u32[]{:S(2)}, u32[]{:S(2)}) collective-permute-start(f32[144,256]{1,0:T(8,128)S(1)} %add.88), channel_id=1, source_target_pairs={{0,1},{1,0},{2,3},{3,2},{4,5},{5,4},{6,7},{7,6},{8,10},{9,11},{10,... | collective-permute-start | bytes 442376 | tf_op jit(solution)/shard_map/ppermute | solution.py:331
  91.3 5.8 %collective-permute-start.18 = (f32[200,256]{1,0:T(8,128)S(1)}, f32[200,256]{1,0:T(8,128)S(1)}, u32[]{:S(2)}, u32[]{:S(2)}) collective-permute-start(f32[200,256]{1,0:T(8,128)S(1)} %add.97), channel_id=1, source_target_pairs={{0,1},{1,0},{2,3},{3,2},{4,5},{5,4},{6,7},{7,6},{8,10},{9,11},{10,... | collective-permute-start | bytes 614408 | tf_op jit(solution)/shard_map/ppermute | solution.py:331
  92.9 4.4 %collective-permute-start.12 = (f32[288,256]{1,0:T(8,128)S(1)}, f32[288,256]{1,0:T(8,128)S(1)}, u32[]{:S(2)}, u32[]{:S(2)}) collective-permute-start(f32[288,256]{1,0:T(8,128)S(1)} %pad_maximum_fusion.2), channel_id=1, source_target_pairs={{0,8},{1,9},{2,10},{3,11},{4,12},{5,13},{6,14},{7,15},{8,0},{9,1},... | collective-permute-start | bytes 884744 | tf_op jit(solution)/shard_map/ppermute | solution.py:331
  97.1 1.8 %collective-permute-start.19 = (f32[400,256]{1,0:T(8,128)S(1)}, f32[400,256]{1,0:T(8,128)S(1)}, u32[]{:S(2)}, u32[]{:S(2)}) collective-permute-start(f32[400,256]{1,0:T(8,128)S(1)} %pad_maximum_fusion.1), channel_id=1, source_target_pairs={{0,8},{1,9},{2,10},{3,11},{4,12},{5,13},{6,14},{7,15},{8,0},{9,1},... | collective-permute-start | bytes 1228808 | tf_op jit(solution)/shard_map/ppermute | solution.py:331
  (26 other events, 219.1 us)

commit v2 on v1

--- a/solution.py
+++ b/solution.py
@@ -14,7 +14,7 @@
 EPS = 1e-05
 GELU_A = math.sqrt(2.0 / math.pi)
 GELU_B = 0.044715
-VMEM_LIMIT = 50 * 1024 * 1024
+VMEM_LIMIT = 16 * 1024 * 1024
 
 
 def split(value):
@@ -75,21 +75,49 @@
     return rstd * (grad - first - hat * second)
 
 
+def row_total(left, right):
+    value = split(left * right)
+    ones = jnp.ones((16, left.shape[1]), BF16)
+    nt = (((1,), (1,)), ((), ()))
+    total = lax.dot_general(ones, value[0], nt, preferred_element_type=F32)
+    total = total + lax.dot_general(ones, value[1], nt, preferred_element_type=F32)
+    return total[0:1]
+
+
+def fetch(sources, targets, sems):
+    copies = [
+        pltpu.make_async_copy(source, target, sems.at[i])
+        for i, (source, target) in enumerate(zip(sources, targets))
+    ]
+    for copy in copies:
+        copy.start()
+    return copies
+
+
 def front_kernel(
-    x, gain, fx_weight, x_weight, logit_weight, temper,
-    weight_h, weight_l, fx_h, fx_l, assign_h, assign_l, normal_h, normal_l, x_t, sums,
-):
+    x_hbm, gain_hbm, fx_hbm, xw_hbm, logit_hbm, temper_hbm,
+    weight_h, weight_l, fx_h, fx_l, assign_h, assign_l, hat_h, hat_l, x_t, both_h, both_l, sums,
+    x, gain, fx_weight, x_weight, logit_weight, temper, sems,
+):
+    sources = (x_hbm, gain_hbm, fx_hbm, xw_hbm, logit_hbm, temper_hbm)
+    targets = (x, gain, fx_weight, x_weight, logit_weight, temper)
+    copies = fetch(sources, targets, sems)
     head_size, slices = logit_weight.shape
     heads = temper.shape[0]
     points = x.shape[1]
     width = x.shape[2]
+    copies[0].wait()
     columns = x[0].T
     x_t[...] = columns
     hat, _ = standardise(columns)
-    normal = split(hat * column(gain[...]))
-    normal_h[...], normal_l[...] = normal
-    both = split(jnp.concatenate([fx_weight[...], x_weight[...]], axis=1))
-    projected = split(product(both, normal, 0, 0))
+    hat = split(hat)
+    hat_h[...], hat_l[...] = hat
+    for copy in copies[1:]:
+        copy.wait()
+    both = jnp.concatenate([fx_weight[...], x_weight[...]], axis=1)
+    both = split(both * column(gain[...]))
+    both_h[...], both_l[...] = both
+    projected = split(product(both, hat, 0, 0))
     fx = rows_of(projected, 0, width)
     assign = rows_of(projected, width, width)
     fx_h[...], fx_l[...] = fx
@@ -122,21 +150,35 @@
     sums[head_size : head_size + 8] = jnp.concatenate(dens, axis=1)
 
 
+def ready_kernel(
+    cotangent, out_weight, gain, expand_weight, down_weight, query, key, value,
+    cot_t, hidden_grad, out_t_h, out_t_l, expand_h, expand_l, expand_t_h, expand_t_l, maps_h,
+    maps_l,
+):
+    columns = cotangent[0].T
+    cot_t[...] = columns
+    hidden_grad[...] = product(split(down_weight[...]), split(columns), 1, 0)
+    out_t_h[...], out_t_l[...] = split(out_weight[...].T)
+    expand = expand_weight[...] * column(gain[...])
+    expand_h[...], expand_l[...] = split(expand)
+    expand_t_h[...], expand_t_l[...] = split(expand.T)
+    maps = jnp.concatenate([query[...], key[...], value[...]], axis=1)
+    maps_h[...], maps_l[...] = split(maps.T)
+
+
 def back_kernel(
-    factor,
-    sums, x_t, weight_h, weight_l, cotangent, query, key, value, out_weight, gain,
-    expand_weight, down_weight,
-    out_sum, mixed_grad, spread_grad_h, spread_grad_l, middle, attn, early,
-):
-    head_size = query.shape[0]
+    sums, x_t, weight_h, weight_l, cot_t, hidden_grad, out_weight, out_t_h, out_t_l, expand_h,
+    expand_l, expand_t_h, expand_t_l, maps_h, maps_l,
+    out_sum, mixed_grad, spread_grad_h, spread_grad_l, middle, attn, spread_h, spread_l, hat_h,
+    hat_l, before_grad_h, before_grad_l, hidden_h, hidden_l,
+):
+    head_size = maps_h.shape[1]
     slices = attn.shape[0] // 2
     heads = weight_h.shape[0] // slices
     rows, lanes = GROUP * head_size, GROUP * slices
     denom = sums[head_size : head_size + 1] + EPS
     tokens = sums[0:head_size] / denom
-    token_pair = split(tokens)
-    maps = split(jnp.concatenate([query[...], key[...], value[...]], axis=1).T)
-    qkv = product(maps, token_pair, 1, 0)
+    qkv = product((maps_h[...], maps_l[...]), split(tokens), 1, 0)
     qkv_pair = split(qkv)
     wide = 2 * slices
     same = (lax.broadcasted_iota(jnp.int32, (wide, wide), 0) // slices) == (
@@ -166,27 +208,23 @@
         blocks = split(spread_blocks(result[:, span], mask))
         spread.append(product(blocks, (weight_h[span], weight_l[span]), 1, 0))
     spread = split(jnp.concatenate(spread, axis=0))
-    out_pair = split(out_weight[...])
-    mixed = x_t[...] + product(out_pair, spread, 0, 0)
+    spread_h[...], spread_l[...] = spread
+    mixed = x_t[...] + product((out_t_h[...], out_t_l[...]), spread, 1, 0)
     hat, rstd = standardise(mixed)
-    gain_column = column(gain[...])
-    normal = split(hat * gain_column)
-    expand = split(expand_weight[...])
-    before = product(expand, normal, 0, 0)
+    hat_pair = split(hat)
+    hat_h[...], hat_l[...] = hat_pair
+    before = product((expand_t_h[...], expand_t_l[...]), hat_pair, 1, 0)
     square = before * before
     bent = jnp.tanh(GELU_A * (before + GELU_B * before * square))
     half = 0.5 * (1.0 + bent)
-    hidden = split(before * half)
+    hidden_h[...], hidden_l[...] = split(before * half)
     slope = half + 0.5 * before * (1.0 - bent * bent) * (GELU_A * (1.0 + 3.0 * GELU_B * square))
-    cot = cotangent[0]
-    cot_t = cot.T
-    hidden_grad = product(split(down_weight[...]), split(cot_t), 1, 0)
-    before_grad = split(hidden_grad * slope)
-    normal_grad = product(expand, before_grad, 1, 0)
-    grad = cot_t + standardise_pull(normal_grad * gain_column, hat, rstd)
+    before_grad = split(hidden_grad[...] * slope)
+    before_grad_h[...], before_grad_l[...] = before_grad
+    hat_grad = product((expand_h[...], expand_l[...]), before_grad, 1, 0)
+    grad = cot_t[...] + standardise_pull(hat_grad, hat, rstd)
     mixed_grad[...] = grad
-    grad_pair = split(grad)
-    spread_grad = split(product(out_pair, grad_pair, 1, 0))
+    spread_grad = split(product(split(out_weight[...]), split(grad), 1, 0))
     spread_grad_h[...], spread_grad_l[...] = spread_grad
     sums_out = []
     for g in range(heads // GROUP):
@@ -196,31 +234,34 @@
         )
         sums_out.append(fold_blocks(full, mask, head_size))
     out_sum[...] = jnp.concatenate(sums_out, axis=1)
-    width = out_weight.shape[0]
-    early[0:width] = product(spread, grad_pair, 1, 1) * factor
-    early[width : 2 * width] = product(normal, before_grad, 1, 1) * factor
-    early[2 * width : 3 * width] = product(hidden, split(cot), 1, 0) * factor
-    ones = jnp.ones((16, hat.shape[1]), BF16)
-    nt = (((1,), (1,)), ((), ()))
-    gains = split(normal_grad * hat)
-    gain_row = lax.dot_general(ones, gains[0], nt, preferred_element_type=F32)
-    gain_row = gain_row + lax.dot_general(ones, gains[1], nt, preferred_element_type=F32)
-    early[3 * width :] = jnp.zeros((early.shape[0] - 3 * width, width), F32)
-    early[3 * width : 3 * width + 8] = gain_row[:8] * factor
+
+
+def early_kernel(
+    factor,
+    spread_h, spread_l, mixed_grad, hat_h, hat_l, before_grad_h, before_grad_l, hidden_h,
+    hidden_l, cotangent,
+    early,
+):
+    width = mixed_grad.shape[0]
+    spread = (spread_h[...], spread_l[...])
+    early[0:width] = product(spread, split(mixed_grad[...]), 1, 1) * factor
+    hat = (hat_h[...], hat_l[...])
+    before_grad = (before_grad_h[...], before_grad_l[...])
+    early[width : 2 * width] = product(hat, before_grad, 1, 1) * factor
+    hidden = (hidden_h[...], hidden_l[...])
+    early[2 * width :] = product(hidden, split(cotangent[0]), 1, 0) * factor
 
 
 def end_kernel(
     factor, middle_factor,
-    out_sum, sums, middle, attn, weight_h, weight_l, fx_h, fx_l, assign_h, assign_l, normal_h,
-    normal_l, x_t, mixed_grad, spread_grad_h, spread_grad_l, query, key, value, fx_weight,
-    x_weight, logit_weight, temper, gain,
-    x_grad, late,
+    out_sum, sums, middle, attn, weight_h, weight_l, fx_h, fx_l, assign_h, assign_l, hat_h,
+    hat_l, spread_grad_h, spread_grad_l, query, key, value, logit_weight, temper,
+    late, both_grad_h, both_grad_l,
 ):
     head_size, slices = logit_weight.shape
     heads = temper.shape[0]
     rows, lanes = GROUP * head_size, GROUP * slices
-    points = x_t.shape[1]
-    width = x_t.shape[0]
+    width, points = hat_h.shape
     tokens = middle[0:head_size]
     qkv_pair = split(middle[head_size : 4 * head_size])
     result = middle[4 * head_size : 5 * head_size]
@@ -282,13 +323,8 @@
         full = product((assign_h[piece], assign_l[piece]), grads, 1, 1)
         logit_grad = logit_grad + fold_blocks(full, mask, head_size)
     both_grad = split(jnp.concatenate(fx_grads + assign_grads, axis=0))
-    both = split(jnp.concatenate([fx_weight[...], x_weight[...]], axis=1))
-    normal_grad = product(both, both_grad, 1, 0)
-    hat, rstd = standardise(x_t[...])
-    columns = mixed_grad[...] + standardise_pull(normal_grad * column(gain[...]), hat, rstd)
-    x_grad[0] = columns.T
-    normal = (normal_h[...], normal_l[...])
-    matrix = product(normal, both_grad, 1, 1) * factor
+    both_grad_h[...], both_grad_l[...] = both_grad
+    matrix = product((hat_h[...], hat_l[...]), both_grad, 1, 1) * factor
     late[0:width] = matrix[:, :width]
     late[width : 2 * width] = matrix[:, width:]
     logit_grad = logit_grad[:, : 2 * slices] + logit_grad[:, 2 * slices :]
@@ -297,27 +333,77 @@
     late[base:] = jnp.zeros((late.shape[0] - base, width), F32)
     late[base : base + head_size, 0 : 3 * head_size] = map_grad * middle_factor
     late[base : base + head_size, 128 : 128 + slices] = logit_grad * factor
-    ones = jnp.ones((16, points), BF16)
-    nt = (((1,), (1,)), ((), ()))
-    gains = split(normal_grad * hat)
-    gain_row = lax.dot_general(ones, gains[0], nt, preferred_element_type=F32)
-    gain_row = gain_row + lax.dot_general(ones, gains[1], nt, preferred_element_type=F32)
-    late[base + head_size : base + head_size + 8] = gain_row[:8] * factor
+
+
+def rows_kernel(both_h, both_l, both_grad_h, both_grad_l, x_t, mixed_grad, x_grad):
+    both = (both_h[...], both_l[...])
+    hat_grad = product(both, (both_grad_h[...], both_grad_l[...]), 1, 0)
+    hat, rstd = standardise(x_t[...])
+    x_grad[0] = (mixed_grad[...] + standardise_pull(hat_grad, hat, rstd)).T
+
+
+def early_out_kernel(
+    early, gain, expand_weight,
+    matrices, gain_row, scaled, sems,
+):
+    width = gain.shape[1]
+    copies = [
+        pltpu.make_async_copy(early.at[0:width], matrices.at[2], sems.at[0]),
+        pltpu.make_async_copy(early.at[2 * width : 3 * width], matrices.at[4], sems.at[1]),
+        pltpu.make_async_copy(scaled, matrices.at[3], sems.at[2]),
+    ]
+    copies[0].start()
+    copies[1].start()
+    grad = early[width : 2 * width]
+    scaled[...] = grad * column(gain[...])
+    copies[2].start()
+    gain_row[...] = row_total(grad, expand_weight[...])
+    for copy in copies:
+        copy.wait()
+
+
+def late_out_kernel(
+    late, gain, fx_weight, x_weight, gain_row, given,
+    matrices, maps, logit, gains, scaled, sems,
+):
+    width = gain.shape[1]
+    head_size, slices = logit.shape
+    gain_column = column(gain[...])
+    copies = []
+    total = jnp.zeros((1, width), F32)
+    for i, weight in enumerate((fx_weight, x_weight)):
+        grad = late[i * width : (i + 1) * width]
+        scaled[i] = grad * gain_column
+        copies.append(pltpu.make_async_copy(scaled.at[i], matrices.at[i], sems.at[i]))
+        copies[i].start()
+        total = total + row_total(grad, weight[...])
+    base = 2 * width
+    for i in range(3):
+        maps[i] = late[base : base + head_size, i * head_size : (i + 1) * head_size]
+    logit[...] = late[base : base + head_size, 128 : 128 + slices]
+    gains[...] = jnp.concatenate([total, gain_row[...]], axis=0)
+    for copy in copies:
+        copy.wait()
 
 
 VMEM = pl.BlockSpec(memory_space=pltpu.VMEM)
 SMEM = pl.BlockSpec(memory_space=pltpu.SMEM)
 
 
-def call(body, name, in_specs, out_shape, args, flops):
+HBM = pl.BlockSpec(memory_space=pltpu.HBM)
+
+
+def call(body, name, in_specs, out_specs, out_shape, args, flops, scratch=(), aliases=None):
     return pl.pallas_call(
         body,
         name=name,
         in_specs=in_specs,
-        out_specs=[VMEM] * len(out_shape),
+        out_specs=out_specs,
         out_shape=out_shape,
+        scratch_shapes=scratch,
+        input_output_aliases=aliases or {},
         compiler_params=pltpu.CompilerParams(vmem_limit_bytes=VMEM_LIMIT),
-        cost_estimate=pl.CostEstimate(flops=flops, bytes_accessed=4 << 20, transcendentals=0),
+        cost_estimate=pl.CostEstimate(flops=flops, bytes_accessed=1 << 20, transcendentals=0),
     )(*args)
 
 
@@ -345,12 +431,8 @@
     return count & (count - 1) == 0
 
 
-def sum_points(value, sizes):
-    if not power(sizes[1]):
-        return lax.psum(value, "point")
-    for bit in bits(sizes[1]):
-        value = value + swap(value, flip(1, bit), sizes)
-    return value
+def tie(*values):
+    return lax.optimization_barrier(values)
 
 
 def halve(value, upper):
@@ -366,31 +448,51 @@
     return jnp.concatenate([low, high], axis=0)
 
 
-def sum_all(value, sizes):
+def point_steps(sizes):
+    if not power(sizes[1]):
+        return [lambda value: lax.psum(value, "point")]
+
+    def step(bit):
+        return lambda value: value + swap(value, flip(1, bit), sizes)
+
+    return [step(bit) for bit in bits(sizes[1])]
+
+
+def all_steps(sizes):
     dp, point = sizes
     if not (power(dp) and power(point)) or dp < 2 or point < 2:
-        return lax.psum(value, ("dp", "point"))
+        return [lambda value: lax.psum(value, ("dp", "point"))]
     d, p = lax.axis_index("dp"), lax.axis_index("point")
-    steps = [(1, 1)] + [(0, b) for b in bits(dp)[1:]] + [(1, b) for b in bits(point)[1:]]
-    turn = len(steps) // 2
-    orders = [steps, steps[turn:] + steps[:turn]]
+    axes = [(1, 1)] + [(0, b) for b in bits(dp)[1:]] + [(1, b) for b in bits(point)[1:]]
+    turned = list(axes)
+    for i in range(0, len(axes) - 1, 2):
+        turned[i], turned[i + 1] = axes[i + 1], axes[i]
 
     def move(i):
-        choices = [flip(*order[i]) for order in orders]
+        choices = [flip(*order[i]) for order in (axes, turned)]
         return lambda d, p: choices[d & 1](d, p)
 
     core = d & 1
-    mine, other = halve(value, core)
-    value = mine + swap(other, flip(0, 1), sizes)
-    axis_bits = [order[0] for order in orders]
-    places = [((d if a == 0 else p) // b) & 1 for a, b in axis_bits]
+    places = [((d if order[0][0] == 0 else p) & order[0][1]) // order[0][1]
+              for order in (axes, turned)]
     upper = jnp.where(core == 0, places[0], places[1])
-    mine, other = halve(value, upper)
-    value = mine + swap(other, move(0), sizes)
-    for i in range(1, len(steps)):
-        value = value + swap(value, move(i), sizes)
-    value = join(value, swap(value, move(0), sizes), upper)
-    return join(value, swap(value, flip(0, 1), sizes), core)
+
+    def scatter(upper, moves):
+        def step(value):
+            mine, other = halve(value, upper)
+            return mine + swap(other, moves, sizes)
+        return step
+
+    def add(moves):
+        return lambda value: value + swap(value, moves, sizes)
+
+    def gather(upper, moves):
+        return lambda value: join(value, swap(value, moves, sizes), upper)
+
+    cores = flip(0, 1)
+    steps = [scatter(core, cores), scatter(upper, move(0))]
+    steps += [add(move(i)) for i in range(1, len(axes))]
+    return steps + [gather(upper, move(0)), gather(core, cores)]
 
 
 def shards(
@@ -409,47 +511,103 @@
     def shape(*dims, dtype=F32):
         return jax.ShapeDtypeStruct(dims, dtype)
 
-    half = functools.partial(shape, dtype=BF16)
-    pair = [half(width, points)] * 2
+    def pair(*dims):
+        return [shape(*dims, dtype=BF16)] * 2
+
+    tall = pair(width, points)
     dense = 6 * points * width * width
-    (w_h, w_l, fx_h, fx_l, as_h, as_l, n_h, n_l, x_t, sums) = call(
-        front_kernel, "front", [VMEM] * 5 + [SMEM],
-        [half(total, points)] * 2 + pair * 3 + [shape(width, points), shape(head_size + 8, total)],
+    (w_h, w_l, fx_h, fx_l, as_h, as_l, h1_h, h1_l, x_t, both_h, both_l, sums) = call(
+        front_kernel, "front", [HBM] * 6, [VMEM] * 12,
+        pair(total, points) + tall * 3
+        + [shape(width, points)] + pair(width, 2 * width) + [shape(head_size + 8, total)],
         (inputs, gain_one, fx_weight, x_weight, slice_logit_weight, temper),
         4 * dense,
-    )
-    sums = sum_points(sums, sizes)
-    out_sum, mixed_grad, sg_h, sg_l, middle, attn, early = call(
-        functools.partial(back_kernel, factor), "back", [VMEM] * 12,
-        [shape(head_size, total), shape(width, points)] + pair
-        + [shape(5 * head_size, total), shape(2 * slices, total), shape(3 * width + 32, width)],
-        (sums, x_t, w_h, w_l, cotangent, slice_query_matrix, slice_key_matrix,
-         slice_value_matrix, out_weight, gain_two, expand_weight, down_weight),
-        10 * dense,
-    )
-    out_sum = sum_points(out_sum, sizes)
-    input_grad, late = call(
+        [
+            pltpu.VMEM(inputs.shape, F32), pltpu.VMEM((1, width), F32),
+            pltpu.VMEM((width, width), F32), pltpu.VMEM((width, width), F32),
+            pltpu.VMEM((head_size, slices), F32), pltpu.SMEM((heads,), F32),
+            pltpu.SemaphoreType.DMA((6,)),
+        ],
+    )
+    ready = call(
+        ready_kernel, "ready", [VMEM] * 8, [VMEM] * 10,
+        [shape(width, points)] * 2 + pair(width, width) * 3 + pair(3 * head_size, head_size),
+        (cotangent, out_weight, gain_two, expand_weight, down_weight, slice_query_matrix,
+         slice_key_matrix, slice_value_matrix),
+        2 * dense,
+    )
+    for step in point_steps(sizes):
+        sums = step(sums)
+    cot_t, hidden_grad, out_t_h, out_t_l, ex_h, ex_l, ext_h, ext_l, maps_h, maps_l = ready
+    (out_sum, mixed_grad, sg_h, sg_l, middle, attn, sp_h, sp_l, h2_h, h2_l, bg_h, bg_l, hd_h,
+     hd_l) = call(
+        back_kernel, "back", [VMEM] * 15, [VMEM] * 14,
+        [shape(head_size, total), shape(width, points)] + tall
+        + [shape(5 * head_size, total), shape(2 * slices, total)] + tall * 4,
+        (sums, x_t, w_h, w_l, cot_t, hidden_grad, out_weight, out_t_h, out_t_l, ex_h, ex_l,
+         ext_h, ext_l, maps_h, maps_l),
+        6 * dense,
+    )
+    early_value = call(
+        functools.partial(early_kernel, factor), "early", [VMEM] * 10, VMEM,
+        shape(3 * width, width),
+        (sp_h, sp_l, mixed_grad, h2_h, h2_l, bg_h, bg_l, hd_h, hd_l, cotangent),
+        3 * dense,
+    )
+    early_steps = all_steps(sizes)
+    early_at = 0
+    for i, step in enumerate(point_steps(sizes)):
+        before = out_sum
+        if early_at < len(early_steps) and i > 0:
+            early_new = early_steps[early_at](early_value)
+            early_at += 1
+        else:
+            early_new = early_value
+        out_sum = step(before)
+        out_sum, early_value = tie(out_sum, early_new)
+    if early_at < len(early_steps):
+        early_value = early_steps[early_at](early_value)
+        early_at += 1
+    late, bgr_h, bgr_l = call(
         functools.partial(end_kernel, factor, factor / sizes[1]), "end",
-        [VMEM] * 22 + [SMEM] + [VMEM],
-        [shape(1, points, width), shape(2 * width + head_size + 32, width)],
-        (out_sum, sums, middle, attn, w_h, w_l, fx_h, fx_l, as_h, as_l, n_h, n_l, x_t,
-         mixed_grad, sg_h, sg_l, slice_query_matrix, slice_key_matrix, slice_value_matrix,
-         fx_weight, x_weight, slice_logit_weight, temper, gain_one),
-        10 * dense,
-    )
-    early = sum_all(early, sizes)
-    late = sum_all(late, sizes)
-    matrix_grads = jnp.concatenate([late[: 2 * width], early[: 3 * width]], axis=0)
-    small = late[2 * width : 2 * width + head_size]
-    maps = jnp.stack([small[:, i * head_size : (i + 1) * head_size] for i in range(3)])
-    gains = jnp.stack([late[2 * width + head_size], early[3 * width]])
-    return (
-        input_grad,
-        matrix_grads.reshape(5, width, width),
-        maps,
-        small[:, 128 : 128 + slices],
-        gains,
-    )
+        [VMEM] * 18 + [SMEM], [VMEM] * 3,
+        [shape(2 * width + head_size, width)] + pair(2 * width, points),
+        (out_sum, sums, middle, attn, w_h, w_l, fx_h, fx_l, as_h, as_l, h1_h, h1_l, sg_h, sg_l,
+         slice_query_matrix, slice_key_matrix, slice_value_matrix, slice_logit_weight, temper),
+        8 * dense,
+    )
+    input_grad = call(
+        rows_kernel, "rows", [VMEM] * 6, VMEM, shape(1, points, width),
+        (both_h, both_l, bgr_h, bgr_l, x_t, mixed_grad),
+        2 * dense,
+    )
+    for i, step in enumerate(all_steps(sizes)):
+        if i > 0 and early_at < len(early_steps):
+            early_new = early_steps[early_at](early_value)
+            early_at += 1
+            late = step(late)
+            late, early_value = tie(late, early_new)
+        else:
+            late = step(late)
+            late, early_value = tie(late, early_value)
+    any_space = pl.BlockSpec(memory_space=pltpu.HBM)
+    matrices, gain_row = call(
+        early_out_kernel, "early_out", [VMEM] * 3, [any_space, VMEM],
+        [shape(5, width, width), shape(1, width)],
+        (early_value, gain_two, expand_weight),
+        dense // 8,
+        [pltpu.VMEM((width, width), F32), pltpu.SemaphoreType.DMA((3,))],
+    )
+    matrices, maps, logit, gains = call(
+        late_out_kernel, "late_out", [VMEM] * 5 + [any_space], [any_space] + [VMEM] * 3,
+        [shape(5, width, width), shape(3, head_size, head_size), shape(head_size, slices),
+         shape(2, width)],
+        (late, gain_one, fx_weight, x_weight, gain_row, matrices),
+        dense // 8,
+        [pltpu.VMEM((2, width, width), F32), pltpu.SemaphoreType.DMA((2,))],
+        {5: 0},
+    )
+    return input_grad, matrices, maps, logit, gains
 
 
 def solution(mesh):

time: 101 us -> 132 us (1.31)
  local copies, waits for them, and re-layouts: 13.1 us -> 37.4 us
  waiting for transfers between devices: 33.3 us -> 42.2 us
  starting transfers between devices: 31.6 us -> 26.9 us
    unnamed x60 -> x130, local copies, waits for them, and re-layouts: 9.54 us -> 36.6 us
    ppermute x20, waiting for transfers between devices: 33.3 us -> 42.2 us  [swap(): return lax.ppermute(value, ('dp', 'point'), pairs)]
    ppermute x20, starting transfers between devices: 31.6 us -> 26.9 us  [swap(): return lax.ppermute(value, ('dp', 'point'), pairs)]
    add x16, other arithmetic: 1.39 us -> 4.69 us  [the longest x4 2.04 us: step(): return mine + swap(other, moves, sizes)]
    dynamic_slice x4, local copies, waits for them, and re-layouts: 2.87 us -> 0.8 us  [halve(): other = lax.dynamic_slice_in_dim(value, (1 - upper) * half, half, 0)]
    pallas_call x3 -> x8, Pallas kernels: 17.8 us -> 18.1 us  [call(): pl.pallas_call(body, name=name, in_specs=in_specs, out_specs=out_specs, o...]
  transfers between devices with their start and end apart: 20 -> 20, of which waited for: 13 -> 13; matrix products, arithmetic and copies ran while one was open for 6% -> 2% of each run, Pallas kernels for 7% -> 2%
where the time goes in v2:
time: 132 us; the launch traced here: 131 us
  waiting for transfers between devices  42.2 us (32%)
  local copies, waits for them, and re-layouts  37.4 us (28%)
  starting transfers between devices  26.9 us (20%)
  Pallas kernels  18.1 us (14%)
  other arithmetic  4.99 us (4%)
    ppermute x20, waiting for transfers between devices, swap(): return lax.ppermute(value, ('dp', 'point'), pairs)  42.2 us
    unnamed x130, local copies, waits for them, and re-layouts  36.6 us
    ppermute x20, starting transfers between devices, swap(): return lax.ppermute(value, ('dp', 'point'), pairs)  26.9 us
    pallas_call x8, Pallas kernels, call(): pl.pallas_call(body, name=name, in_specs=in_specs, out_specs=out_specs, o...  18.1 us
  transfers between devices with their start and end apart: 20, of which 13 were waited for; matrix products, arithmetic and copies ran while one was open for 2% of the time, Pallas kernels for 2%

profile of v2, /device:TPU:0, one launch (start us, length us, event | category | flops | bytes accessed | tf_op | source)
XLA Modules:
  0.0 130.8 jit_solution(13862018923928501919)
XLA Ops:
  5.7 3.3 %front.1 = (bf16[512,512]{1,0:T(8,128)(2,1)S(1)}, bf16[512,512]{1,0:T(8,128)(2,1)S(1)}, bf16[256,512]{1,0:T(8,128)(2,1)S(1)}, bf16[256,512]{1,0:T(8,128)(2,1)S(1...) custom-call(f32[1,512,256]{2,1,0:T(8,128)S(1)} %copy-done.26, ...), custom_call_target="tpu_custom_call" | custom-call | flops 805306368 | bytes 1048576 | tf_op jit(solution)/shard_map/front/pallas_call | solution.py:397
  12.6 3.0 %collective-permute-start = (f32[40,512]{1,0:T(8,128)S(1)}, f32[40,512]{1,0:T(8,128)S(1)}, u32[]{:S(2)}, u32[]{:S(2)}) collective-permute-start(f32[40,512]{1,0:T(8,128)S(1)} %get-tuple-element.72), channel_id=1, source_target_pairs={{0,1},{1,0},{2,3},{3,2},{4,5},{5,4},{6,7},{7,6},{8,9},{9,8},{10,11... | collective-permute-start | bytes 245768 | tf_op jit(solution)/shard_map/ppermute | solution.py:417
  15.6 2.4 %collective-permute-done = f32[40,512]{1,0:T(8,128)S(1)} collective-permute-done((f32[40,512]{1,0:T(8,128)S(1)}, f32[40,512]{1,0:T(8,128)S(1)}, u32[]{:S(2)}, u32[]{:S(2)}) %collective-permute-start) | collective-permute-done | bytes 81952 | tf_op jit(solution)/shard_map/ppermute | solution.py:417
  18.1 2.1 %collective-permute-start.1 = (f32[40,512]{1,0:T(8,128)S(1)}, f32[40,512]{1,0:T(8,128)S(1)}, u32[]{:S(2)}, u32[]{:S(2)}) collective-permute-start(f32[40,512]{1,0:T(8,128)S(1)} %add.74), channel_id=1, source_target_pairs={{0,2},{1,3},{2,0},{3,1},{4,6},{5,7},{6,4},{7,5},{8,10},{9,11},{10,... | collective-permute-start | bytes 245768 | tf_op jit(solution)/shard_map/ppermute | solution.py:417
  20.2 2.4 %collective-permute-done.1 = f32[40,512]{1,0:T(8,128)S(1)} collective-permute-done((f32[40,512]{1,0:T(8,128)S(1)}, f32[40,512]{1,0:T(8,128)S(1)}, u32[]{:S(2)}, u32[]{:S(2)}) %collective-permute-start.1) | collective-permute-done | bytes 81952 | tf_op jit(solution)/shard_map/ppermute | solution.py:417
  22.6 3.1 %collective-permute-start.2 = (f32[40,512]{1,0:T(8,128)S(1)}, f32[40,512]{1,0:T(8,128)S(1)}, u32[]{:S(2)}, u32[]{:S(2)}) collective-permute-start(f32[40,512]{1,0:T(8,128)S(1)} %add.75), channel_id=1, source_target_pairs={{0,4},{1,5},{2,6},{3,7},{4,0},{5,1},{6,2},{7,3},{8,12},{9,13},{10,... | collective-permute-start | bytes 245768 | tf_op jit(solution)/shard_map/ppermute | solution.py:417
  26.4 1.8 %collective-permute-done.2 = f32[40,512]{1,0:T(8,128)S(1)} collective-permute-done((f32[40,512]{1,0:T(8,128)S(1)}, f32[40,512]{1,0:T(8,128)S(1)}, u32[]{:S(2)}, u32[]{:S(2)}) %collective-permute-start.2) | collective-permute-done | bytes 81952 | tf_op jit(solution)/shard_map/ppermute | solution.py:417
  28.2 4.2 %back.1 = (f32[32,512]{1,0:T(8,128)S(1)}, f32[256,512]{1,0:T(8,128)S(1)}, bf16[256,512]{1,0:T(8,128)(2,1)S(1)}, bf16[256,512]{1,0:T(8,128)(2,1)S(1)}, f32[160,51...) custom-call(f32[40,512]{1,0:T(8,128)S(1)} %add.76.sums, ...), custom_call_target="tpu_custom_call" | custom-call | flops 1207959552 | bytes 1048576 | tf_op jit(solution)/shard_map/back/pallas_call | solution.py:397
  40.2 1.8 %collective-permute-start.3 = (f32[32,512]{1,0:T(8,128)S(1)}, f32[32,512]{1,0:T(8,128)}, u32[]{:S(2)}, u32[]{:S(2)}) collective-permute-start(f32[32,512]{1,0:T(8,128)S(1)} %get-tuple-element.86), channel_id=1, source_target_pairs={{0,1},{1,0},{2,3},{3,2},{4,5},{5,4},{6,7},{7,6},{8,9},{9,8},{10,11... | collective-permute-start | bytes 196616 | tf_op jit(solution)/shard_map/ppermute | solution.py:417
  50.4 1.7 %collective-permute-start.4 = (f32[32,512]{1,0:T(8,128)S(1)}, f32[32,512]{1,0:T(8,128)S(1)}, u32[]{:S(2)}, u32[]{:S(2)}) collective-permute-start(f32[32,512]{1,0:T(8,128)S(1)} %add.77), channel_id=1, source_target_pairs={{0,2},{1,3},{2,0},{3,1},{4,6},{5,7},{6,4},{7,5},{8,10},{9,11},{10,... | collective-permute-start | bytes 196616 | tf_op jit(solution)/shard_map/ppermute | solution.py:417
  52.1 2.8 %collective-permute-done.4 = f32[32,512]{1,0:T(8,128)S(1)} collective-permute-done((f32[32,512]{1,0:T(8,128)S(1)}, f32[32,512]{1,0:T(8,128)S(1)}, u32[]{:S(2)}, u32[]{:S(2)}) %collective-permute-start.4) | collective-permute-done | bytes 65568 | tf_op jit(solution)/shard_map/ppermute | solution.py:417
  55.5 3.4 %collective-permute-start.6 = (f32[32,512]{1,0:T(8,128)S(1)}, f32[32,512]{1,0:T(8,128)S(1)}, u32[]{:S(2)}, u32[]{:S(2)}) collective-permute-start(f32[32,512]{1,0:T(8,128)S(1)} %add.78), channel_id=1, source_target_pairs={{0,4},{1,5},{2,6},{3,7},{4,0},{5,1},{6,2},{7,3},{8,12},{9,13},{10,... | collective-permute-start | bytes 196616 | tf_op jit(solution)/shard_map/ppermute | solution.py:417
  58.9 4.2 %collective-permute-done.6 = f32[32,512]{1,0:T(8,128)S(1)} collective-permute-done((f32[32,512]{1,0:T(8,128)S(1)}, f32[32,512]{1,0:T(8,128)S(1)}, u32[]{:S(2)}, u32[]{:S(2)}) %collective-permute-start.6) | collective-permute-done | bytes 65568 | tf_op jit(solution)/shard_map/ppermute | solution.py:417
  75.5 4.9 %end.1 = (f32[544,256]{1,0:T(8,128)S(1)}, bf16[512,512]{1,0:T(8,128)(2,1)S(1)}, bf16[512,512]{1,0:T(8,128)(2,1)S(1)}) custom-call(f32[32,512]{1,0:T(8,128)S(1)} %add.82.out_sum, f32[40,512]{1,0:T(8,128)S(1)} %add.76.sums, f32[160,512]{1,0:T(8,128)S(1)} %copy-done.44, f32[128,512]{1,0:T(8,128)S(1)} %copy-done.50, bf16[512,512]{1,0:T(8,128)(2,1)S(1)} %copy-done.40, ...), custom_call_target="tpu_custom_call" | custom-call | flops 1610612736 | bytes 1048576 | tf_op jit(solution)/shard_map/end/pallas_call | solution.py:397
  81.2 5.7 %collective-permute-done.9 = f32[192,256]{1,0:T(8,128)} collective-permute-done((f32[192,256]{1,0:T(8,128)S(1)}, f32[192,256]{1,0:T(8,128)}, u32[]{:S(2)}, u32[]{:S(2)}) %collective-permute-start.9) | collective-permute-done | bytes 196640 | tf_op jit(solution)/shard_map/ppermute | solution.py:417
  91.7 3.7 %collective-permute-done.10 = f32[136,256]{1,0:T(8,128)S(1)} collective-permute-done((f32[136,256]{1,0:T(8,128)S(1)}, f32[136,256]{1,0:T(8,128)S(1)}, u32[]{:S(2)}, u32[]{:S(2)}) %collective-permute-start.10) | collective-permute-done | bytes 139296 | tf_op jit(solution)/shard_map/ppermute | solution.py:417
  97.9 2.5 %collective-permute-start.13 = (f32[192,256]{1,0:T(8,128)S(1)}, f32[192,256]{1,0:T(8,128)S(1)}, u32[]{:S(2)}, u32[]{:S(2)}) collective-permute-start(f32[192,256]{1,0:T(8,128)S(1)} %add.93), channel_id=1, source_target_pairs={{0,4},{1,5},{2,6},{3,7},{4,0},{5,1},{6,2},{7,3},{8,10},{9,11},{10,... | collective-permute-start | bytes 589832 | tf_op jit(solution)/shard_map/ppermute | solution.py:417
  101.8 3.6 %collective-permute-done.12 = f32[136,256]{1,0:T(8,128)S(1)} collective-permute-done((f32[136,256]{1,0:T(8,128)S(1)}, f32[136,256]{1,0:T(8,128)S(1)}, u32[]{:S(2)}, u32[]{:S(2)}) %collective-permute-start.12) | collective-permute-done | bytes 139296 | tf_op jit(solution)/shard_map/ppermute | solution.py:417
  107.1 3.9 %collective-permute-start.14 = (f32[136,256]{1,0:T(8,128)S(1)}, f32[136,256]{1,0:T(8,128)S(1)}, u32[]{:S(2)}, u32[]{:S(2)}) collective-permute-start(f32[136,256]{1,0:T(8,128)S(1)} %add.94), channel_id=1, source_target_pairs={{0,2},{1,3},{2,0},{3,1},{4,6},{5,7},{6,4},{7,5},{8,12},{9,13},{10,... | collective-permute-start | bytes 417800 | tf_op jit(solution)/shard_map/ppermute | solution.py:417
  110.9 3.0 %collective-permute-done.14 = f32[136,256]{1,0:T(8,128)S(1)} collective-permute-done((f32[136,256]{1,0:T(8,128)S(1)}, f32[136,256]{1,0:T(8,128)S(1)}, u32[]{:S(2)}, u32[]{:S(2)}) %collective-permute-start.14) | collective-permute-done | bytes 139296 | tf_op jit(solution)/shard_map/ppermute | solution.py:417
  115.4 4.9 %collective-permute-done.16 = f32[136,256]{1,0:T(8,128)S(1)} collective-permute-done((f32[136,256]{1,0:T(8,128)S(1)}, f32[136,256]{1,0:T(8,128)S(1)}, u32[]{:S(2)}, u32[]{:S(2)}) %collective-permute-start.16) | collective-permute-done | bytes 139296 | tf_op jit(solution)/shard_map/ppermute | solution.py:417
  120.6 5.0 %collective-permute-done.18 = f32[136,256]{1,0:T(8,128)S(1)} collective-permute-done((f32[136,256]{1,0:T(8,128)S(1)}, f32[136,256]{1,0:T(8,128)S(1)}, u32[]{:S(2)}, u32[]{:S(2)}) %collective-permute-start.18) | collective-permute-done | bytes 139296 | tf_op jit(solution)/shard_map/ppermute | solution.py:417
  125.7 1.6 %rows.1 = f32[1,512,256]{2,1,0:T(8,128)} custom-call(bf16[256,512]{1,0:T(8,128)(2,1)S(1)} %get-tuple-element.70.both_h, bf16[256,512]{1,0:T(8,128)(2,1)S(1)} %copy-done.3, bf16[512,512]{1,0:T(8,128)(2,1)S(1)} %get-tuple-element.111.both_grad_h, bf16[512,512]{1,0:T(8,128)(2,1)S(1)} %get-tuple-element.112.both_grad_l, f32[256,512]{1,0:T(8,128)S(1)} %get-tuple-element.73.x_t, ...), custom_call_target="tpu_custom_call" | custom-call | flops 402653184 | bytes 1048576 | tf_op jit(solution)/shard_map/rows/pallas_call | solution.py:397
  129.1 1.7 %late_out.1 = (f32[5,256,256]{2,1,0:T(8,128)}, f32[3,32,32]{2,1,0:T(8,128)}, f32[32,64]{1,0:T(8,128)}, f32[2,256]{1,0:T(2,128)}) custom-call(f32[544,256]{1,0:T(8,128)S(1)} %pad_maximum_fusion.1.late, f32[1,256]{1,0:T(1,128)S(1)} %bitcast.5, f32[256,256]{1,0:T(8,128)S(1)} %copy-done.5, f32[256,256]{1,0:T(8,128)S(1)} %copy-done.7, ...), custom_call_target="tpu_custom_call", output_to_operand_aliasing={{0}: (5, {})} | custom-call | flops 25165824 | bytes 1048576 | tf_op jit(solution)/shard_map/late_out/pallas_call | solution.py:397
  (182 shorter events, 52.9 us)
Async XLA Ops:
  5.6 20.1 %copy-start.22 = (f32[256]{0:T(256)S(1)}, f32[256]{0:T(256)}, u32[]{:S(2)}) copy-start(f32[256]{0:T(256)} %param.25) | copy-start | bytes 3076
  5.6 20.1 %copy-start.27 = (f32[256,256]{1,0:T(8,128)S(1)}, f32[256,256]{1,0:T(8,128)}, u32[]{:S(2)}) copy-start(f32[256,256]{1,0:T(8,128)} %down_weight.1) | copy-start | bytes 786436
  5.6 20.1 %copy-start.28 = (f32[256,256]{1,0:T(8,128)S(1)}, f32[256,256]{1,0:T(8,128)}, u32[]{:S(2)}) copy-start(f32[256,256]{1,0:T(8,128)} %out_weight.3) | copy-start | bytes 786436
  5.7 20.1 %copy-start.31 = (f32[32,32]{1,0:T(8,128)S(1)}, f32[32,32]{1,0:T(8,128)}, u32[]{:S(2)}) copy-start(f32[32,32]{1,0:T(8,128)} %query.3) | copy-start | bytes 12292
  12.6 5.4 %collective-permute-start = (f32[40,512]{1,0:T(8,128)S(1)}, f32[40,512]{1,0:T(8,128)S(1)}, u32[]{:S(2)}, u32[]{:S(2)}) collective-permute-start(f32[40,512]{1,0:T(8,128)S(1)} %get-tuple-element.72), channel_id=1, source_target_pairs={{0,1},{1,0},{2,3},{3,2},{4,5},{5,4},{6,7},{7,6},{8,9},{9,8},{10,11... | collective-permute-start | bytes 245768 | tf_op jit(solution)/shard_map/ppermute | solution.py:417
  18.1 4.6 %collective-permute-start.1 = (f32[40,512]{1,0:T(8,128)S(1)}, f32[40,512]{1,0:T(8,128)S(1)}, u32[]{:S(2)}, u32[]{:S(2)}) collective-permute-start(f32[40,512]{1,0:T(8,128)S(1)} %add.74), channel_id=1, source_target_pairs={{0,2},{1,3},{2,0},{3,1},{4,6},{5,7},{6,4},{7,5},{8,10},{9,11},{10,... | collective-permute-start | bytes 245768 | tf_op jit(solution)/shard_map/ppermute | solution.py:417
  22.6 5.5 %collective-permute-start.2 = (f32[40,512]{1,0:T(8,128)S(1)}, f32[40,512]{1,0:T(8,128)S(1)}, u32[]{:S(2)}, u32[]{:S(2)}) collective-permute-start(f32[40,512]{1,0:T(8,128)S(1)} %add.75), channel_id=1, source_target_pairs={{0,4},{1,5},{2,6},{3,7},{4,0},{5,1},{6,2},{7,3},{8,12},{9,13},{10,... | collective-permute-start | bytes 245768 | tf_op jit(solution)/shard_map/ppermute | solution.py:417
  40.2 9.3 %collective-permute-start.3 = (f32[32,512]{1,0:T(8,128)S(1)}, f32[32,512]{1,0:T(8,128)}, u32[]{:S(2)}, u32[]{:S(2)}) collective-permute-start(f32[32,512]{1,0:T(8,128)S(1)} %get-tuple-element.86), channel_id=1, source_target_pairs={{0,1},{1,0},{2,3},{3,2},{4,5},{5,4},{6,7},{7,6},{8,9},{9,8},{10,11... | collective-permute-start | bytes 196616 | tf_op jit(solution)/shard_map/ppermute | solution.py:417
  50.4 4.6 %collective-permute-start.5 = (f32[384,256]{1,0:T(8,128)S(1)}, f32[384,256]{1,0:T(8,128)S(1)}, u32[]{:S(2)}, u32[]{:S(2)}) collective-permute-start(f32[384,256]{1,0:T(8,128)S(1)} %constant_dynamic-slice_fusion.3), channel_id=1, source_target_pairs={{0,8},{1,9},{2,10},{3,11},{4,12},{5,13},{6,14},{7,15},{8,0},{9,1},... | collective-permute-start | bytes 1179656 | tf_op jit(solution)/shard_map/ppermute | solution.py:417
  50.4 4.5 %collective-permute-start.4 = (f32[32,512]{1,0:T(8,128)S(1)}, f32[32,512]{1,0:T(8,128)S(1)}, u32[]{:S(2)}, u32[]{:S(2)}) collective-permute-start(f32[32,512]{1,0:T(8,128)S(1)} %add.77), channel_id=1, source_target_pairs={{0,2},{1,3},{2,0},{3,1},{4,6},{5,7},{6,4},{7,5},{8,10},{9,11},{10,... | collective-permute-start | bytes 196616 | tf_op jit(solution)/shard_map/ppermute | solution.py:417
  55.1 8.0 %collective-permute-start.7 = (f32[192,256]{1,0:T(8,128)S(1)}, f32[192,256]{1,0:T(8,128)S(1)}, u32[]{:S(2)}, u32[]{:S(2)}) collective-permute-start(f32[192,256]{1,0:T(8,128)S(1)} %constant_dynamic-slice_fusion.2), channel_id=1, source_target_pairs={{0,1},{1,0},{2,3},{3,2},{4,5},{5,4},{6,7},{7,6},{8,24},{9,25},{10,... | collective-permute-start | bytes 589832 | tf_op jit(solution)/shard_map/ppermute | solution.py:417
  55.5 7.6 %collective-permute-start.6 = (f32[32,512]{1,0:T(8,128)S(1)}, f32[32,512]{1,0:T(8,128)S(1)}, u32[]{:S(2)}, u32[]{:S(2)}) collective-permute-start(f32[32,512]{1,0:T(8,128)S(1)} %add.78), channel_id=1, source_target_pairs={{0,4},{1,5},{2,6},{3,7},{4,0},{5,1},{6,2},{7,3},{8,12},{9,13},{10,... | collective-permute-start | bytes 196616 | tf_op jit(solution)/shard_map/ppermute | solution.py:417
  81.1 7.4 %collective-permute-start.8 = (f32[272,256]{1,0:T(8,128)}, f32[272,256]{1,0:T(8,128)}, u32[]{:S(2)}, u32[]{:S(2)}) collective-permute-start(f32[272,256]{1,0:T(8,128)} %constant_dynamic-slice_fusion.1), channel_id=1, source_target_pairs={{0,8},{1,9},{2,10},{3,11},{4,12},{5,13},{6,14},{7,15},{8,0},{9,1},... | collective-permute-start | bytes 835592 | tf_op jit(solution)/shard_map/ppermute | solution.py:417
  81.1 5.8 %collective-permute-start.9 = (f32[192,256]{1,0:T(8,128)S(1)}, f32[192,256]{1,0:T(8,128)}, u32[]{:S(2)}, u32[]{:S(2)}) collective-permute-start(f32[192,256]{1,0:T(8,128)S(1)} %dynamic-slice_add_fusion.2), channel_id=1, source_target_pairs={{0,16},{1,17},{2,18},{3,19},{4,20},{5,21},{6,22},{7,23},{8,9},{9,8... | collective-permute-start | bytes 589832 | tf_op jit(solution)/shard_map/ppermute | solution.py:417
  90.3 5.1 %collective-permute-start.10 = (f32[136,256]{1,0:T(8,128)S(1)}, f32[136,256]{1,0:T(8,128)S(1)}, u32[]{:S(2)}, u32[]{:S(2)}) collective-permute-start(f32[136,256]{1,0:T(8,128)S(1)} %constant_dynamic-slice_fusion), channel_id=1, source_target_pairs={{0,1},{1,0},{2,3},{3,2},{4,5},{5,4},{6,7},{7,6},{8,24},{9,25},{10,... | collective-permute-start | bytes 417800 | tf_op jit(solution)/shard_map/ppermute | solution.py:417
  91.2 6.6 %collective-permute-start.11 = (f32[192,256]{1,0:T(8,128)}, f32[192,256]{1,0:T(8,128)S(1)}, u32[]{:S(2)}, u32[]{:S(2)}) collective-permute-start(f32[192,256]{1,0:T(8,128)} %add.89), channel_id=1, source_target_pairs={{0,2},{1,3},{2,0},{3,1},{4,6},{5,7},{6,4},{7,5},{8,12},{9,13},{10,... | collective-permute-start | bytes 589832 | tf_op jit(solution)/shard_map/ppermute | solution.py:417
  97.9 8.8 %collective-permute-start.13 = (f32[192,256]{1,0:T(8,128)S(1)}, f32[192,256]{1,0:T(8,128)S(1)}, u32[]{:S(2)}, u32[]{:S(2)}) collective-permute-start(f32[192,256]{1,0:T(8,128)S(1)} %add.93), channel_id=1, source_target_pairs={{0,4},{1,5},{2,6},{3,7},{4,0},{5,1},{6,2},{7,3},{8,10},{9,11},{10,... | collective-permute-start | bytes 589832 | tf_op jit(solution)/shard_map/ppermute | solution.py:417
  100.3 5.1 %collective-permute-start.12 = (f32[136,256]{1,0:T(8,128)S(1)}, f32[136,256]{1,0:T(8,128)S(1)}, u32[]{:S(2)}, u32[]{:S(2)}) collective-permute-start(f32[136,256]{1,0:T(8,128)S(1)} %dynamic-slice_add_fusion.3), channel_id=1, source_target_pairs={{0,16},{1,17},{2,18},{3,19},{4,20},{5,21},{6,22},{7,23},{8,9},{9,8... | collective-permute-start | bytes 417800 | tf_op jit(solution)/shard_map/ppermute | solution.py:417
  106.7 7.3 %collective-permute-start.15 = (f32[192,256]{1,0:T(8,128)S(1)}, f32[192,256]{1,0:T(8,128)S(1)}, u32[]{:S(2)}, u32[]{:S(2)}) collective-permute-start(f32[192,256]{1,0:T(8,128)S(1)} %add.95), channel_id=1, source_target_pairs={{0,1},{1,0},{2,3},{3,2},{4,5},{5,4},{6,7},{7,6},{8,24},{9,25},{10,... | collective-permute-start | bytes 589832 | tf_op jit(solution)/shard_map/ppermute | solution.py:417
  107.1 6.9 %collective-permute-start.14 = (f32[136,256]{1,0:T(8,128)S(1)}, f32[136,256]{1,0:T(8,128)S(1)}, u32[]{:S(2)}, u32[]{:S(2)}) collective-permute-start(f32[136,256]{1,0:T(8,128)S(1)} %add.94), channel_id=1, source_target_pairs={{0,2},{1,3},{2,0},{3,1},{4,6},{5,7},{6,4},{7,5},{8,12},{9,13},{10,... | collective-permute-start | bytes 417800 | tf_op jit(solution)/shard_map/ppermute | solution.py:417
  114.1 6.2 %collective-permute-start.17 = (f32[384,256]{1,0:T(8,128)S(1)}, f32[384,256]{1,0:T(8,128)S(1)}, u32[]{:S(2)}, u32[]{:S(2)}) collective-permute-start(f32[384,256]{1,0:T(8,128)S(1)} %pad_maximum_fusion.2), channel_id=1, source_target_pairs={{0,8},{1,9},{2,10},{3,11},{4,12},{5,13},{6,14},{7,15},{8,0},{9,1},... | collective-permute-start | bytes 1179656 | tf_op jit(solution)/shard_map/ppermute | solution.py:417
  114.1 6.1 %collective-permute-start.16 = (f32[136,256]{1,0:T(8,128)S(1)}, f32[136,256]{1,0:T(8,128)S(1)}, u32[]{:S(2)}, u32[]{:S(2)}) collective-permute-start(f32[136,256]{1,0:T(8,128)S(1)} %add.96), channel_id=1, source_target_pairs={{0,4},{1,5},{2,6},{3,7},{4,0},{5,1},{6,2},{7,3},{8,10},{9,11},{10,... | collective-permute-start | bytes 417800 | tf_op jit(solution)/shard_map/ppermute | solution.py:417
  120.4 5.1 %collective-permute-start.18 = (f32[136,256]{1,0:T(8,128)S(1)}, f32[136,256]{1,0:T(8,128)S(1)}, u32[]{:S(2)}, u32[]{:S(2)}) collective-permute-start(f32[136,256]{1,0:T(8,128)S(1)} %add.97), channel_id=1, source_target_pairs={{0,1},{1,0},{2,3},{3,2},{4,5},{5,4},{6,7},{7,6},{8,24},{9,25},{10,... | collective-permute-start | bytes 417800 | tf_op jit(solution)/shard_map/ppermute | solution.py:417
  125.6 1.7 %collective-permute-start.19 = (f32[272,256]{1,0:T(8,128)S(1)}, f32[272,256]{1,0:T(8,128)S(1)}, u32[]{:S(2)}, u32[]{:S(2)}) collective-permute-start(f32[272,256]{1,0:T(8,128)S(1)} %pad_maximum_fusion.3), channel_id=1, source_target_pairs={{0,8},{1,9},{2,10},{3,11},{4,12},{5,13},{6,14},{7,15},{8,0},{9,1},... | collective-permute-start | bytes 835592 | tf_op jit(solution)/shard_map/ppermute | solution.py:417
  (61 other events, 255.7 us)

commit v3 on v2

--- a/solution.py
+++ b/solution.py
@@ -12,9 +12,12 @@
 BF16 = jnp.bfloat16
 GROUP = 4
 EPS = 1e-05
+EARLY = 2
+LATE = 1
 GELU_A = math.sqrt(2.0 / math.pi)
 GELU_B = 0.044715
-VMEM_LIMIT = 16 * 1024 * 1024
+SMALL = 16 * 1024 * 1024
+FRONT_LIMIT = 16 * 1024 * 1024
 
 
 def split(value):
@@ -94,13 +97,26 @@
     return copies
 
 
+def views(ref, *sizes):
+    result, start = [], 0
+    for size in sizes:
+        result.append(ref.at[start : start + size])
+        start += size
+    return result
+
+
 def front_kernel(
     x_hbm, gain_hbm, fx_hbm, xw_hbm, logit_hbm, temper_hbm,
-    weight_h, weight_l, fx_h, fx_l, assign_h, assign_l, hat_h, hat_l, x_t, both_h, both_l, sums,
+    packed, wide_packed, sums,
     x, gain, fx_weight, x_weight, logit_weight, temper, sems,
 ):
     sources = (x_hbm, gain_hbm, fx_hbm, xw_hbm, logit_hbm, temper_hbm)
     targets = (x, gain, fx_weight, x_weight, logit_weight, temper)
+    width, total = x.shape[2], packed.shape[1]
+    weight_h, weight_l, fx_h, fx_l, assign_h, assign_l, hat_h, hat_l, both_h, both_l = views(
+        packed, *[total] * 2, *[width] * 8
+    )
+    x_t, rstd_rows, temper_rows = views(wide_packed, width, 8, temper.shape[0])
     copies = fetch(sources, targets, sems)
     head_size, slices = logit_weight.shape
     heads = temper.shape[0]
@@ -109,7 +125,8 @@
     copies[0].wait()
     columns = x[0].T
     x_t[...] = columns
-    hat, _ = standardise(columns)
+    hat, rstd = standardise(columns)
+    rstd_rows[...] = jnp.broadcast_to(rstd, (8, points))
     hat = split(hat)
     hat_h[...], hat_l[...] = hat
     for copy in copies[1:]:
@@ -132,7 +149,9 @@
         logits = product(logit_blocks, rows_of(assign, g * rows, rows), 0, 0)
         parts = []
         for i in range(GROUP):
-            scale = jnp.full((1, points), temper[g * GROUP + i], F32)
+            head = g * GROUP + i
+            scale = jnp.full((1, points), temper[head], F32)
+            temper_rows[head : head + 1] = scale
             scaled = logits[i * slices : (i + 1) * slices] / scale
             scaled = scaled - jnp.max(scaled, axis=0, keepdims=True)
             grown = jnp.exp(scaled)
@@ -150,33 +169,69 @@
     sums[head_size : head_size + 8] = jnp.concatenate(dens, axis=1)
 
 
+def map_views(packed, width, head_size, slices):
+    views_of = views(
+        packed, *[width] * 8, *[GROUP * head_size] * 2, *[3 * head_size] * 2, *[head_size] * 2
+    )
+    maps_t = [ref.at[:, 0:head_size] for ref in views_of[10:12]]
+    maps = [ref.at[:, 0 : 3 * head_size] for ref in views_of[12:14]]
+    logits = [ref.at[:, 0 : GROUP * slices] for ref in views_of[8:10]]
+    return views_of[:8], logits, maps_t, maps
+
+
 def ready_kernel(
-    cotangent, out_weight, gain, expand_weight, down_weight, query, key, value,
-    cot_t, hidden_grad, out_t_h, out_t_l, expand_h, expand_l, expand_t_h, expand_t_l, maps_h,
-    maps_l,
+    cotangent, out_weight, gain, expand_weight, down_weight, query, key, value, logit_weight,
+    columns_packed, packed,
 ):
+    width = cotangent.shape[2]
+    head_size, slices = logit_weight.shape
+    cot_t, hidden_grad = views(columns_packed, width, width)
+    (out_h, out_l, out_t_h, out_t_l, expand_h, expand_l, expand_t_h, expand_t_l), logits, maps_t, maps = (
+        map_views(packed, width, head_size, slices)
+    )
     columns = cotangent[0].T
     cot_t[...] = columns
     hidden_grad[...] = product(split(down_weight[...]), split(columns), 1, 0)
+    out_h[...], out_l[...] = split(out_weight[...])
     out_t_h[...], out_t_l[...] = split(out_weight[...].T)
     expand = expand_weight[...] * column(gain[...])
     expand_h[...], expand_l[...] = split(expand)
     expand_t_h[...], expand_t_l[...] = split(expand.T)
-    maps = jnp.concatenate([query[...], key[...], value[...]], axis=1)
-    maps_h[...], maps_l[...] = split(maps.T)
+    both = jnp.concatenate([query[...], key[...], value[...]], axis=1)
+    maps_t[0][...], maps_t[1][...] = split(both.T)
+    maps[0][...], maps[1][...] = split(both)
+    wide = jnp.concatenate([logit_weight[...]] * GROUP, axis=1)
+    logits[0][...], logits[1][...] = split(spread_blocks(wide, head_mask(head_size, slices)))
+
+
+def back_views(packed, wide_packed, width, head_size, slices):
+    return views(packed, *[width] * 12) + views(
+        wide_packed, width, 5 * head_size, 2 * slices, 8
+    )
 
 
 def back_kernel(
-    sums, x_t, weight_h, weight_l, cot_t, hidden_grad, out_weight, out_t_h, out_t_l, expand_h,
-    expand_l, expand_t_h, expand_t_l, maps_h, maps_l,
-    out_sum, mixed_grad, spread_grad_h, spread_grad_l, middle, attn, spread_h, spread_l, hat_h,
-    hat_l, before_grad_h, before_grad_l, hidden_h, hidden_l,
+    head_size, slices,
+    sums, front, front_wide, columns_packed, map_packed,
+    out_sum, packed, wide_packed,
 ):
-    head_size = maps_h.shape[1]
-    slices = attn.shape[0] // 2
-    heads = weight_h.shape[0] // slices
+    total = front.shape[1]
+    heads = total // slices
+    width = (wide_packed.shape[0] - 8) - 5 * head_size - 2 * slices
+    weight_h, weight_l = views(front, total, total)
+    x_t = front_wide.at[0:width]
+    cot_t, hidden_grad = views(columns_packed, width, width)
+    (out_h, out_l, out_t_h, out_t_l, expand_h, expand_l, expand_t_h, expand_t_l), _, maps_t, _ = (
+        map_views(map_packed, width, head_size, slices)
+    )
+    maps_h, maps_l = maps_t
+    (spread_grad_h, spread_grad_l, spread_h, spread_l, hat_h, hat_l, before_grad_h, before_grad_l,
+     hidden_h, hidden_l, grad_h, grad_l, mixed_grad, middle, attn, denom_rows) = back_views(
+        packed, wide_packed, width, head_size, slices
+    )
     rows, lanes = GROUP * head_size, GROUP * slices
     denom = sums[head_size : head_size + 1] + EPS
+    denom_rows[...] = jnp.broadcast_to(denom, (8, total))
     tokens = sums[0:head_size] / denom
     qkv = product((maps_h[...], maps_l[...]), split(tokens), 1, 0)
     qkv_pair = split(qkv)
@@ -224,7 +279,9 @@
     hat_grad = product((expand_h[...], expand_l[...]), before_grad, 1, 0)
     grad = cot_t[...] + standardise_pull(hat_grad, hat, rstd)
     mixed_grad[...] = grad
-    spread_grad = split(product(split(out_weight[...]), split(grad), 1, 0))
+    grad_pair = split(grad)
+    grad_h[...], grad_l[...] = grad_pair
+    spread_grad = split(product((out_h[...], out_l[...]), grad_pair, 1, 0))
     spread_grad_h[...], spread_grad_l[...] = spread_grad
     sums_out = []
     for g in range(heads // GROUP):
@@ -236,32 +293,75 @@
     out_sum[...] = jnp.concatenate(sums_out, axis=1)
 
 
-def early_kernel(
-    factor,
-    spread_h, spread_l, mixed_grad, hat_h, hat_l, before_grad_h, before_grad_l, hidden_h,
-    hidden_l, cotangent,
-    early,
+def place(axes):
+    d, p = lax.axis_index("dp"), lax.axis_index("point")
+    halves = [lax.rem((p if axis else d) // bit, 2) for axis, bit in axes]
+    first = lax.rem(d, 2) == 0
+    return jnp.where(first, *halves), jnp.where(first, *halves[::-1])
+
+
+def block(ref, index, size):
+    return ref.at[pl.ds(pl.multiple_of(index * size, 8), size)]
+
+
+def store_halves(value, mine, other):
+    half = mine.shape[0]
+    core = lax.rem(lax.axis_index("dp"), 2)
+    mine[...] = block(value, core, half)[...]
+    other[...] = block(value, 1 - core, half)[...]
+
+
+def add_halve_kernel(axes, mine, received, kept, sent):
+    half = kept.shape[0]
+    upper, _ = place(axes)
+    kept[...] = block(mine, upper, half)[...] + block(received, upper, half)[...]
+    sent[...] = block(mine, 1 - upper, half)[...] + block(received, 1 - upper, half)[...]
+
+
+def arrange(levels, own, partner, result):
+    core = lax.rem(lax.axis_index("dp"), 2)
+    count = 1 << len(levels)
+    size = own.shape[0] // count
+    for side, ref in enumerate((own, partner)):
+        uppers = [place(axes)[side] for axes in levels]
+        for i in range(count):
+            index = core if side == 0 else 1 - core
+            for level, upper in enumerate(uppers):
+                same = (i >> (len(levels) - 1 - level)) & 1 == 0
+                index = 2 * index + (upper if same else 1 - upper)
+            block(result, index, size)[...] = ref[i * size : (i + 1) * size]
+
+
+def early_kernel(factor, columns_packed, packed, mine, other, early):
+    width = early.shape[1]
+    pieces = [ref[...] for ref in views(packed, *[width] * 12)[2:]]
+    spread, hat, before_grad, hidden, grad = (pieces[i : i + 2] for i in range(0, 10, 2))
+    early[0:width] = product(spread, grad, 1, 1) * factor
+    early[width : 2 * width] = product(hat, before_grad, 1, 1) * factor
+    early[2 * width :] = product(hidden, split(columns_packed[0:width]), 1, 1) * factor
+    store_halves(early, mine, other)
+
+
+def end_kernel(
+    factor, middle_factor, head_size, slices,
+    out_sum, front, front_wide, map_packed, back, back_wide,
+    late_mine, late_other, packed,
+    late,
 ):
-    width = mixed_grad.shape[0]
-    spread = (spread_h[...], spread_l[...])
-    early[0:width] = product(spread, split(mixed_grad[...]), 1, 1) * factor
-    hat = (hat_h[...], hat_l[...])
-    before_grad = (before_grad_h[...], before_grad_l[...])
-    early[width : 2 * width] = product(hat, before_grad, 1, 1) * factor
-    hidden = (hidden_h[...], hidden_l[...])
-    early[2 * width :] = product(hidden, split(cotangent[0]), 1, 0) * factor
-
-
-def end_kernel(
-    factor, middle_factor,
-    out_sum, sums, middle, attn, weight_h, weight_l, fx_h, fx_l, assign_h, assign_l, hat_h,
-    hat_l, spread_grad_h, spread_grad_l, query, key, value, logit_weight, temper,
-    late, both_grad_h, both_grad_l,
-):
-    head_size, slices = logit_weight.shape
-    heads = temper.shape[0]
+    width = late.shape[1]
+    points = front.shape[1]
+    total = out_sum.shape[1]
+    heads = total // slices
+    weight_h, weight_l, fx_h, fx_l, assign_h, assign_l, hat_h, hat_l = views(
+        front, *[total] * 2, *[width] * 6
+    )
+    temper_rows = front_wide.at[width + 8 : width + 8 + heads]
+    both_grad_h, both_grad_l = views(packed, 2 * width, 2 * width)
+    _, logit_maps, _, maps = map_views(map_packed, width, head_size, slices)
+    spread_grad_h, spread_grad_l, *_, middle, attn, denom_rows = back_views(
+        back, back_wide, width, head_size, slices
+    )
     rows, lanes = GROUP * head_size, GROUP * slices
-    width, points = hat_h.shape
     tokens = middle[0:head_size]
     qkv_pair = split(middle[head_size : 4 * head_size])
     result = middle[4 * head_size : 5 * head_size]
@@ -284,14 +384,13 @@
         key_grad = product(q, score_grad, 1, 1)
         parts.append(jnp.concatenate([query_grad, key_grad, value_grad], axis=0))
     qkv_grad = split(jnp.concatenate(parts, axis=1))
-    maps = split(jnp.concatenate([query[...], key[...], value[...]], axis=1))
+    maps = (maps[0][...], maps[1][...])
     map_grad = product(split(tokens), qkv_grad, 1, 1)
-    denom = sums[head_size : head_size + 1] + EPS
+    denom = denom_rows[0:1]
     num_grad = product(maps, qkv_grad, 1, 0) / denom
     den_grad = column(-jnp.sum(num_grad * tokens, axis=0, keepdims=True))
     mask = head_mask(head_size, slices)
-    logit_wide = jnp.concatenate([logit_weight[...]] * GROUP, axis=1)
-    logit_blocks = split(spread_blocks(logit_wide, mask))
+    logit_blocks = (logit_maps[0][...], logit_maps[1][...])
     fx_grads, assign_grads = [], []
     logit_grad = jnp.zeros((head_size, lanes), F32)
     for g in range(heads // GROUP):
@@ -313,7 +412,8 @@
         grads = []
         for i in range(GROUP):
             block = slice(i * slices, (i + 1) * slices)
-            scale = jnp.full((1, points), temper[g * GROUP + i], F32)
+            head = g * GROUP + i
+            scale = temper_rows[head : head + 1]
             w = weights[0][block].astype(F32) + weights[1][block].astype(F32)
             weighted = w * weight_grad[block]
             total = jnp.sum(weighted, axis=0, keepdims=True)
@@ -333,19 +433,27 @@
     late[base:] = jnp.zeros((late.shape[0] - base, width), F32)
     late[base : base + head_size, 0 : 3 * head_size] = map_grad * middle_factor
     late[base : base + head_size, 128 : 128 + slices] = logit_grad * factor
-
-
-def rows_kernel(both_h, both_l, both_grad_h, both_grad_l, x_t, mixed_grad, x_grad):
-    both = (both_h[...], both_l[...])
-    hat_grad = product(both, (both_grad_h[...], both_grad_l[...]), 1, 0)
-    hat, rstd = standardise(x_t[...])
-    x_grad[0] = (mixed_grad[...] + standardise_pull(hat_grad, hat, rstd)).T
+    store_halves(late, late_mine, late_other)
+
+
+def rows_kernel(front, front_wide, back_wide, end, x_grad):
+    width = x_grad.shape[2]
+    total = front.shape[1]
+    _, hat_h, hat_l, both_h, both_l = views(front, 2 * total + 4 * width, *[width] * 4)
+    rstd = front_wide[width : width + 1]
+    grads = [ref[...] for ref in views(end, 2 * width, 2 * width)]
+    hat_grad = product((both_h[...], both_l[...]), grads, 1, 0)
+    hat = hat_h[...].astype(F32) + hat_l[...].astype(F32)
+    x_grad[0] = (back_wide[0:width] + standardise_pull(hat_grad, hat, rstd)).T
 
 
 def early_out_kernel(
-    early, gain, expand_weight,
-    matrices, gain_row, scaled, sems,
+    levels,
+    own, partner, gain, expand_weight,
+    matrices, gain_row,
+    early, scaled, sems,
 ):
+    arrange(levels, own, partner, early)
     width = gain.shape[1]
     copies = [
         pltpu.make_async_copy(early.at[0:width], matrices.at[2], sems.at[0]),
@@ -363,9 +471,12 @@
 
 
 def late_out_kernel(
-    late, gain, fx_weight, x_weight, gain_row, given,
-    matrices, maps, logit, gains, scaled, sems,
+    levels,
+    own, partner, gain, fx_weight, x_weight, gain_row, given,
+    matrices, maps, logit, gains,
+    late, scaled, sems,
 ):
+    arrange(levels, own, partner, late)
     width = gain.shape[1]
     head_size, slices = logit.shape
     gain_column = column(gain[...])
@@ -393,7 +504,8 @@
 HBM = pl.BlockSpec(memory_space=pltpu.HBM)
 
 
-def call(body, name, in_specs, out_specs, out_shape, args, flops, scratch=(), aliases=None):
+def call(body, name, in_specs, out_specs, out_shape, args, flops, limit=SMALL, scratch=(),
+         aliases=None):
     return pl.pallas_call(
         body,
         name=name,
@@ -402,7 +514,7 @@
         out_shape=out_shape,
         scratch_shapes=scratch,
         input_output_aliases=aliases or {},
-        compiler_params=pltpu.CompilerParams(vmem_limit_bytes=VMEM_LIMIT),
+        compiler_params=pltpu.CompilerParams(vmem_limit_bytes=limit),
         cost_estimate=pl.CostEstimate(flops=flops, bytes_accessed=1 << 20, transcendentals=0),
     )(*args)
 
@@ -417,82 +529,91 @@
     return lax.ppermute(value, ("dp", "point"), pairs)
 
 
-def flip(axis, bit):
-    if axis == 0:
-        return lambda d, p: (d ^ bit, p)
-    return lambda d, p: (d, p ^ bit)
-
-
 def bits(count):
     return [1 << i for i in range(count.bit_length() - 1)]
 
 
-def power(count):
-    return count & (count - 1) == 0
-
-
 def tie(*values):
     return lax.optimization_barrier(values)
 
 
-def halve(value, upper):
-    half = value.shape[0] // 2
-    mine = lax.dynamic_slice_in_dim(value, upper * half, half, 0)
-    other = lax.dynamic_slice_in_dim(value, (1 - upper) * half, half, 0)
-    return mine, other
-
-
-def join(mine, other, upper):
-    low = jnp.where(upper == 0, mine, other)
-    high = jnp.where(upper == 0, other, mine)
-    return jnp.concatenate([low, high], axis=0)
-
-
-def point_steps(sizes):
-    if not power(sizes[1]):
-        return [lambda value: lax.psum(value, "point")]
-
-    def step(bit):
-        return lambda value: value + swap(value, flip(1, bit), sizes)
-
-    return [step(bit) for bit in bits(sizes[1])]
-
-
-def all_steps(sizes):
-    dp, point = sizes
-    if not (power(dp) and power(point)) or dp < 2 or point < 2:
-        return [lambda value: lax.psum(value, ("dp", "point"))]
-    d, p = lax.axis_index("dp"), lax.axis_index("point")
-    axes = [(1, 1)] + [(0, b) for b in bits(dp)[1:]] + [(1, b) for b in bits(point)[1:]]
+def flips(axes):
+    def moves(d, p):
+        axis, bit = axes[d & 1]
+        return (d, p ^ bit) if axis else (d ^ bit, p)
+
+    return moves
+
+
+CORES = ((0, 1), (0, 1))
+
+
+def paired(axes):
     turned = list(axes)
     for i in range(0, len(axes) - 1, 2):
         turned[i], turned[i + 1] = axes[i + 1], axes[i]
-
-    def move(i):
-        choices = [flip(*order[i]) for order in (axes, turned)]
-        return lambda d, p: choices[d & 1](d, p)
-
-    core = d & 1
-    places = [((d if order[0][0] == 0 else p) & order[0][1]) // order[0][1]
-              for order in (axes, turned)]
-    upper = jnp.where(core == 0, places[0], places[1])
-
-    def scatter(upper, moves):
+    return list(zip(axes, turned))
+
+
+def point_steps(sizes):
+    masks = bits(sizes[1])
+    groups = [[bit] for bit in masks[:-2]]
+    groups.append([masks[-2], masks[-1], masks[-2] | masks[-1]] if len(masks) > 1 else masks)
+
+    def step(group):
+        def run(value):
+            parts = [swap(value, flips(((1, mask),) * 2), sizes) for mask in group]
+            if len(parts) == 1:
+                return value + parts[0]
+            return (value + parts[0]) + (parts[1] + parts[2])
+        return run
+
+    return [step(group) for group in groups]
+
+
+def all_axes(sizes):
+    return paired(
+        [(1, 1)] + [(0, b) for b in bits(sizes[0])[1:]] + [(1, b) for b in bits(sizes[1])[1:]]
+    )
+
+
+def all_steps(sizes, scatters):
+    steps_axes = all_axes(sizes)
+
+    def add_halve(i, mine, received):
+        half = (mine.shape[0] // 2, mine.shape[1])
+        return call(
+            functools.partial(add_halve_kernel, steps_axes[i]), "add_halve", [VMEM] * 2,
+            [VMEM] * 2, [jax.ShapeDtypeStruct(half, F32)] * 2, (mine, received), mine.size,
+        )
+
+    def cores(value):
+        return add_halve(0, value[0], swap(value[1], flips(CORES), sizes))
+
+    def scatter(i):
         def step(value):
-            mine, other = halve(value, upper)
-            return mine + swap(other, moves, sizes)
+            received = swap(value[1], flips(steps_axes[i]), sizes)
+            if i + 1 < scatters:
+                return add_halve(i + 1, value[0], received)
+            return value[0] + received
         return step
 
-    def add(moves):
-        return lambda value: value + swap(value, moves, sizes)
-
-    def gather(upper, moves):
-        return lambda value: join(value, swap(value, moves, sizes), upper)
-
-    cores = flip(0, 1)
-    steps = [scatter(core, cores), scatter(upper, move(0))]
-    steps += [add(move(i)) for i in range(1, len(axes))]
-    return steps + [gather(upper, move(0)), gather(core, cores)]
+    def add(i):
+        return lambda value: value + swap(value, flips(steps_axes[i]), sizes)
+
+    def gather(i):
+        return lambda value: jnp.concatenate(
+            [value, swap(value, flips(steps_axes[i]), sizes)], axis=0
+        )
+
+    def last(value):
+        return value, swap(value, flips(CORES), sizes)
+
+    return (
+        [cores] + [scatter(i) for i in range(scatters)]
+        + [add(i) for i in range(scatters, len(steps_axes))]
+        + [gather(i) for i in reversed(range(scatters))] + [last]
+    )
 
 
 def shards(
@@ -507,6 +628,7 @@
     total = heads * slices
     gain_one, gain_two = gain_one[None], gain_two[None]
     factor = 1.0 / math.sqrt(points * sizes[0] * sizes[1])
+    axes = all_axes(sizes)
 
     def shape(*dims, dtype=F32):
         return jax.ShapeDtypeStruct(dims, dtype)
@@ -514,14 +636,18 @@
     def pair(*dims):
         return [shape(*dims, dtype=BF16)] * 2
 
-    tall = pair(width, points)
     dense = 6 * points * width * width
-    (w_h, w_l, fx_h, fx_l, as_h, as_l, h1_h, h1_l, x_t, both_h, both_l, sums) = call(
-        front_kernel, "front", [HBM] * 6, [VMEM] * 12,
-        pair(total, points) + tall * 3
-        + [shape(width, points)] + pair(width, 2 * width) + [shape(head_size + 8, total)],
-        (inputs, gain_one, fx_weight, x_weight, slice_logit_weight, temper),
+    pinned = [
+        pltpu.with_memory_space_constraint(array, pltpu.HBM)
+        for array in (inputs, gain_one, fx_weight, x_weight, slice_logit_weight, temper)
+    ]
+    front, front_wide, sums = call(
+        front_kernel, "front", [HBM] * 6, [VMEM] * 3,
+        [shape(2 * total + 8 * width, points, dtype=BF16), shape(width + 8 + heads, points),
+         shape(head_size + 8, total)],
+        pinned,
         4 * dense,
+        FRONT_LIMIT,
         [
             pltpu.VMEM(inputs.shape, F32), pltpu.VMEM((1, width), F32),
             pltpu.VMEM((width, width), F32), pltpu.VMEM((width, width), F32),
@@ -529,85 +655,85 @@
             pltpu.SemaphoreType.DMA((6,)),
         ],
     )
-    ready = call(
-        ready_kernel, "ready", [VMEM] * 8, [VMEM] * 10,
-        [shape(width, points)] * 2 + pair(width, width) * 3 + pair(3 * head_size, head_size),
+    sums, cotangent, out_weight, gain_two, expand_weight, down_weight = tie(
+        sums, cotangent, out_weight, gain_two, expand_weight, down_weight
+    )
+    columns, maps = call(
+        ready_kernel, "ready", [VMEM] * 9, [VMEM] * 2,
+        [shape(2 * width, points),
+         shape(8 * width + (2 * GROUP + 8) * head_size, width, dtype=BF16)],
         (cotangent, out_weight, gain_two, expand_weight, down_weight, slice_query_matrix,
-         slice_key_matrix, slice_value_matrix),
+         slice_key_matrix, slice_value_matrix, slice_logit_weight),
         2 * dense,
     )
     for step in point_steps(sizes):
         sums = step(sums)
-    cot_t, hidden_grad, out_t_h, out_t_l, ex_h, ex_l, ext_h, ext_l, maps_h, maps_l = ready
-    (out_sum, mixed_grad, sg_h, sg_l, middle, attn, sp_h, sp_l, h2_h, h2_l, bg_h, bg_l, hd_h,
-     hd_l) = call(
-        back_kernel, "back", [VMEM] * 15, [VMEM] * 14,
-        [shape(head_size, total), shape(width, points)] + tall
-        + [shape(5 * head_size, total), shape(2 * slices, total)] + tall * 4,
-        (sums, x_t, w_h, w_l, cot_t, hidden_grad, out_weight, out_t_h, out_t_l, ex_h, ex_l,
-         ext_h, ext_l, maps_h, maps_l),
+    out_sum, back, back_wide = call(
+        functools.partial(back_kernel, head_size, slices), "back", [VMEM] * 5, [VMEM] * 3,
+        [shape(head_size, total), shape(12 * width, points, dtype=BF16),
+         shape(width + 5 * head_size + 2 * slices + 8, points)],
+        (sums, front, front_wide, columns, maps),
         6 * dense,
     )
     early_value = call(
-        functools.partial(early_kernel, factor), "early", [VMEM] * 10, VMEM,
-        shape(3 * width, width),
-        (sp_h, sp_l, mixed_grad, h2_h, h2_l, bg_h, bg_l, hd_h, hd_l, cotangent),
-        3 * dense,
-    )
-    early_steps = all_steps(sizes)
-    early_at = 0
+        functools.partial(early_kernel, factor), "early", [VMEM] * 2, [VMEM] * 2,
+        [shape(3 * width // 2, width)] * 2, (columns, back), 3 * dense,
+        scratch=[pltpu.VMEM((3 * width, width), F32)],
+    )
+    early_steps = all_steps(sizes, EARLY)
+    taken = 0
     for i, step in enumerate(point_steps(sizes)):
-        before = out_sum
-        if early_at < len(early_steps) and i > 0:
-            early_new = early_steps[early_at](early_value)
-            early_at += 1
+        if taken < len(early_steps):
+            early_new = early_steps[taken](early_value)
+            taken += 1
         else:
             early_new = early_value
-        out_sum = step(before)
-        out_sum, early_value = tie(out_sum, early_new)
-    if early_at < len(early_steps):
-        early_value = early_steps[early_at](early_value)
-        early_at += 1
-    late, bgr_h, bgr_l = call(
-        functools.partial(end_kernel, factor, factor / sizes[1]), "end",
-        [VMEM] * 18 + [SMEM], [VMEM] * 3,
-        [shape(2 * width + head_size, width)] + pair(2 * width, points),
-        (out_sum, sums, middle, attn, w_h, w_l, fx_h, fx_l, as_h, as_l, h1_h, h1_l, sg_h, sg_l,
-         slice_query_matrix, slice_key_matrix, slice_value_matrix, slice_logit_weight, temper),
+        out_sum, early_value = tie(step(out_sum), early_new)
+    if taken < len(early_steps):
+        early_value = early_steps[taken](early_value)
+        taken += 1
+    rows = 2 * width + head_size
+    mine, other, end = call(
+        functools.partial(end_kernel, factor, factor / sizes[1], head_size, slices), "end",
+        [VMEM] * 6, [VMEM] * 3,
+        [shape(rows // 2, width)] * 2 + [shape(4 * width, points, dtype=BF16)],
+        (out_sum, front, front_wide, maps, back, back_wide),
         8 * dense,
-    )
+        scratch=[pltpu.VMEM((rows, width), F32)],
+    )
+    late, early_value = tie((mine, other), early_value)
     input_grad = call(
-        rows_kernel, "rows", [VMEM] * 6, VMEM, shape(1, points, width),
-        (both_h, both_l, bgr_h, bgr_l, x_t, mixed_grad),
-        2 * dense,
-    )
-    for i, step in enumerate(all_steps(sizes)):
-        if i > 0 and early_at < len(early_steps):
-            early_new = early_steps[early_at](early_value)
-            early_at += 1
-            late = step(late)
-            late, early_value = tie(late, early_new)
-        else:
-            late = step(late)
-            late, early_value = tie(late, early_value)
-    any_space = pl.BlockSpec(memory_space=pltpu.HBM)
+        rows_kernel, "rows", [VMEM] * 4, VMEM, shape(1, points, width),
+        (front, front_wide, back_wide, end), 2 * dense,
+    )
+    steps = all_steps(sizes, LATE)
+    for i, step in enumerate(steps):
+        late = step(late)
+        if i > 0 and taken < len(early_steps):
+            late, early_value = tie(late, early_steps[taken](early_value))
+            taken += 1
+        if i == 0:
+            late, input_grad = tie(late, input_grad)
     matrices, gain_row = call(
-        early_out_kernel, "early_out", [VMEM] * 3, [any_space, VMEM],
+        functools.partial(early_out_kernel, tuple(axes[:EARLY])), "early_out", [VMEM] * 4, [HBM, VMEM],
         [shape(5, width, width), shape(1, width)],
-        (early_value, gain_two, expand_weight),
+        (*early_value, gain_two, expand_weight),
         dense // 8,
-        [pltpu.VMEM((width, width), F32), pltpu.SemaphoreType.DMA((3,))],
-    )
-    matrices, maps, logit, gains = call(
-        late_out_kernel, "late_out", [VMEM] * 5 + [any_space], [any_space] + [VMEM] * 3,
+        scratch=[pltpu.VMEM((3 * width, width), F32), pltpu.VMEM((width, width), F32),
+                 pltpu.SemaphoreType.DMA((3,))],
+    )
+    matrices, map_grads, logit_grad, gains = call(
+        functools.partial(late_out_kernel, tuple(axes[:LATE])), "late_out", [VMEM] * 6 + [HBM],
+        [HBM] + [VMEM] * 3,
         [shape(5, width, width), shape(3, head_size, head_size), shape(head_size, slices),
          shape(2, width)],
-        (late, gain_one, fx_weight, x_weight, gain_row, matrices),
+        (*late, gain_one, fx_weight, x_weight, gain_row, matrices),
         dense // 8,
-        [pltpu.VMEM((2, width, width), F32), pltpu.SemaphoreType.DMA((2,))],
-        {5: 0},
-    )
-    return input_grad, matrices, maps, logit, gains
+        scratch=[pltpu.VMEM((rows, width), F32), pltpu.VMEM((2, width, width), F32),
+                 pltpu.SemaphoreType.DMA((2,))],
+        aliases={6: 0},
+    )
+    return input_grad, matrices, map_grads, logit_grad, gains
 
 
 def solution(mesh):

time: 132 us -> 85.4 us (0.65)
  local copies, waits for them, and re-layouts: 37.4 us -> 0.05 us
  other arithmetic: 4.99 us -> 0.25 us
  starting transfers between devices: 26.9 us -> 23.5 us
    unnamed x130 -> x24, local copies, waits for them, and re-layouts: 36.6 us -> 0.05 us
    add x16 -> x11, other arithmetic: 4.69 us -> 0.19 us  [the longest x5 0.09 us: add(): return lambda value: value + swap(value, flips(steps_axes[i]), sizes)]
    ppermute x20 -> x23, starting transfers between devices: 26.9 us -> 23.5 us  [swap(): return lax.ppermute(value, ('dp', 'point'), pairs)]
    pallas_call x8 -> x11, Pallas kernels: 18.1 us -> 18.9 us  [call(): pl.pallas_call(body, name=name, in_specs=in_specs, out_specs=out_specs, o...]
    ppermute x20 -> x23, waiting for transfers between devices: 42.2 us -> 41.6 us  [swap(): return lax.ppermute(value, ('dp', 'point'), pairs)]
  transfers between devices with their start and end apart: 20 -> 23, of which waited for: 13 -> 14; matrix products, arithmetic and copies ran while one was open for 2% -> 0% of each run, Pallas kernels for 2% -> 9%
where the time goes in v3:
time: 85.4 us; the launch traced here: 85.3 us
  waiting for transfers between devices  41.6 us (49%)
  starting transfers between devices  23.5 us (28%)
  Pallas kernels  18.9 us (22%)
  between operations  0.99 us (1%)
    ppermute x23, waiting for transfers between devices, swap(): return lax.ppermute(value, ('dp', 'point'), pairs)  41.6 us
    ppermute x23, starting transfers between devices, swap(): return lax.ppermute(value, ('dp', 'point'), pairs)  23.5 us
    pallas_call x11, Pallas kernels, call(): pl.pallas_call(body, name=name, in_specs=in_specs, out_specs=out_specs, o...  18.9 us
  transfers between devices with their start and end apart: 23, of which 14 were waited for; matrix products, arithmetic and copies ran while one was open for 0% of the time, Pallas kernels for 9%

profile of v3, /device:TPU:0, one launch (start us, length us, event | category | flops | bytes accessed | tf_op | source)
XLA Modules:
  0.0 85.3 jit_solution(2544661556083122028)
XLA Ops:
  0.7 4.2 %front.1 = (bf16[3072,512]{1,0:T(8,128)(2,1)S(1)}, f32[272,512]{1,0:T(8,128)S(1)}, f32[40,512]{1,0:T(8,128)S(1)}) custom-call(f32[1,512,256]{2,1,0:T(8,128)} %x_hbm.1, f32[1,256]{1,0:T(1,128)} %bitcast.4, f32[256,256]{1,0:T(8,128)} %fx_weight.1, f32[256,256]{1,0:T(8,128)} %x_weight.1, f32[32,64]{1,0:T(8,128)} %logit_weight.1, f32[8]{0:T(128)} %temper_hbm.1), custom_call_target="tpu_custom_call" | custom-call | flops 805306368 | bytes 1048576 | tf_op jit(solution)/shard_map/front/pallas_call | solution.py:509
  5.0 3.0 %collective-permute-start = (f32[40,512]{1,0:T(8,128)S(1)}, f32[40,512]{1,0:T(8,128)S(1)}, u32[]{:S(2)}, u32[]{:S(2)}) collective-permute-start(f32[40,512]{1,0:T(8,128)S(1)} %get-tuple-element.60), channel_id=1, source_target_pairs={{0,1},{1,0},{2,3},{3,2},{4,5},{5,4},{6,7},{7,6},{8,9},{9,8},{10,11... | collective-permute-start | bytes 245768 | tf_op jit(solution)/shard_map/ppermute | solution.py:529
  8.0 2.4 %collective-permute-done = f32[40,512]{1,0:T(8,128)S(1)} collective-permute-done((f32[40,512]{1,0:T(8,128)S(1)}, f32[40,512]{1,0:T(8,128)S(1)}, u32[]{:S(2)}, u32[]{:S(2)}) %collective-permute-start) | collective-permute-done | bytes 81952 | tf_op jit(solution)/shard_map/ppermute | solution.py:529
  10.4 4.2 %collective-permute-start.3 = (f32[40,512]{1,0:T(8,128)S(1)}, f32[40,512]{1,0:T(8,128)S(1)}, u32[]{:S(2)}, u32[]{:S(2)}) collective-permute-start(f32[40,512]{1,0:T(8,128)S(1)} %add.45), channel_id=1, source_target_pairs={{0,6},{1,7},{2,4},{3,5},{4,2},{5,3},{6,0},{7,1},{8,14},{9,15},{10,... | collective-permute-start | bytes 245768 | tf_op jit(solution)/shard_map/ppermute | solution.py:529
  17.4 3.4 %collective-permute-done.2 = f32[40,512]{1,0:T(8,128)S(1)} collective-permute-done((f32[40,512]{1,0:T(8,128)S(1)}, f32[40,512]{1,0:T(8,128)S(1)}, u32[]{:S(2)}, u32[]{:S(2)}) %collective-permute-start.2) | collective-permute-done | bytes 81952 | tf_op jit(solution)/shard_map/ppermute | solution.py:529
  20.8 4.1 %back.1 = (f32[32,512]{1,0:T(8,128)S(1)}, bf16[3072,512]{1,0:T(8,128)(2,1)S(1)}, f32[552,512]{1,0:T(8,128)S(1)}) custom-call(f32[40,512]{1,0:T(8,128)S(1)} %add_add_fusion.sums, bf16[3072,512]{1,0:T(8,128)(2,1)S(1)} %get-tuple-element.61.front, f32[272,512]{1,0:T(8,128)S(1)} %get-tuple-element.62.front_wide, ...), custom_call_target="tpu_custom_call" | custom-call | flops 1207959552 | bytes 1048576 | tf_op jit(solution)/shard_map/back/pallas_call | solution.py:509
  25.9 1.6 %collective-permute-start.4 = (f32[32,512]{1,0:T(8,128)S(1)}, f32[32,512]{1,0:T(8,128)S(1)}, u32[]{:S(2)}, u32[]{:S(2)}) collective-permute-start(f32[32,512]{1,0:T(8,128)S(1)} %get-tuple-element.70), channel_id=1, source_target_pairs={{0,1},{1,0},{2,3},{3,2},{4,5},{5,4},{6,7},{7,6},{8,9},{9,8},{10,11... | collective-permute-start | bytes 196616 | tf_op jit(solution)/shard_map/ppermute | solution.py:529
  27.5 2.9 %collective-permute-done.4 = f32[32,512]{1,0:T(8,128)S(1)} collective-permute-done((f32[32,512]{1,0:T(8,128)S(1)}, f32[32,512]{1,0:T(8,128)S(1)}, u32[]{:S(2)}, u32[]{:S(2)}) %collective-permute-start.4) | collective-permute-done | bytes 65568 | tf_op jit(solution)/shard_map/ppermute | solution.py:529
  30.5 2.3 %collective-permute-start.8 = (f32[32,512]{1,0:T(8,128)S(1)}, f32[32,512]{1,0:T(8,128)S(1)}, u32[]{:S(2)}, u32[]{:S(2)}) collective-permute-start(f32[32,512]{1,0:T(8,128)S(1)} %add.49), channel_id=1, source_target_pairs={{0,6},{1,7},{2,4},{3,5},{4,2},{5,3},{6,0},{7,1},{8,14},{9,15},{10,... | collective-permute-start | bytes 196616 | tf_op jit(solution)/shard_map/ppermute | solution.py:529
  32.8 2.1 %collective-permute-start.6 = (f32[32,512]{1,0:T(8,128)S(1)}, f32[32,512]{1,0:T(8,128)S(1)}, u32[]{:S(2)}, u32[]{:S(2)}) collective-permute-start(f32[32,512]{1,0:T(8,128)S(1)} %add.49), channel_id=1, source_target_pairs={{0,2},{1,3},{2,0},{3,1},{4,6},{5,7},{6,4},{7,5},{8,10},{9,11},{10,... | collective-permute-start | bytes 196616 | tf_op jit(solution)/shard_map/ppermute | solution.py:529
  35.0 1.5 %collective-permute-start.9 = (f32[192,256]{1,0:T(8,128)S(1)}, f32[192,256]{1,0:T(8,128)S(1)}, u32[]{:S(2)}, u32[]{:S(2)}) collective-permute-start(f32[192,256]{1,0:T(8,128)S(1)} %get-tuple-element.78), channel_id=1, source_target_pairs={{0,1},{1,0},{2,3},{3,2},{4,5},{5,4},{6,7},{7,6},{8,24},{9,25},{10,... | collective-permute-start | bytes 589832 | tf_op jit(solution)/shard_map/ppermute | solution.py:529
  36.9 2.1 %collective-permute-done.7 = f32[32,512]{1,0:T(8,128)S(1)} collective-permute-done((f32[32,512]{1,0:T(8,128)S(1)}, f32[32,512]{1,0:T(8,128)S(1)}, u32[]{:S(2)}, u32[]{:S(2)}) %collective-permute-start.7) | collective-permute-done | bytes 65568 | tf_op jit(solution)/shard_map/ppermute | solution.py:529
  39.0 1.6 %collective-permute-done.9.received = f32[192,256]{1,0:T(8,128)S(1)} collective-permute-done((f32[192,256]{1,0:T(8,128)S(1)}, f32[192,256]{1,0:T(8,128)S(1)}, u32[]{:S(2)}, u32[]{:S(2)}) %collective-permute-start.9) | collective-permute-done | bytes 196640 | tf_op jit(solution)/shard_map/ppermute | solution.py:529
  40.7 1.6 %collective-permute-start.10 = (f32[96,256]{1,0:T(8,128)S(1)}, f32[96,256]{1,0:T(8,128)S(1)}, u32[]{:S(2)}, u32[]{:S(2)}) collective-permute-start(f32[96,256]{1,0:T(8,128)S(1)} %get-tuple-element.86), channel_id=1, source_target_pairs={{0,16},{1,17},{2,18},{3,19},{4,20},{5,21},{6,22},{7,23},{8,9},{9,8... | collective-permute-start | bytes 294920 | tf_op jit(solution)/shard_map/ppermute | solution.py:529
  42.3 4.5 %end.1 = (f32[272,256]{1,0:T(8,128)S(1)}, f32[272,256]{1,0:T(8,128)S(1)}, bf16[1024,512]{1,0:T(8,128)(2,1)S(1)}) custom-call(f32[32,512]{1,0:T(8,128)S(1)} %add_add_fusion.1.out_sum, bf16[3072,512]{1,0:T(8,128)(2,1)S(1)} %get-tuple-element.61.front, f32[272,512]{1,0:T(8,128)S(1)} %get-tuple-element.62.front_wide, ...), custom_call_target="tpu_custom_call" | custom-call | flops 1610612736 | bytes 1048576 | tf_op jit(solution)/shard_map/end/pallas_call | solution.py:509
  46.9 1.6 %rows.1 = f32[1,512,256]{2,1,0:T(8,128)} custom-call(bf16[3072,512]{1,0:T(8,128)(2,1)S(1)} %get-tuple-element.61.front, f32[272,512]{1,0:T(8,128)S(1)} %get-tuple-element.62.front_wide, f32[552,512]{1,0:T(8,128)S(1)} %get-tuple-element.82.back_wide, bf16[1024,512]{1,0:T(8,128)(2,1)S(1)} %get-tuple-element.91.end), custom_call_target="tpu_custom_call" | custom-call | flops 402653184 | bytes 1048576 | tf_op jit(solution)/shard_map/rows/pallas_call | solution.py:509
  48.5 1.6 %collective-permute-start.12 = (f32[136,256]{1,0:T(8,128)S(1)}, f32[136,256]{1,0:T(8,128)S(1)}, u32[]{:S(2)}, u32[]{:S(2)}) collective-permute-start(f32[136,256]{1,0:T(8,128)S(1)} %get-tuple-element.94), channel_id=1, source_target_pairs={{0,1},{1,0},{2,3},{3,2},{4,5},{5,4},{6,7},{7,6},{8,24},{9,25},{10,... | collective-permute-start | bytes 417800 | tf_op jit(solution)/shard_map/ppermute | solution.py:529
  50.1 5.5 %collective-permute-done.13 = f32[96,256]{1,0:T(8,128)S(1)} collective-permute-done((f32[96,256]{1,0:T(8,128)S(1)}, f32[96,256]{1,0:T(8,128)S(1)}, u32[]{:S(2)}, u32[]{:S(2)}) %collective-permute-start.13) | collective-permute-done | bytes 98336 | tf_op jit(solution)/shard_map/ppermute | solution.py:529
  56.7 5.6 %collective-permute-done.15 = f32[96,256]{1,0:T(8,128)S(1)} collective-permute-done((f32[96,256]{1,0:T(8,128)S(1)}, f32[96,256]{1,0:T(8,128)S(1)}, u32[]{:S(2)}, u32[]{:S(2)}) %collective-permute-start.15) | collective-permute-done | bytes 98336 | tf_op jit(solution)/shard_map/ppermute | solution.py:529
  63.6 3.5 %collective-permute-done.17 = f32[96,256]{1,0:T(8,128)S(1)} collective-permute-done((f32[96,256]{1,0:T(8,128)S(1)}, f32[96,256]{1,0:T(8,128)S(1)}, u32[]{:S(2)}, u32[]{:S(2)}) %collective-permute-start.17) | collective-permute-done | bytes 98336 | tf_op jit(solution)/shard_map/ppermute | solution.py:529
  67.1 1.5 %collective-permute-done.16 = f32[136,256]{1,0:T(8,128)S(1)} collective-permute-done((f32[136,256]{1,0:T(8,128)S(1)}, f32[136,256]{1,0:T(8,128)S(1)}, u32[]{:S(2)}, u32[]{:S(2)}) %collective-permute-start.16) | collective-permute-done | bytes 139296 | tf_op jit(solution)/shard_map/ppermute | solution.py:529
  70.0 6.6 %collective-permute-done.18 = f32[136,256]{1,0:T(8,128)S(1)} collective-permute-done((f32[136,256]{1,0:T(8,128)S(1)}, f32[136,256]{1,0:T(8,128)S(1)}, u32[]{:S(2)}, u32[]{:S(2)}) %collective-permute-start.18) | collective-permute-done | bytes 139296 | tf_op jit(solution)/shard_map/ppermute | solution.py:529
  77.9 4.0 %collective-permute-done.20 = f32[136,256]{1,0:T(8,128)S(1)} collective-permute-done((f32[136,256]{1,0:T(8,128)S(1)}, f32[136,256]{1,0:T(8,128)S(1)}, u32[]{:S(2)}, u32[]{:S(2)}) %collective-permute-start.20) | collective-permute-done | bytes 139296 | tf_op jit(solution)/shard_map/ppermute | solution.py:529
  83.6 1.7 %late_out.1 = (f32[5,256,256]{2,1,0:T(8,128)}, f32[3,32,32]{2,1,0:T(8,128)}, f32[32,64]{1,0:T(8,128)}, f32[2,256]{1,0:T(2,128)}) custom-call(f32[272,256]{1,0:T(8,128)S(1)} %pad_maximum_fusion.1.own, f32[272,256]{1,0:T(8,128)S(1)} %collective-permute-done.22.partner, f32[1,256]{1,0:T(1,128)S(1)} %bitcast.5, ...), custom_call_target="tpu_custom_call", output_to_operand_aliasing={{0}: (6, {})} | custom-call | flops 25165824 | bytes 1048576 | tf_op jit(solution)/shard_map/late_out/pallas_call | solution.py:509
  (71 shorter events, 11.0 us)
Async XLA Ops:
  5.0 5.4 %collective-permute-start = (f32[40,512]{1,0:T(8,128)S(1)}, f32[40,512]{1,0:T(8,128)S(1)}, u32[]{:S(2)}, u32[]{:S(2)}) collective-permute-start(f32[40,512]{1,0:T(8,128)S(1)} %get-tuple-element.60), channel_id=1, source_target_pairs={{0,1},{1,0},{2,3},{3,2},{4,5},{5,4},{6,7},{7,6},{8,9},{9,8},{10,11... | collective-permute-start | bytes 245768 | tf_op jit(solution)/shard_map/ppermute | solution.py:529
  10.4 6.9 %collective-permute-start.3 = (f32[40,512]{1,0:T(8,128)S(1)}, f32[40,512]{1,0:T(8,128)S(1)}, u32[]{:S(2)}, u32[]{:S(2)}) collective-permute-start(f32[40,512]{1,0:T(8,128)S(1)} %add.45), channel_id=1, source_target_pairs={{0,6},{1,7},{2,4},{3,5},{4,2},{5,3},{6,0},{7,1},{8,14},{9,15},{10,... | collective-permute-start | bytes 245768 | tf_op jit(solution)/shard_map/ppermute | solution.py:529
  14.6 6.1 %collective-permute-start.2 = (f32[40,512]{1,0:T(8,128)S(1)}, f32[40,512]{1,0:T(8,128)S(1)}, u32[]{:S(2)}, u32[]{:S(2)}) collective-permute-start(f32[40,512]{1,0:T(8,128)S(1)} %add.45), channel_id=1, source_target_pairs={{0,4},{1,5},{2,6},{3,7},{4,0},{5,1},{6,2},{7,3},{8,12},{9,13},{10,... | collective-permute-start | bytes 245768 | tf_op jit(solution)/shard_map/ppermute | solution.py:529
  14.6 6.1 %collective-permute-start.1 = (f32[40,512]{1,0:T(8,128)S(1)}, f32[40,512]{1,0:T(8,128)S(1)}, u32[]{:S(2)}, u32[]{:S(2)}) collective-permute-start(f32[40,512]{1,0:T(8,128)S(1)} %add.45), channel_id=1, source_target_pairs={{0,2},{1,3},{2,0},{3,1},{4,6},{5,7},{6,4},{7,5},{8,10},{9,11},{10,... | collective-permute-start | bytes 245768 | tf_op jit(solution)/shard_map/ppermute | solution.py:529
  25.8 4.6 %collective-permute-start.5 = (f32[384,256]{1,0:T(8,128)S(1)}, f32[384,256]{1,0:T(8,128)S(1)}, u32[]{:S(2)}, u32[]{:S(2)}) collective-permute-start(f32[384,256]{1,0:T(8,128)S(1)} %get-tuple-element.73), channel_id=1, source_target_pairs={{0,8},{1,9},{2,10},{3,11},{4,12},{5,13},{6,14},{7,15},{8,0},{9,1},... | collective-permute-start | bytes 1179656 | tf_op jit(solution)/shard_map/ppermute | solution.py:529
  25.9 4.5 %collective-permute-start.4 = (f32[32,512]{1,0:T(8,128)S(1)}, f32[32,512]{1,0:T(8,128)S(1)}, u32[]{:S(2)}, u32[]{:S(2)}) collective-permute-start(f32[32,512]{1,0:T(8,128)S(1)} %get-tuple-element.70), channel_id=1, source_target_pairs={{0,1},{1,0},{2,3},{3,2},{4,5},{5,4},{6,7},{7,6},{8,9},{9,8},{10,11... | collective-permute-start | bytes 196616 | tf_op jit(solution)/shard_map/ppermute | solution.py:529
  30.5 6.4 %collective-permute-start.8 = (f32[32,512]{1,0:T(8,128)S(1)}, f32[32,512]{1,0:T(8,128)S(1)}, u32[]{:S(2)}, u32[]{:S(2)}) collective-permute-start(f32[32,512]{1,0:T(8,128)S(1)} %add.49), channel_id=1, source_target_pairs={{0,6},{1,7},{2,4},{3,5},{4,2},{5,3},{6,0},{7,1},{8,14},{9,15},{10,... | collective-permute-start | bytes 196616 | tf_op jit(solution)/shard_map/ppermute | solution.py:529
  32.8 6.2 %collective-permute-start.7 = (f32[32,512]{1,0:T(8,128)S(1)}, f32[32,512]{1,0:T(8,128)S(1)}, u32[]{:S(2)}, u32[]{:S(2)}) collective-permute-start(f32[32,512]{1,0:T(8,128)S(1)} %add.49), channel_id=1, source_target_pairs={{0,4},{1,5},{2,6},{3,7},{4,0},{5,1},{6,2},{7,3},{8,12},{9,13},{10,... | collective-permute-start | bytes 196616 | tf_op jit(solution)/shard_map/ppermute | solution.py:529
  32.8 6.2 %collective-permute-start.6 = (f32[32,512]{1,0:T(8,128)S(1)}, f32[32,512]{1,0:T(8,128)S(1)}, u32[]{:S(2)}, u32[]{:S(2)}) collective-permute-start(f32[32,512]{1,0:T(8,128)S(1)} %add.49), channel_id=1, source_target_pairs={{0,2},{1,3},{2,0},{3,1},{4,6},{5,7},{6,4},{7,5},{8,10},{9,11},{10,... | collective-permute-start | bytes 196616 | tf_op jit(solution)/shard_map/ppermute | solution.py:529
  35.0 5.7 %collective-permute-start.9 = (f32[192,256]{1,0:T(8,128)S(1)}, f32[192,256]{1,0:T(8,128)S(1)}, u32[]{:S(2)}, u32[]{:S(2)}) collective-permute-start(f32[192,256]{1,0:T(8,128)S(1)} %get-tuple-element.78), channel_id=1, source_target_pairs={{0,1},{1,0},{2,3},{3,2},{4,5},{5,4},{6,7},{7,6},{8,24},{9,25},{10,... | collective-permute-start | bytes 589832 | tf_op jit(solution)/shard_map/ppermute | solution.py:529
  40.7 6.1 %collective-permute-start.10 = (f32[96,256]{1,0:T(8,128)S(1)}, f32[96,256]{1,0:T(8,128)S(1)}, u32[]{:S(2)}, u32[]{:S(2)}) collective-permute-start(f32[96,256]{1,0:T(8,128)S(1)} %get-tuple-element.86), channel_id=1, source_target_pairs={{0,16},{1,17},{2,18},{3,19},{4,20},{5,21},{6,22},{7,23},{8,9},{9,8... | collective-permute-start | bytes 294920 | tf_op jit(solution)/shard_map/ppermute | solution.py:529
  46.8 1.7 %collective-permute-start.11 = (f32[272,256]{1,0:T(8,128)S(1)}, f32[272,256]{1,0:T(8,128)S(1)}, u32[]{:S(2)}, u32[]{:S(2)}) collective-permute-start(f32[272,256]{1,0:T(8,128)S(1)} %get-tuple-element.88), channel_id=1, source_target_pairs={{0,8},{1,9},{2,10},{3,11},{4,12},{5,13},{6,14},{7,15},{8,0},{9,1},... | collective-permute-start | bytes 835592 | tf_op jit(solution)/shard_map/ppermute | solution.py:529
  48.5 7.1 %collective-permute-start.12 = (f32[136,256]{1,0:T(8,128)S(1)}, f32[136,256]{1,0:T(8,128)S(1)}, u32[]{:S(2)}, u32[]{:S(2)}) collective-permute-start(f32[136,256]{1,0:T(8,128)S(1)} %get-tuple-element.94), channel_id=1, source_target_pairs={{0,1},{1,0},{2,3},{3,2},{4,5},{5,4},{6,7},{7,6},{8,24},{9,25},{10,... | collective-permute-start | bytes 417800 | tf_op jit(solution)/shard_map/ppermute | solution.py:529
  50.1 5.5 %collective-permute-start.13 = (f32[96,256]{1,0:T(8,128)S(1)}, f32[96,256]{1,0:T(8,128)S(1)}, u32[]{:S(2)}, u32[]{:S(2)}) collective-permute-start(f32[96,256]{1,0:T(8,128)S(1)} %add.53), channel_id=1, source_target_pairs={{0,2},{1,3},{2,0},{3,1},{4,6},{5,7},{6,4},{7,5},{8,12},{9,13},{10,... | collective-permute-start | bytes 294920 | tf_op jit(solution)/shard_map/ppermute | solution.py:529
  55.6 6.7 %collective-permute-start.14 = (f32[136,256]{1,0:T(8,128)S(1)}, f32[136,256]{1,0:T(8,128)S(1)}, u32[]{:S(2)}, u32[]{:S(2)}) collective-permute-start(f32[136,256]{1,0:T(8,128)S(1)} %add.54), channel_id=1, source_target_pairs={{0,16},{1,17},{2,18},{3,19},{4,20},{5,21},{6,22},{7,23},{8,9},{9,8... | collective-permute-start | bytes 417800 | tf_op jit(solution)/shard_map/ppermute | solution.py:529
  56.4 6.0 %collective-permute-start.15 = (f32[96,256]{1,0:T(8,128)S(1)}, f32[96,256]{1,0:T(8,128)S(1)}, u32[]{:S(2)}, u32[]{:S(2)}) collective-permute-start(f32[96,256]{1,0:T(8,128)S(1)} %add.55), channel_id=1, source_target_pairs={{0,4},{1,5},{2,6},{3,7},{4,0},{5,1},{6,2},{7,3},{8,10},{9,11},{10,... | collective-permute-start | bytes 294920 | tf_op jit(solution)/shard_map/ppermute | solution.py:529
  62.4 4.7 %collective-permute-start.17 = (f32[96,256]{1,0:T(8,128)S(1)}, f32[96,256]{1,0:T(8,128)S(1)}, u32[]{:S(2)}, u32[]{:S(2)}) collective-permute-start(f32[96,256]{1,0:T(8,128)S(1)} %add.57), channel_id=1, source_target_pairs={{0,16},{1,17},{2,18},{3,19},{4,20},{5,21},{6,22},{7,23},{8,9},{9,8... | collective-permute-start | bytes 294920 | tf_op jit(solution)/shard_map/ppermute | solution.py:529
  63.6 5.1 %collective-permute-start.16 = (f32[136,256]{1,0:T(8,128)S(1)}, f32[136,256]{1,0:T(8,128)S(1)}, u32[]{:S(2)}, u32[]{:S(2)}) collective-permute-start(f32[136,256]{1,0:T(8,128)S(1)} %add.56), channel_id=1, source_target_pairs={{0,2},{1,3},{2,0},{3,1},{4,6},{5,7},{6,4},{7,5},{8,12},{9,13},{10,... | collective-permute-start | bytes 417800 | tf_op jit(solution)/shard_map/ppermute | solution.py:529
  68.6 14.9 %copy-start.1 = (f32[256,256]{1,0:T(8,128)S(1)}, f32[256,256]{1,0:T(8,128)}, u32[]{:S(2)}) copy-start(f32[256,256]{1,0:T(8,128)} %fx_weight.1) | copy-start | bytes 786436
  68.7 8.0 %collective-permute-start.19 = (f32[192,256]{1,0:T(8,128)S(1)}, f32[192,256]{1,0:T(8,128)S(1)}, u32[]{:S(2)}, u32[]{:S(2)}) collective-permute-start(f32[192,256]{1,0:T(8,128)S(1)} %pad_maximum_fusion.2), channel_id=1, source_target_pairs={{0,1},{1,0},{2,3},{3,2},{4,5},{5,4},{6,7},{7,6},{8,24},{9,25},{10,... | collective-permute-start | bytes 589832 | tf_op jit(solution)/shard_map/ppermute | solution.py:529
  69.7 6.9 %collective-permute-start.18 = (f32[136,256]{1,0:T(8,128)S(1)}, f32[136,256]{1,0:T(8,128)S(1)}, u32[]{:S(2)}, u32[]{:S(2)}) collective-permute-start(f32[136,256]{1,0:T(8,128)S(1)} %add.58), channel_id=1, source_target_pairs={{0,4},{1,5},{2,6},{3,7},{4,0},{5,1},{6,2},{7,3},{8,10},{9,11},{10,... | collective-permute-start | bytes 417800 | tf_op jit(solution)/shard_map/ppermute | solution.py:529
  76.7 5.2 %collective-permute-start.21 = (f32[384,256]{1,0:T(8,128)S(1)}, f32[384,256]{1,0:T(8,128)S(1)}, u32[]{:S(2)}, u32[]{:S(2)}) collective-permute-start(f32[384,256]{1,0:T(8,128)S(1)} %pad_maximum_fusion.own), channel_id=1, source_target_pairs={{0,8},{1,9},{2,10},{3,11},{4,12},{5,13},{6,14},{7,15},{8,0},{9,1},... | collective-permute-start | bytes 1179656 | tf_op jit(solution)/shard_map/ppermute | solution.py:529
  76.8 5.1 %collective-permute-start.20 = (f32[136,256]{1,0:T(8,128)S(1)}, f32[136,256]{1,0:T(8,128)S(1)}, u32[]{:S(2)}, u32[]{:S(2)}) collective-permute-start(f32[136,256]{1,0:T(8,128)S(1)} %add.59), channel_id=1, source_target_pairs={{0,1},{1,0},{2,3},{3,2},{4,5},{5,4},{6,7},{7,6},{8,24},{9,25},{10,... | collective-permute-start | bytes 417800 | tf_op jit(solution)/shard_map/ppermute | solution.py:529
  81.9 1.6 %collective-permute-start.22 = (f32[272,256]{1,0:T(8,128)S(1)}, f32[272,256]{1,0:T(8,128)S(1)}, u32[]{:S(2)}, u32[]{:S(2)}) collective-permute-start(f32[272,256]{1,0:T(8,128)S(1)} %pad_maximum_fusion.1.own), channel_id=1, source_target_pairs={{0,8},{1,9},{2,10},{3,11},{4,12},{5,13},{6,14},{7,15},{8,0},{9,1},... | collective-permute-start | bytes 835592 | tf_op jit(solution)/shard_map/ppermute | solution.py:529
  (11 other events, 161.1 us)

commit v4 on v3

--- a/solution.py
+++ b/solution.py
@@ -12,8 +12,8 @@
 BF16 = jnp.bfloat16
 GROUP = 4
 EPS = 1e-05
-EARLY = 2
-LATE = 1
+EARLY = 0
+LATE = 0
 GELU_A = math.sqrt(2.0 / math.pi)
 GELU_B = 0.044715
 SMALL = 16 * 1024 * 1024
@@ -31,6 +31,11 @@
             a, b, (((left_dim,), (right_dim,)), ((), ())), preferred_element_type=F32
         )
 
+    if left[0].shape[left_dim] % 128 == 0:
+        return one(
+            jnp.concatenate([left[0], left[0], left[1]], axis=left_dim),
+            jnp.concatenate([right[0], right[1], right[0]], axis=right_dim),
+        )
     return one(left[0], right[0]) + (one(left[0], right[1]) + one(left[1], right[0]))
 
 
@@ -311,6 +316,25 @@
     other[...] = block(value, 1 - core, half)[...]
 
 
+def quarter():
+    return 2 * lax.rem(lax.axis_index("point"), 2) + lax.rem(lax.axis_index("dp") // 2, 2)
+
+
+def add_quarter_kernel(mine, received, *parts):
+    size = parts[0].shape[0]
+    for i, part in enumerate(parts):
+        index = quarter() ^ i
+        part[...] = block(mine, index, size)[...] + block(received, index, size)[...]
+
+
+def arrange_quarters(own, partner, result):
+    core = lax.rem(lax.axis_index("dp"), 2)
+    size = own.shape[0] // 4
+    for side, ref in ((core, own), (1 - core, partner)):
+        for i in range(4):
+            block(result, 4 * side + (quarter() ^ i), size)[...] = ref[i * size : (i + 1) * size]
+
+
 def add_halve_kernel(axes, mine, received, kept, sent):
     half = kept.shape[0]
     upper, _ = place(axes)
@@ -319,6 +343,8 @@
 
 
 def arrange(levels, own, partner, result):
+    if not levels:
+        return arrange_quarters(own, partner, result)
     core = lax.rem(lax.axis_index("dp"), 2)
     count = 1 << len(levels)
     size = own.shape[0] // count
@@ -577,7 +603,37 @@
     )
 
 
+def quarter_steps(sizes):
+    group = [lambda d, p: (d ^ 2, p), lambda d, p: (d, p ^ 1), lambda d, p: (d ^ 2, p ^ 1)]
+    others = paired([(0, b) for b in bits(sizes[0])[2:]] + [(1, b) for b in bits(sizes[1])[1:]])
+
+    def cores(value):
+        received = swap(value[1], flips(CORES), sizes)
+        part = (value[0].shape[0] // 4, value[0].shape[1])
+        return call(
+            add_quarter_kernel, "add_quarter", [VMEM] * 2, [VMEM] * 4,
+            [jax.ShapeDtypeStruct(part, F32)] * 4, (value[0], received), received.size,
+        )
+
+    def scatter(value):
+        parts = [swap(part, moves, sizes) for part, moves in zip(value[1:], group)]
+        return (value[0] + parts[0]) + (parts[1] + parts[2])
+
+    def add(axes):
+        return lambda value: value + swap(value, flips(axes), sizes)
+
+    def gather(value):
+        return jnp.concatenate([value] + [swap(value, moves, sizes) for moves in group], axis=0)
+
+    def last(value):
+        return value, swap(value, flips(CORES), sizes)
+
+    return [cores, scatter] + [add(axes) for axes in others] + [gather, last]
+
+
 def all_steps(sizes, scatters):
+    if scatters == 0:
+        return quarter_steps(sizes)
     steps_axes = all_axes(sizes)
 
     def add_halve(i, mine, received):
@@ -680,19 +736,15 @@
         [shape(3 * width // 2, width)] * 2, (columns, back), 3 * dense,
         scratch=[pltpu.VMEM((3 * width, width), F32)],
     )
-    early_steps = all_steps(sizes, EARLY)
-    taken = 0
+    behind = [early_value]
+    for step in all_steps(sizes, EARLY):
+        behind.append(step(behind[-1]))
+    order = [0, 1]
     for i, step in enumerate(point_steps(sizes)):
-        if taken < len(early_steps):
-            early_new = early_steps[taken](early_value)
-            taken += 1
-        else:
-            early_new = early_value
-        out_sum, early_value = tie(step(out_sum), early_new)
-    if taken < len(early_steps):
-        early_value = early_steps[taken](early_value)
-        taken += 1
-    rows = 2 * width + head_size
+        out_sum = step(out_sum)
+        if i < len(order) and order[i] is not None:
+            out_sum, _ = tie(out_sum, behind[order[i]])
+    rows = -(-(2 * width + head_size) // 64) * 64
     mine, other, end = call(
         functools.partial(end_kernel, factor, factor / sizes[1], head_size, slices), "end",
         [VMEM] * 6, [VMEM] * 3,
@@ -701,7 +753,7 @@
         8 * dense,
         scratch=[pltpu.VMEM((rows, width), F32)],
     )
-    late, early_value = tie((mine, other), early_value)
+    late, _ = tie((mine, other), behind[1])
     input_grad = call(
         rows_kernel, "rows", [VMEM] * 4, VMEM, shape(1, points, width),
         (front, front_wide, back_wide, end), 2 * dense,
@@ -709,15 +761,12 @@
     steps = all_steps(sizes, LATE)
     for i, step in enumerate(steps):
         late = step(late)
-        if i > 0 and taken < len(early_steps):
-            late, early_value = tie(late, early_steps[taken](early_value))
-            taken += 1
         if i == 0:
             late, input_grad = tie(late, input_grad)
     matrices, gain_row = call(
         functools.partial(early_out_kernel, tuple(axes[:EARLY])), "early_out", [VMEM] * 4, [HBM, VMEM],
         [shape(5, width, width), shape(1, width)],
-        (*early_value, gain_two, expand_weight),
+        (*behind[-1], gain_two, expand_weight),
         dense // 8,
         scratch=[pltpu.VMEM((3 * width, width), F32), pltpu.VMEM((width, width), F32),
                  pltpu.SemaphoreType.DMA((3,))],

time: 85.4 us -> 78.2 us (0.916)
  waiting for transfers between devices: 41.6 us -> 23.5 us
  starting transfers between devices: 23.5 us -> 35.3 us
    ppermute x23 -> x28, waiting for transfers between devices: 41.6 us -> 23.5 us  [swap(): return lax.ppermute(value, ('dp', 'point'), pairs)]
    ppermute x23 -> x28, starting transfers between devices: 23.5 us -> 35.3 us  [swap(): return lax.ppermute(value, ('dp', 'point'), pairs)]
    pallas_call x11 -> x10, Pallas kernels: 18.9 us -> 18.1 us  [call(): pl.pallas_call(body, name=name, in_specs=in_specs, out_specs=out_specs, o...]
  transfers between devices with their start and end apart: 23 -> 28, of which waited for: 14 -> 13; matrix products, arithmetic and copies ran while one was open for 0% -> 0% of each run, Pallas kernels for 9% -> 9%
where the time goes in v4:
time: 78.2 us; the launch traced here: 78.1 us
  starting transfers between devices  35.3 us (45%)
  waiting for transfers between devices  23.5 us (30%)
  Pallas kernels  18.1 us (23%)
  between operations  0.96 us (1%)
    ppermute x28, starting transfers between devices, swap(): return lax.ppermute(value, ('dp', 'point'), pairs)  35.3 us
    ppermute x28, waiting for transfers between devices, swap(): return lax.ppermute(value, ('dp', 'point'), pairs)  23.5 us
    pallas_call x10, Pallas kernels, call(): pl.pallas_call(body, name=name, in_specs=in_specs, out_specs=out_specs, o...  18.1 us
  transfers between devices with their start and end apart: 28, of which 13 were waited for; matrix products, arithmetic and copies ran while one was open for 0% of the time, Pallas kernels for 9%

profile of v4, /device:TPU:0, one launch (start us, length us, event | category | flops | bytes accessed | tf_op | source)
XLA Modules:
  0.0 78.1 jit_solution(5135169040074197521)
XLA Ops:
  0.7 4.0 %front.1 = (bf16[3072,512]{1,0:T(8,128)(2,1)S(1)}, f32[272,512]{1,0:T(8,128)S(1)}, f32[40,512]{1,0:T(8,128)S(1)}) custom-call(f32[1,512,256]{2,1,0:T(8,128)} %x_hbm.1, f32[1,256]{1,0:T(1,128)} %bitcast.4, f32[256,256]{1,0:T(8,128)} %fx_weight.1, f32[256,256]{1,0:T(8,128)} %x_weight.1, f32[32,64]{1,0:T(8,128)} %logit_weight.1, f32[8]{0:T(128)} %temper_hbm.1), custom_call_target="tpu_custom_call" | custom-call | flops 805306368 | bytes 1048576 | tf_op jit(solution)/shard_map/front/pallas_call | solution.py:535
  4.8 3.0 %collective-permute-start = (f32[40,512]{1,0:T(8,128)S(1)}, f32[40,512]{1,0:T(8,128)S(1)}, u32[]{:S(2)}, u32[]{:S(2)}) collective-permute-start(f32[40,512]{1,0:T(8,128)S(1)} %get-tuple-element.48), channel_id=1, source_target_pairs={{0,1},{1,0},{2,3},{3,2},{4,5},{5,4},{6,7},{7,6},{8,9},{9,8},{10,11... | collective-permute-start | bytes 245768 | tf_op jit(solution)/shard_map/ppermute | solution.py:555
  7.8 2.5 %collective-permute-done = f32[40,512]{1,0:T(8,128)S(1)} collective-permute-done((f32[40,512]{1,0:T(8,128)S(1)}, f32[40,512]{1,0:T(8,128)S(1)}, u32[]{:S(2)}, u32[]{:S(2)}) %collective-permute-start) | collective-permute-done | bytes 81952 | tf_op jit(solution)/shard_map/ppermute | solution.py:555
  10.2 4.2 %collective-permute-start.3 = (f32[40,512]{1,0:T(8,128)S(1)}, f32[40,512]{1,0:T(8,128)S(1)}, u32[]{:S(2)}, u32[]{:S(2)}) collective-permute-start(f32[40,512]{1,0:T(8,128)S(1)} %add.54), channel_id=1, source_target_pairs={{0,6},{1,7},{2,4},{3,5},{4,2},{5,3},{6,0},{7,1},{8,14},{9,15},{10,... | collective-permute-start | bytes 245768 | tf_op jit(solution)/shard_map/ppermute | solution.py:555
  17.2 3.4 %collective-permute-done.2 = f32[40,512]{1,0:T(8,128)S(1)} collective-permute-done((f32[40,512]{1,0:T(8,128)S(1)}, f32[40,512]{1,0:T(8,128)S(1)}, u32[]{:S(2)}, u32[]{:S(2)}) %collective-permute-start.2) | collective-permute-done | bytes 81952 | tf_op jit(solution)/shard_map/ppermute | solution.py:555
  20.6 4.1 %back.1 = (f32[32,512]{1,0:T(8,128)S(1)}, bf16[3072,512]{1,0:T(8,128)(2,1)S(1)}, f32[552,512]{1,0:T(8,128)S(1)}) custom-call(f32[40,512]{1,0:T(8,128)S(1)} %add_add_fusion.1.sums, bf16[3072,512]{1,0:T(8,128)(2,1)S(1)} %get-tuple-element.49.front, f32[272,512]{1,0:T(8,128)S(1)} %get-tuple-element.50.front_wide, ...), custom_call_target="tpu_custom_call" | custom-call | flops 1207959552 | bytes 1048576 | tf_op jit(solution)/shard_map/back/pallas_call | solution.py:535
  25.7 1.5 %collective-permute-start.4 = (f32[32,512]{1,0:T(8,128)S(1)}, f32[32,512]{1,0:T(8,128)S(1)}, u32[]{:S(2)}, u32[]{:S(2)}) collective-permute-start(f32[32,512]{1,0:T(8,128)S(1)} %get-tuple-element.58), channel_id=1, source_target_pairs={{0,1},{1,0},{2,3},{3,2},{4,5},{5,4},{6,7},{7,6},{8,9},{9,8},{10,11... | collective-permute-start | bytes 196616 | tf_op jit(solution)/shard_map/ppermute | solution.py:555
  27.2 3.0 %collective-permute-done.4 = f32[32,512]{1,0:T(8,128)S(1)} collective-permute-done((f32[32,512]{1,0:T(8,128)S(1)}, f32[32,512]{1,0:T(8,128)S(1)}, u32[]{:S(2)}, u32[]{:S(2)}) %collective-permute-start.4) | collective-permute-done | bytes 65568 | tf_op jit(solution)/shard_map/ppermute | solution.py:555
  30.2 2.3 %collective-permute-start.7 = (f32[32,512]{1,0:T(8,128)S(1)}, f32[32,512]{1,0:T(8,128)S(1)}, u32[]{:S(2)}, u32[]{:S(2)}) collective-permute-start(f32[32,512]{1,0:T(8,128)S(1)} %add.58), channel_id=1, source_target_pairs={{0,6},{1,7},{2,4},{3,5},{4,2},{5,3},{6,0},{7,1},{8,14},{9,15},{10,... | collective-permute-start | bytes 196616 | tf_op jit(solution)/shard_map/ppermute | solution.py:555
  32.5 2.1 %collective-permute-start.5 = (f32[32,512]{1,0:T(8,128)S(1)}, f32[32,512]{1,0:T(8,128)S(1)}, u32[]{:S(2)}, u32[]{:S(2)}) collective-permute-start(f32[32,512]{1,0:T(8,128)S(1)} %add.58), channel_id=1, source_target_pairs={{0,2},{1,3},{2,0},{3,1},{4,6},{5,7},{6,4},{7,5},{8,10},{9,11},{10,... | collective-permute-start | bytes 196616 | tf_op jit(solution)/shard_map/ppermute | solution.py:555
  34.7 1.9 %collective-permute-done.7 = f32[32,512]{1,0:T(8,128)S(1)} collective-permute-done((f32[32,512]{1,0:T(8,128)S(1)}, f32[32,512]{1,0:T(8,128)S(1)}, u32[]{:S(2)}, u32[]{:S(2)}) %collective-permute-start.7) | collective-permute-done | bytes 65568 | tf_op jit(solution)/shard_map/ppermute | solution.py:555
  36.6 2.1 %collective-permute-done.6 = f32[32,512]{1,0:T(8,128)S(1)} collective-permute-done((f32[32,512]{1,0:T(8,128)S(1)}, f32[32,512]{1,0:T(8,128)S(1)}, u32[]{:S(2)}, u32[]{:S(2)}) %collective-permute-start.6) | collective-permute-done | bytes 65568 | tf_op jit(solution)/shard_map/ppermute | solution.py:555
  38.7 1.6 %collective-permute-start.19 = (f32[96,256]{1,0:T(8,128)S(1)}, f32[96,256]{1,0:T(8,128)S(1)}, u32[]{:S(2)}, u32[]{:S(2)}) collective-permute-start(f32[96,256]{1,0:T(8,128)S(1)} %get-tuple-element.64), channel_id=1, source_target_pairs={{0,16},{1,17},{2,18},{3,19},{4,20},{5,21},{6,22},{7,23},{8,24},{9,... | collective-permute-start | bytes 294920 | tf_op jit(solution)/shard_map/ppermute | solution.py:555
  40.3 1.5 %collective-permute-start.20 = (f32[96,256]{1,0:T(8,128)S(1)}, f32[96,256]{1,0:T(8,128)S(1)}, u32[]{:S(2)}, u32[]{:S(2)}) collective-permute-start(f32[96,256]{1,0:T(8,128)S(1)} %get-tuple-element.65), channel_id=1, source_target_pairs={{0,1},{1,0},{2,3},{3,2},{4,5},{5,4},{6,7},{7,6},{8,9},{9,8},{10,11... | collective-permute-start | bytes 294920 | tf_op jit(solution)/shard_map/ppermute | solution.py:555
  42.3 3.9 %end.1 = (f32[288,256]{1,0:T(8,128)S(1)}, f32[288,256]{1,0:T(8,128)S(1)}, bf16[1024,512]{1,0:T(8,128)(2,1)S(1)}) custom-call(f32[32,512]{1,0:T(8,128)S(1)} %add_add_fusion.3.out_sum, bf16[3072,512]{1,0:T(8,128)(2,1)S(1)} %get-tuple-element.49.front, f32[272,512]{1,0:T(8,128)S(1)} %get-tuple-element.50.front_wide, ...), custom_call_target="tpu_custom_call" | custom-call | flops 1610612736 | bytes 1048576 | tf_op jit(solution)/shard_map/end/pallas_call | solution.py:535
  47.8 1.6 %rows.1 = f32[1,512,256]{2,1,0:T(8,128)} custom-call(bf16[3072,512]{1,0:T(8,128)(2,1)S(1)} %get-tuple-element.49.front, f32[272,512]{1,0:T(8,128)S(1)} %get-tuple-element.50.front_wide, f32[552,512]{1,0:T(8,128)S(1)} %get-tuple-element.68.back_wide, bf16[1024,512]{1,0:T(8,128)(2,1)S(1)} %get-tuple-element.77.end), custom_call_target="tpu_custom_call" | custom-call | flops 402653184 | bytes 1048576 | tf_op jit(solution)/shard_map/rows/pallas_call | solution.py:535
  53.1 2.4 %collective-permute-start.23 = (f32[96,256]{1,0:T(8,128)S(1)}, f32[96,256]{1,0:T(8,128)S(1)}, u32[]{:S(2)}, u32[]{:S(2)}) collective-permute-start(f32[96,256]{1,0:T(8,128)S(1)} %add.70), channel_id=1, source_target_pairs={{0,4},{1,5},{2,6},{3,7},{4,0},{5,1},{6,2},{7,3},{8,10},{9,11},{10,... | collective-permute-start | bytes 294920 | tf_op jit(solution)/shard_map/ppermute | solution.py:555
  57.0 2.0 %collective-permute-start.13 = (f32[72,256]{1,0:T(8,128)S(1)}, f32[72,256]{1,0:T(8,128)S(1)}, u32[]{:S(2)}, u32[]{:S(2)}) collective-permute-start(f32[72,256]{1,0:T(8,128)S(1)} %add_add_fusion.2), channel_id=1, source_target_pairs={{0,2},{1,3},{2,0},{3,1},{4,6},{5,7},{6,4},{7,5},{8,12},{9,13},{10,... | collective-permute-start | bytes 221192 | tf_op jit(solution)/shard_map/ppermute | solution.py:555
  59.0 1.7 %collective-permute-start.26 = (f32[96,256]{1,0:T(8,128)S(1)}, f32[96,256]{1,0:T(8,128)S(1)}, u32[]{:S(2)}, u32[]{:S(2)}) collective-permute-start(f32[96,256]{1,0:T(8,128)S(1)} %add.71), channel_id=1, source_target_pairs={{0,17},{1,16},{2,19},{3,18},{4,21},{5,20},{6,23},{7,22},{8,25},{9,... | collective-permute-start | bytes 294920 | tf_op jit(solution)/shard_map/ppermute | solution.py:555
  62.6 2.1 %collective-permute-start.14 = (f32[72,256]{1,0:T(8,128)S(1)}, f32[72,256]{1,0:T(8,128)S(1)}, u32[]{:S(2)}, u32[]{:S(2)}) collective-permute-start(f32[72,256]{1,0:T(8,128)S(1)} %add.65), channel_id=1, source_target_pairs={{0,4},{1,5},{2,6},{3,7},{4,0},{5,1},{6,2},{7,3},{8,10},{9,11},{10,... | collective-permute-start | bytes 221192 | tf_op jit(solution)/shard_map/ppermute | solution.py:555
  64.7 3.2 %collective-permute-done.14 = f32[72,256]{1,0:T(8,128)S(1)} collective-permute-done((f32[72,256]{1,0:T(8,128)S(1)}, f32[72,256]{1,0:T(8,128)S(1)}, u32[]{:S(2)}, u32[]{:S(2)}) %collective-permute-start.14) | collective-permute-done | bytes 73760 | tf_op jit(solution)/shard_map/ppermute | solution.py:555
  68.0 1.7 %collective-permute-start.17 = (f32[72,256]{1,0:T(8,128)S(1)}, f32[72,256]{1,0:T(8,128)S(1)}, u32[]{:S(2)}, u32[]{:S(2)}) collective-permute-start(f32[72,256]{1,0:T(8,128)S(1)} %add.66), channel_id=1, source_target_pairs={{0,17},{1,16},{2,19},{3,18},{4,21},{5,20},{6,23},{7,22},{8,25},{9,... | collective-permute-start | bytes 221192 | tf_op jit(solution)/shard_map/ppermute | solution.py:555
  71.7 1.6 %collective-permute-done.17 = f32[72,256]{1,0:T(8,128)S(1)} collective-permute-done((f32[72,256]{1,0:T(8,128)S(1)}, f32[72,256]{1,0:T(8,128)S(1)}, u32[]{:S(2)}, u32[]{:S(2)}) %collective-permute-start.17) | collective-permute-done | bytes 73760 | tf_op jit(solution)/shard_map/ppermute | solution.py:555
  76.3 1.7 %late_out.1 = (f32[5,256,256]{2,1,0:T(8,128)}, f32[3,32,32]{2,1,0:T(8,128)}, f32[32,64]{1,0:T(8,128)}, f32[2,256]{1,0:T(2,128)}) custom-call(f32[288,256]{1,0:T(8,128)S(1)} %pad_maximum_fusion.1.own, f32[288,256]{1,0:T(8,128)S(1)} %collective-permute-done.18.partner, f32[1,256]{1,0:T(1,128)S(1)} %bitcast.5, ...), custom_call_target="tpu_custom_call", output_to_operand_aliasing={{0}: (6, {})} | custom-call | flops 25165824 | bytes 1048576 | tf_op jit(solution)/shard_map/late_out/pallas_call | solution.py:535
  (78 shorter events, 17.9 us)
Async XLA Ops:
  4.8 5.5 %collective-permute-start = (f32[40,512]{1,0:T(8,128)S(1)}, f32[40,512]{1,0:T(8,128)S(1)}, u32[]{:S(2)}, u32[]{:S(2)}) collective-permute-start(f32[40,512]{1,0:T(8,128)S(1)} %get-tuple-element.48), channel_id=1, source_target_pairs={{0,1},{1,0},{2,3},{3,2},{4,5},{5,4},{6,7},{7,6},{8,9},{9,8},{10,11... | collective-permute-start | bytes 245768 | tf_op jit(solution)/shard_map/ppermute | solution.py:555
  10.2 6.9 %collective-permute-start.3 = (f32[40,512]{1,0:T(8,128)S(1)}, f32[40,512]{1,0:T(8,128)S(1)}, u32[]{:S(2)}, u32[]{:S(2)}) collective-permute-start(f32[40,512]{1,0:T(8,128)S(1)} %add.54), channel_id=1, source_target_pairs={{0,6},{1,7},{2,4},{3,5},{4,2},{5,3},{6,0},{7,1},{8,14},{9,15},{10,... | collective-permute-start | bytes 245768 | tf_op jit(solution)/shard_map/ppermute | solution.py:555
  14.4 6.1 %collective-permute-start.2 = (f32[40,512]{1,0:T(8,128)S(1)}, f32[40,512]{1,0:T(8,128)S(1)}, u32[]{:S(2)}, u32[]{:S(2)}) collective-permute-start(f32[40,512]{1,0:T(8,128)S(1)} %add.54), channel_id=1, source_target_pairs={{0,4},{1,5},{2,6},{3,7},{4,0},{5,1},{6,2},{7,3},{8,12},{9,13},{10,... | collective-permute-start | bytes 245768 | tf_op jit(solution)/shard_map/ppermute | solution.py:555
  14.4 6.1 %collective-permute-start.1 = (f32[40,512]{1,0:T(8,128)S(1)}, f32[40,512]{1,0:T(8,128)S(1)}, u32[]{:S(2)}, u32[]{:S(2)}) collective-permute-start(f32[40,512]{1,0:T(8,128)S(1)} %add.54), channel_id=1, source_target_pairs={{0,2},{1,3},{2,0},{3,1},{4,6},{5,7},{6,4},{7,5},{8,10},{9,11},{10,... | collective-permute-start | bytes 245768 | tf_op jit(solution)/shard_map/ppermute | solution.py:555
  25.6 13.1 %collective-permute-start.8 = (f32[384,256]{1,0:T(8,128)S(1)}, f32[384,256]{1,0:T(8,128)S(1)}, u32[]{:S(2)}, u32[]{:S(2)}) collective-permute-start(f32[384,256]{1,0:T(8,128)S(1)} %get-tuple-element.61), channel_id=1, source_target_pairs={{0,8},{1,9},{2,10},{3,11},{4,12},{5,13},{6,14},{7,15},{8,0},{9,1},... | collective-permute-start | bytes 1179656 | tf_op jit(solution)/shard_map/ppermute | solution.py:555
  25.7 4.5 %collective-permute-start.4 = (f32[32,512]{1,0:T(8,128)S(1)}, f32[32,512]{1,0:T(8,128)S(1)}, u32[]{:S(2)}, u32[]{:S(2)}) collective-permute-start(f32[32,512]{1,0:T(8,128)S(1)} %get-tuple-element.58), channel_id=1, source_target_pairs={{0,1},{1,0},{2,3},{3,2},{4,5},{5,4},{6,7},{7,6},{8,9},{9,8},{10,11... | collective-permute-start | bytes 196616 | tf_op jit(solution)/shard_map/ppermute | solution.py:555
  30.2 6.4 %collective-permute-start.7 = (f32[32,512]{1,0:T(8,128)S(1)}, f32[32,512]{1,0:T(8,128)S(1)}, u32[]{:S(2)}, u32[]{:S(2)}) collective-permute-start(f32[32,512]{1,0:T(8,128)S(1)} %add.58), channel_id=1, source_target_pairs={{0,6},{1,7},{2,4},{3,5},{4,2},{5,3},{6,0},{7,1},{8,14},{9,15},{10,... | collective-permute-start | bytes 196616 | tf_op jit(solution)/shard_map/ppermute | solution.py:555
  32.5 6.1 %collective-permute-start.6 = (f32[32,512]{1,0:T(8,128)S(1)}, f32[32,512]{1,0:T(8,128)S(1)}, u32[]{:S(2)}, u32[]{:S(2)}) collective-permute-start(f32[32,512]{1,0:T(8,128)S(1)} %add.58), channel_id=1, source_target_pairs={{0,4},{1,5},{2,6},{3,7},{4,0},{5,1},{6,2},{7,3},{8,12},{9,13},{10,... | collective-permute-start | bytes 196616 | tf_op jit(solution)/shard_map/ppermute | solution.py:555
  32.5 6.1 %collective-permute-start.5 = (f32[32,512]{1,0:T(8,128)S(1)}, f32[32,512]{1,0:T(8,128)S(1)}, u32[]{:S(2)}, u32[]{:S(2)}) collective-permute-start(f32[32,512]{1,0:T(8,128)S(1)} %add.58), channel_id=1, source_target_pairs={{0,2},{1,3},{2,0},{3,1},{4,6},{5,7},{6,4},{7,5},{8,10},{9,11},{10,... | collective-permute-start | bytes 196616 | tf_op jit(solution)/shard_map/ppermute | solution.py:555
  38.7 7.6 %collective-permute-start.19 = (f32[96,256]{1,0:T(8,128)S(1)}, f32[96,256]{1,0:T(8,128)S(1)}, u32[]{:S(2)}, u32[]{:S(2)}) collective-permute-start(f32[96,256]{1,0:T(8,128)S(1)} %get-tuple-element.64), channel_id=1, source_target_pairs={{0,16},{1,17},{2,18},{3,19},{4,20},{5,21},{6,22},{7,23},{8,24},{9,... | collective-permute-start | bytes 294920 | tf_op jit(solution)/shard_map/ppermute | solution.py:555
  40.3 6.0 %collective-permute-start.20 = (f32[96,256]{1,0:T(8,128)S(1)}, f32[96,256]{1,0:T(8,128)S(1)}, u32[]{:S(2)}, u32[]{:S(2)}) collective-permute-start(f32[96,256]{1,0:T(8,128)S(1)} %get-tuple-element.65), channel_id=1, source_target_pairs={{0,1},{1,0},{2,3},{3,2},{4,5},{5,4},{6,7},{7,6},{8,9},{9,8},{10,11... | collective-permute-start | bytes 294920 | tf_op jit(solution)/shard_map/ppermute | solution.py:555
  41.8 5.5 %collective-permute-start.21 = (f32[96,256]{1,0:T(8,128)S(1)}, f32[96,256]{1,0:T(8,128)S(1)}, u32[]{:S(2)}, u32[]{:S(2)}) collective-permute-start(f32[96,256]{1,0:T(8,128)S(1)} %get-tuple-element.66), channel_id=1, source_target_pairs={{0,17},{1,16},{2,19},{3,18},{4,21},{5,20},{6,23},{7,22},{8,25},{9,... | collective-permute-start | bytes 294920 | tf_op jit(solution)/shard_map/ppermute | solution.py:555
  47.4 5.7 %collective-permute-start.22 = (f32[96,256]{1,0:T(8,128)S(1)}, f32[96,256]{1,0:T(8,128)S(1)}, u32[]{:S(2)}, u32[]{:S(2)}) collective-permute-start(f32[96,256]{1,0:T(8,128)S(1)} %add_add_fusion), channel_id=1, source_target_pairs={{0,2},{1,3},{2,0},{3,1},{4,6},{5,7},{6,4},{7,5},{8,12},{9,13},{10,... | collective-permute-start | bytes 294920 | tf_op jit(solution)/shard_map/ppermute | solution.py:555
  49.5 6.0 %collective-permute-start.10 = (f32[72,256]{1,0:T(8,128)S(1)}, f32[72,256]{1,0:T(8,128)S(1)}, u32[]{:S(2)}, u32[]{:S(2)}) collective-permute-start(f32[72,256]{1,0:T(8,128)S(1)} %get-tuple-element.80), channel_id=1, source_target_pairs={{0,16},{1,17},{2,18},{3,19},{4,20},{5,21},{6,22},{7,23},{8,24},{9,... | collective-permute-start | bytes 221192 | tf_op jit(solution)/shard_map/ppermute | solution.py:555
  50.3 5.2 %collective-permute-start.11 = (f32[72,256]{1,0:T(8,128)S(1)}, f32[72,256]{1,0:T(8,128)S(1)}, u32[]{:S(2)}, u32[]{:S(2)}) collective-permute-start(f32[72,256]{1,0:T(8,128)S(1)} %get-tuple-element.81), channel_id=1, source_target_pairs={{0,1},{1,0},{2,3},{3,2},{4,5},{5,4},{6,7},{7,6},{8,9},{9,8},{10,11... | collective-permute-start | bytes 221192 | tf_op jit(solution)/shard_map/ppermute | solution.py:555
  51.7 5.3 %collective-permute-start.12 = (f32[72,256]{1,0:T(8,128)S(1)}, f32[72,256]{1,0:T(8,128)S(1)}, u32[]{:S(2)}, u32[]{:S(2)}) collective-permute-start(f32[72,256]{1,0:T(8,128)S(1)} %get-tuple-element.82), channel_id=1, source_target_pairs={{0,17},{1,16},{2,19},{3,18},{4,21},{5,20},{6,23},{7,22},{8,25},{9,... | collective-permute-start | bytes 221192 | tf_op jit(solution)/shard_map/ppermute | solution.py:555
  53.1 5.9 %collective-permute-start.23 = (f32[96,256]{1,0:T(8,128)S(1)}, f32[96,256]{1,0:T(8,128)S(1)}, u32[]{:S(2)}, u32[]{:S(2)}) collective-permute-start(f32[96,256]{1,0:T(8,128)S(1)} %add.70), channel_id=1, source_target_pairs={{0,4},{1,5},{2,6},{3,7},{4,0},{5,1},{6,2},{7,3},{8,10},{9,11},{10,... | collective-permute-start | bytes 294920 | tf_op jit(solution)/shard_map/ppermute | solution.py:555
  57.0 5.6 %collective-permute-start.13 = (f32[72,256]{1,0:T(8,128)S(1)}, f32[72,256]{1,0:T(8,128)S(1)}, u32[]{:S(2)}, u32[]{:S(2)}) collective-permute-start(f32[72,256]{1,0:T(8,128)S(1)} %add_add_fusion.2), channel_id=1, source_target_pairs={{0,2},{1,3},{2,0},{3,1},{4,6},{5,7},{6,4},{7,5},{8,12},{9,13},{10,... | collective-permute-start | bytes 221192 | tf_op jit(solution)/shard_map/ppermute | solution.py:555
  59.0 11.3 %collective-permute-start.26 = (f32[96,256]{1,0:T(8,128)S(1)}, f32[96,256]{1,0:T(8,128)S(1)}, u32[]{:S(2)}, u32[]{:S(2)}) collective-permute-start(f32[96,256]{1,0:T(8,128)S(1)} %add.71), channel_id=1, source_target_pairs={{0,17},{1,16},{2,19},{3,18},{4,21},{5,20},{6,23},{7,22},{8,25},{9,... | collective-permute-start | bytes 294920 | tf_op jit(solution)/shard_map/ppermute | solution.py:555
  60.7 10.8 %collective-permute-start.25 = (f32[96,256]{1,0:T(8,128)S(1)}, f32[96,256]{1,0:T(8,128)S(1)}, u32[]{:S(2)}, u32[]{:S(2)}) collective-permute-start(f32[96,256]{1,0:T(8,128)S(1)} %add.71), channel_id=1, source_target_pairs={{0,1},{1,0},{2,3},{3,2},{4,5},{5,4},{6,7},{7,6},{8,9},{9,8},{10,11... | collective-permute-start | bytes 294920 | tf_op jit(solution)/shard_map/ppermute | solution.py:555
  61.4 10.2 %collective-permute-start.24 = (f32[96,256]{1,0:T(8,128)S(1)}, f32[96,256]{1,0:T(8,128)S(1)}, u32[]{:S(2)}, u32[]{:S(2)}) collective-permute-start(f32[96,256]{1,0:T(8,128)S(1)} %add.71), channel_id=1, source_target_pairs={{0,16},{1,17},{2,18},{3,19},{4,20},{5,21},{6,22},{7,23},{8,24},{9,... | collective-permute-start | bytes 294920 | tf_op jit(solution)/shard_map/ppermute | solution.py:555
  62.6 5.3 %collective-permute-start.14 = (f32[72,256]{1,0:T(8,128)S(1)}, f32[72,256]{1,0:T(8,128)S(1)}, u32[]{:S(2)}, u32[]{:S(2)}) collective-permute-start(f32[72,256]{1,0:T(8,128)S(1)} %add.65), channel_id=1, source_target_pairs={{0,4},{1,5},{2,6},{3,7},{4,0},{5,1},{6,2},{7,3},{8,10},{9,11},{10,... | collective-permute-start | bytes 221192 | tf_op jit(solution)/shard_map/ppermute | solution.py:555
  68.0 5.3 %collective-permute-start.17 = (f32[72,256]{1,0:T(8,128)S(1)}, f32[72,256]{1,0:T(8,128)S(1)}, u32[]{:S(2)}, u32[]{:S(2)}) collective-permute-start(f32[72,256]{1,0:T(8,128)S(1)} %add.66), channel_id=1, source_target_pairs={{0,17},{1,16},{2,19},{3,18},{4,21},{5,20},{6,23},{7,22},{8,25},{9,... | collective-permute-start | bytes 221192 | tf_op jit(solution)/shard_map/ppermute | solution.py:555
  70.3 4.4 %collective-permute-start.15 = (f32[72,256]{1,0:T(8,128)S(1)}, f32[72,256]{1,0:T(8,128)S(1)}, u32[]{:S(2)}, u32[]{:S(2)}) collective-permute-start(f32[72,256]{1,0:T(8,128)S(1)} %add.66), channel_id=1, source_target_pairs={{0,16},{1,17},{2,18},{3,19},{4,20},{5,21},{6,22},{7,23},{8,24},{9,... | collective-permute-start | bytes 221192 | tf_op jit(solution)/shard_map/ppermute | solution.py:555
  (16 other events, 183.2 us)

commit v5 on v4

--- a/solution.py
+++ b/solution.py
@@ -14,6 +14,7 @@
 EPS = 1e-05
 EARLY = 0
 LATE = 0
+SIDE = 4
 GELU_A = math.sqrt(2.0 / math.pi)
 GELU_B = 0.044715
 SMALL = 16 * 1024 * 1024
@@ -31,7 +32,7 @@
             a, b, (((left_dim,), (right_dim,)), ((), ())), preferred_element_type=F32
         )
 
-    if left[0].shape[left_dim] % 128 == 0:
+    if left[0].shape[left_dim] % 128 == 0 or left_dim == right_dim == 0:
         return one(
             jnp.concatenate([left[0], left[0], left[1]], axis=left_dim),
             jnp.concatenate([right[0], right[1], right[0]], axis=right_dim),
@@ -123,6 +124,7 @@
     )
     x_t, rstd_rows, temper_rows = views(wide_packed, width, 8, temper.shape[0])
     copies = fetch(sources, targets, sems)
+    sums[sums.shape[0] - 8 :] = jnp.zeros((8, 128), F32)
     head_size, slices = logit_weight.shape
     heads = temper.shape[0]
     points = x.shape[1]
@@ -148,7 +150,7 @@
     wide = jnp.concatenate([logit_weight[...]] * GROUP, axis=1)
     logit_blocks = split(spread_blocks(wide, mask))
     ones = jnp.ones((16, points), BF16)
-    nums, dens = [], []
+    blocks = total // 128
     for g in range(heads // GROUP):
         rows = GROUP * head_size
         logits = product(logit_blocks, rows_of(assign, g * rows, rows), 0, 0)
@@ -165,13 +167,16 @@
         span = slice(g * GROUP * slices, (g + 1) * GROUP * slices)
         weight_h[span], weight_l[span] = weights
         num = product(rows_of(fx, g * rows, rows), weights, 1, 1)
-        nums.append(fold_blocks(num, mask, head_size))
+        num = fold_blocks(num, mask, head_size)
         nt = (((1,), (1,)), ((), ()))
         den = lax.dot_general(ones, weights[0], nt, preferred_element_type=F32)
         den = den + lax.dot_general(ones, weights[1], nt, preferred_element_type=F32)
-        dens.append(den[:8])
-    sums[0:head_size] = jnp.concatenate(nums, axis=1)
-    sums[head_size : head_size + 8] = jnp.concatenate(dens, axis=1)
+        for i in range(num.shape[1] // 128):
+            j = g * (num.shape[1] // 128) + i
+            lanes = slice(i * 128, (i + 1) * 128)
+            sums[j * head_size : (j + 1) * head_size] = num[:, lanes]
+            row = blocks * head_size + j
+            sums[row : row + 1] = den[0:1, lanes]
 
 
 def map_views(packed, width, head_size, slices):
@@ -211,7 +216,7 @@
 
 def back_views(packed, wide_packed, width, head_size, slices):
     return views(packed, *[width] * 12) + views(
-        wide_packed, width, 5 * head_size, 2 * slices, 8
+        wide_packed, width, 5 * head_size, SIDE * slices, 8
     )
 
 
@@ -222,7 +227,7 @@
 ):
     total = front.shape[1]
     heads = total // slices
-    width = (wide_packed.shape[0] - 8) - 5 * head_size - 2 * slices
+    width = (wide_packed.shape[0] - 8) - 5 * head_size - SIDE * slices
     weight_h, weight_l = views(front, total, total)
     x_t = front_wide.at[0:width]
     cot_t, hidden_grad = views(columns_packed, width, width)
@@ -235,17 +240,20 @@
         packed, wide_packed, width, head_size, slices
     )
     rows, lanes = GROUP * head_size, GROUP * slices
-    denom = sums[head_size : head_size + 1] + EPS
+    blocks = total // 128
+    ends = [blocks * head_size + j for j in range(blocks)]
+    denom = jnp.concatenate([sums[end : end + 1] for end in ends], axis=1) + EPS
+    nums = [sums[j * head_size : (j + 1) * head_size] for j in range(blocks)]
     denom_rows[...] = jnp.broadcast_to(denom, (8, total))
-    tokens = sums[0:head_size] / denom
+    tokens = jnp.concatenate(nums, axis=1) / denom
     qkv = product((maps_h[...], maps_l[...]), split(tokens), 1, 0)
     qkv_pair = split(qkv)
-    wide = 2 * slices
+    wide = SIDE * slices
     same = (lax.broadcasted_iota(jnp.int32, (wide, wide), 0) // slices) == (
         lax.broadcasted_iota(jnp.int32, (wide, wide), 1) // slices
     )
     results = []
-    for pair in range(heads // 2):
+    for pair in range(heads // SIDE):
         span = slice(pair * wide, (pair + 1) * wide)
         q = tuple(a[0:head_size, span] for a in qkv_pair)
         k = tuple(a[head_size : 2 * head_size, span] for a in qkv_pair)
@@ -392,9 +400,9 @@
     qkv_pair = split(middle[head_size : 4 * head_size])
     result = middle[4 * head_size : 5 * head_size]
     result_grad = split(out_sum[...])
-    wide = 2 * slices
+    wide = SIDE * slices
     parts = []
-    for pair in range(heads // 2):
+    for pair in range(heads // SIDE):
         span = slice(pair * wide, (pair + 1) * wide)
         q = tuple(a[0:head_size, span] for a in qkv_pair)
         k = tuple(a[head_size : 2 * head_size, span] for a in qkv_pair)
@@ -499,26 +507,29 @@
 def late_out_kernel(
     levels,
     own, partner, gain, fx_weight, x_weight, gain_row, given,
-    matrices, maps, logit, gains,
-    late, scaled, sems,
+    matrices, maps_out, logit_out, gains_out,
+    late, scaled, maps, logit, gains, sems,
 ):
     arrange(levels, own, partner, late)
     width = gain.shape[1]
     head_size, slices = logit.shape
-    gain_column = column(gain[...])
-    copies = []
-    total = jnp.zeros((1, width), F32)
-    for i, weight in enumerate((fx_weight, x_weight)):
-        grad = late[i * width : (i + 1) * width]
-        scaled[i] = grad * gain_column
-        copies.append(pltpu.make_async_copy(scaled.at[i], matrices.at[i], sems.at[i]))
-        copies[i].start()
-        total = total + row_total(grad, weight[...])
     base = 2 * width
     for i in range(3):
         maps[i] = late[base : base + head_size, i * head_size : (i + 1) * head_size]
     logit[...] = late[base : base + head_size, 128 : 128 + slices]
+    copies = fetch((maps, logit), (maps_out, logit_out), sems)
+    gain_column = column(gain[...])
+    total = jnp.zeros((1, width), F32)
+    for i, weight in enumerate((fx_weight, x_weight)):
+        scaled[i] = late[i * width : (i + 1) * width] * gain_column
+        copy = pltpu.make_async_copy(scaled.at[i], matrices.at[i], sems.at[2 + i])
+        copy.start()
+        copies.append(copy)
+    for i, weight in enumerate((fx_weight, x_weight)):
+        total = total + row_total(late[i * width : (i + 1) * width], weight[...])
     gains[...] = jnp.concatenate([total, gain_row[...]], axis=0)
+    copies.append(pltpu.make_async_copy(gains, gains_out, sems.at[4]))
+    copies[-1].start()
     for copy in copies:
         copy.wait()
 
@@ -700,7 +711,7 @@
     front, front_wide, sums = call(
         front_kernel, "front", [HBM] * 6, [VMEM] * 3,
         [shape(2 * total + 8 * width, points, dtype=BF16), shape(width + 8 + heads, points),
-         shape(head_size + 8, total)],
+         shape(total // 128 * head_size + 8, 128)],
         pinned,
         4 * dense,
         FRONT_LIMIT,
@@ -727,7 +738,7 @@
     out_sum, back, back_wide = call(
         functools.partial(back_kernel, head_size, slices), "back", [VMEM] * 5, [VMEM] * 3,
         [shape(head_size, total), shape(12 * width, points, dtype=BF16),
-         shape(width + 5 * head_size + 2 * slices + 8, points)],
+         shape(width + 5 * head_size + SIDE * slices + 8, points)],
         (sums, front, front_wide, columns, maps),
         6 * dense,
     )
@@ -739,8 +750,8 @@
     behind = [early_value]
     for step in all_steps(sizes, EARLY):
         behind.append(step(behind[-1]))
-    order = [0, 1]
-    for i, step in enumerate(point_steps(sizes)):
+    order = [None, 2]
+    for i, step in enumerate(reversed(point_steps(sizes))):
         out_sum = step(out_sum)
         if i < len(order) and order[i] is not None:
             out_sum, _ = tie(out_sum, behind[order[i]])
@@ -753,7 +764,7 @@
         8 * dense,
         scratch=[pltpu.VMEM((rows, width), F32)],
     )
-    late, _ = tie((mine, other), behind[1])
+    late, _ = tie((mine, other), behind[2])
     input_grad = call(
         rows_kernel, "rows", [VMEM] * 4, VMEM, shape(1, points, width),
         (front, front_wide, back_wide, end), 2 * dense,
@@ -773,13 +784,14 @@
     )
     matrices, map_grads, logit_grad, gains = call(
         functools.partial(late_out_kernel, tuple(axes[:LATE])), "late_out", [VMEM] * 6 + [HBM],
-        [HBM] + [VMEM] * 3,
+        [HBM] * 4,
         [shape(5, width, width), shape(3, head_size, head_size), shape(head_size, slices),
          shape(2, width)],
         (*late, gain_one, fx_weight, x_weight, gain_row, matrices),
         dense // 8,
         scratch=[pltpu.VMEM((rows, width), F32), pltpu.VMEM((2, width, width), F32),
-                 pltpu.SemaphoreType.DMA((2,))],
+                 pltpu.VMEM((3, head_size, head_size), F32), pltpu.VMEM((head_size, slices), F32),
+                 pltpu.VMEM((2, width), F32), pltpu.SemaphoreType.DMA((5,))],
         aliases={6: 0},
     )
     return input_grad, matrices, map_grads, logit_grad, gains

time: 78.2 us -> 74 us (0.946)
  waiting for transfers between devices: 23.5 us -> 19.5 us
  Pallas kernels: 18.1 us -> 17 us
  starting transfers between devices: 35.3 us -> 36.1 us
    ppermute x28, waiting for transfers between devices: 23.5 us -> 19.5 us  [swap(): return lax.ppermute(value, ('dp', 'point'), pairs)]
    pallas_call x10, Pallas kernels: 18.1 us -> 17 us  [call(): pl.pallas_call(body, name=name, in_specs=in_specs, out_specs=out_specs, o...]
  transfers between devices with their start and end apart: 28 -> 28, of which waited for: 13 -> 10; matrix products, arithmetic and copies ran while one was open for 0% -> 0% of each run, Pallas kernels for 9% -> 5%
where the time goes in v5:
time: 74 us; the launch traced here: 73.8 us
  starting transfers between devices  36.1 us (49%)
  waiting for transfers between devices  19.5 us (26%)
  Pallas kernels  17 us (23%)
  between operations  0.97 us (1%)
    ppermute x28, starting transfers between devices, swap(): return lax.ppermute(value, ('dp', 'point'), pairs)  36.1 us
    ppermute x28, waiting for transfers between devices, swap(): return lax.ppermute(value, ('dp', 'point'), pairs)  19.5 us
    pallas_call x10, Pallas kernels, call(): pl.pallas_call(body, name=name, in_specs=in_specs, out_specs=out_specs, o...  17 us
  transfers between devices with their start and end apart: 28, of which 10 were waited for; matrix products, arithmetic and copies ran while one was open for 0% of the time, Pallas kernels for 5%

profile of v5, /device:TPU:0, one launch (start us, length us, event | category | flops | bytes accessed | tf_op | source)
XLA Modules:
  0.0 73.8 jit_solution(1618588889366851975)
XLA Ops:
  0.7 4.0 %front.1 = (bf16[3072,512]{1,0:T(8,128)(2,1)S(1)}, f32[272,512]{1,0:T(8,128)S(1)}, f32[136,128]{1,0:T(8,128)S(1)}) custom-call(f32[1,512,256]{2,1,0:T(8,128)} %x_hbm.1, f32[1,256]{1,0:T(1,128)} %bitcast.4, f32[256,256]{1,0:T(8,128)} %fx_weight.1, f32[256,256]{1,0:T(8,128)} %x_weight.1, f32[32,64]{1,0:T(8,128)} %logit_weight.1, f32[8]{0:T(128)} %temper_hbm.1), custom_call_target="tpu_custom_call" | custom-call | flops 805306368 | bytes 1048576 | tf_op jit(solution)/shard_map/front/pallas_call | solution.py:546
  4.8 3.0 %collective-permute-start = (f32[136,128]{1,0:T(8,128)S(1)}, f32[136,128]{1,0:T(8,128)S(1)}, u32[]{:S(2)}, u32[]{:S(2)}) collective-permute-start(f32[136,128]{1,0:T(8,128)S(1)} %get-tuple-element.47), channel_id=1, source_target_pairs={{0,1},{1,0},{2,3},{3,2},{4,5},{5,4},{6,7},{7,6},{8,9},{9,8},{10,11... | collective-permute-start | bytes 208904 | tf_op jit(solution)/shard_map/ppermute | solution.py:566
  7.8 2.3 %collective-permute-done = f32[136,128]{1,0:T(8,128)S(1)} collective-permute-done((f32[136,128]{1,0:T(8,128)S(1)}, f32[136,128]{1,0:T(8,128)S(1)}, u32[]{:S(2)}, u32[]{:S(2)}) %collective-permute-start) | collective-permute-done | bytes 69664 | tf_op jit(solution)/shard_map/ppermute | solution.py:566
  10.1 4.2 %collective-permute-start.3 = (f32[136,128]{1,0:T(8,128)S(1)}, f32[136,128]{1,0:T(8,128)S(1)}, u32[]{:S(2)}, u32[]{:S(2)}) collective-permute-start(f32[136,128]{1,0:T(8,128)S(1)} %add.54), channel_id=1, source_target_pairs={{0,6},{1,7},{2,4},{3,5},{4,2},{5,3},{6,0},{7,1},{8,14},{9,15},{10,... | collective-permute-start | bytes 208904 | tf_op jit(solution)/shard_map/ppermute | solution.py:566
  16.8 2.9 %collective-permute-done.2 = f32[136,128]{1,0:T(8,128)S(1)} collective-permute-done((f32[136,128]{1,0:T(8,128)S(1)}, f32[136,128]{1,0:T(8,128)S(1)}, u32[]{:S(2)}, u32[]{:S(2)}) %collective-permute-start.2) | collective-permute-done | bytes 69664 | tf_op jit(solution)/shard_map/ppermute | solution.py:566
  19.7 3.8 %back.1 = (f32[32,512]{1,0:T(8,128)S(1)}, bf16[3072,512]{1,0:T(8,128)(2,1)S(1)}, f32[680,512]{1,0:T(8,128)S(1)}) custom-call(f32[136,128]{1,0:T(8,128)S(1)} %add_add_fusion.2.sums, bf16[3072,512]{1,0:T(8,128)(2,1)S(1)} %get-tuple-element.48.front, f32[272,512]{1,0:T(8,128)S(1)} %get-tuple-element.49.front_wide, ...), custom_call_target="tpu_custom_call" | custom-call | flops 1207959552 | bytes 1048576 | tf_op jit(solution)/shard_map/back/pallas_call | solution.py:546
  24.4 2.2 %collective-permute-start.6 = (f32[32,512]{1,0:T(8,128)S(1)}, f32[32,512]{1,0:T(8,128)S(1)}, u32[]{:S(2)}, u32[]{:S(2)}) collective-permute-start(f32[32,512]{1,0:T(8,128)S(1)} %get-tuple-element.57), channel_id=1, source_target_pairs={{0,6},{1,7},{2,4},{3,5},{4,2},{5,3},{6,0},{7,1},{8,14},{9,15},{10,... | collective-permute-start | bytes 196616 | tf_op jit(solution)/shard_map/ppermute | solution.py:566
  26.7 2.2 %collective-permute-start.4 = (f32[32,512]{1,0:T(8,128)S(1)}, f32[32,512]{1,0:T(8,128)S(1)}, u32[]{:S(2)}, u32[]{:S(2)}) collective-permute-start(f32[32,512]{1,0:T(8,128)S(1)} %get-tuple-element.57), channel_id=1, source_target_pairs={{0,2},{1,3},{2,0},{3,1},{4,6},{5,7},{6,4},{7,5},{8,10},{9,11},{10,... | collective-permute-start | bytes 196616 | tf_op jit(solution)/shard_map/ppermute | solution.py:566
  28.9 1.6 %collective-permute-start.9 = (f32[96,256]{1,0:T(8,128)S(1)}, f32[96,256]{1,0:T(8,128)S(1)}, u32[]{:S(2)}, u32[]{:S(2)}) collective-permute-start(f32[96,256]{1,0:T(8,128)S(1)} %get-tuple-element.62), channel_id=1, source_target_pairs={{0,16},{1,17},{2,18},{3,19},{4,20},{5,21},{6,22},{7,23},{8,24},{9,... | collective-permute-start | bytes 294920 | tf_op jit(solution)/shard_map/ppermute | solution.py:566
  30.5 1.5 %collective-permute-start.10 = (f32[96,256]{1,0:T(8,128)S(1)}, f32[96,256]{1,0:T(8,128)S(1)}, u32[]{:S(2)}, u32[]{:S(2)}) collective-permute-start(f32[96,256]{1,0:T(8,128)S(1)} %get-tuple-element.63), channel_id=1, source_target_pairs={{0,1},{1,0},{2,3},{3,2},{4,5},{5,4},{6,7},{7,6},{8,9},{9,8},{10,11... | collective-permute-start | bytes 294920 | tf_op jit(solution)/shard_map/ppermute | solution.py:566
  32.0 1.7 %collective-permute-start.11 = (f32[96,256]{1,0:T(8,128)S(1)}, f32[96,256]{1,0:T(8,128)S(1)}, u32[]{:S(2)}, u32[]{:S(2)}) collective-permute-start(f32[96,256]{1,0:T(8,128)S(1)} %get-tuple-element.64), channel_id=1, source_target_pairs={{0,17},{1,16},{2,19},{3,18},{4,21},{5,20},{6,23},{7,22},{8,25},{9,... | collective-permute-start | bytes 294920 | tf_op jit(solution)/shard_map/ppermute | solution.py:566
  35.1 3.4 %collective-permute-done.7 = f32[32,512]{1,0:T(8,128)S(1)} collective-permute-done((f32[32,512]{1,0:T(8,128)S(1)}, f32[32,512]{1,0:T(8,128)S(1)}, u32[]{:S(2)}, u32[]{:S(2)}) %collective-permute-start.7) | collective-permute-done | bytes 65568 | tf_op jit(solution)/shard_map/ppermute | solution.py:566
  38.6 3.9 %end.1 = (f32[288,256]{1,0:T(8,128)S(1)}, f32[288,256]{1,0:T(8,128)S(1)}, bf16[1024,512]{1,0:T(8,128)(2,1)S(1)}) custom-call(f32[32,512]{1,0:T(8,128)S(1)} %add.61.out_sum, bf16[3072,512]{1,0:T(8,128)(2,1)S(1)} %get-tuple-element.48.front, f32[272,512]{1,0:T(8,128)S(1)} %get-tuple-element.49.front_wide, bf16[2560,256]{1,0:T(8,128)(2,1)S(1)} %get-tuple-element.56.map_packed, ...), custom_call_target="tpu_custom_call" | custom-call | flops 1610612736 | bytes 1048576 | tf_op jit(solution)/shard_map/end/pallas_call | solution.py:546
  42.6 1.6 %rows.1 = f32[1,512,256]{2,1,0:T(8,128)} custom-call(bf16[3072,512]{1,0:T(8,128)(2,1)S(1)} %get-tuple-element.48.front, f32[272,512]{1,0:T(8,128)S(1)} %get-tuple-element.49.front_wide, f32[680,512]{1,0:T(8,128)S(1)} %get-tuple-element.66.back_wide, bf16[1024,512]{1,0:T(8,128)(2,1)S(1)} %get-tuple-element.75.end), custom_call_target="tpu_custom_call" | custom-call | flops 402653184 | bytes 1048576 | tf_op jit(solution)/shard_map/rows/pallas_call | solution.py:546
  44.3 1.4 %collective-permute-start.13 = (f32[72,256]{1,0:T(8,128)S(1)}, f32[72,256]{1,0:T(8,128)S(1)}, u32[]{:S(2)}, u32[]{:S(2)}) collective-permute-start(f32[72,256]{1,0:T(8,128)S(1)} %get-tuple-element.78), channel_id=1, source_target_pairs={{0,16},{1,17},{2,18},{3,19},{4,20},{5,21},{6,22},{7,23},{8,24},{9,... | collective-permute-start | bytes 221192 | tf_op jit(solution)/shard_map/ppermute | solution.py:566
  45.7 1.5 %collective-permute-start.14 = (f32[72,256]{1,0:T(8,128)S(1)}, f32[72,256]{1,0:T(8,128)S(1)}, u32[]{:S(2)}, u32[]{:S(2)}) collective-permute-start(f32[72,256]{1,0:T(8,128)S(1)} %get-tuple-element.79), channel_id=1, source_target_pairs={{0,1},{1,0},{2,3},{3,2},{4,5},{5,4},{6,7},{7,6},{8,9},{9,8},{10,11... | collective-permute-start | bytes 221192 | tf_op jit(solution)/shard_map/ppermute | solution.py:566
  47.9 2.8 %collective-permute-start.23 = (f32[96,256]{1,0:T(8,128)S(1)}, f32[96,256]{1,0:T(8,128)S(1)}, u32[]{:S(2)}, u32[]{:S(2)}) collective-permute-start(f32[96,256]{1,0:T(8,128)S(1)} %add.70), channel_id=1, source_target_pairs={{0,4},{1,5},{2,6},{3,7},{4,0},{5,1},{6,2},{7,3},{8,10},{9,11},{10,... | collective-permute-start | bytes 294920 | tf_op jit(solution)/shard_map/ppermute | solution.py:566
  50.7 1.9 %collective-permute-done.15 = f32[72,256]{1,0:T(8,128)S(1)} collective-permute-done((f32[72,256]{1,0:T(8,128)S(1)}, f32[72,256]{1,0:T(8,128)S(1)}, u32[]{:S(2)}, u32[]{:S(2)}) %collective-permute-start.15) | collective-permute-done | bytes 73760 | tf_op jit(solution)/shard_map/ppermute | solution.py:566
  52.6 1.9 %collective-permute-start.16 = (f32[72,256]{1,0:T(8,128)S(1)}, f32[72,256]{1,0:T(8,128)S(1)}, u32[]{:S(2)}, u32[]{:S(2)}) collective-permute-start(f32[72,256]{1,0:T(8,128)S(1)} %add_add_fusion.1), channel_id=1, source_target_pairs={{0,2},{1,3},{2,0},{3,1},{4,6},{5,7},{6,4},{7,5},{8,12},{9,13},{10,... | collective-permute-start | bytes 221192 | tf_op jit(solution)/shard_map/ppermute | solution.py:566
  54.5 1.9 %collective-permute-start.26 = (f32[96,256]{1,0:T(8,128)S(1)}, f32[96,256]{1,0:T(8,128)S(1)}, u32[]{:S(2)}, u32[]{:S(2)}) collective-permute-start(f32[96,256]{1,0:T(8,128)S(1)} %add.71), channel_id=1, source_target_pairs={{0,17},{1,16},{2,19},{3,18},{4,21},{5,20},{6,23},{7,22},{8,25},{9,... | collective-permute-start | bytes 294920 | tf_op jit(solution)/shard_map/ppermute | solution.py:566
  58.1 1.9 %collective-permute-start.17 = (f32[72,256]{1,0:T(8,128)S(1)}, f32[72,256]{1,0:T(8,128)S(1)}, u32[]{:S(2)}, u32[]{:S(2)}) collective-permute-start(f32[72,256]{1,0:T(8,128)S(1)} %add.68), channel_id=1, source_target_pairs={{0,4},{1,5},{2,6},{3,7},{4,0},{5,1},{6,2},{7,3},{8,10},{9,11},{10,... | collective-permute-start | bytes 221192 | tf_op jit(solution)/shard_map/ppermute | solution.py:566
  60.0 4.2 %collective-permute-done.17 = f32[72,256]{1,0:T(8,128)S(1)} collective-permute-done((f32[72,256]{1,0:T(8,128)S(1)}, f32[72,256]{1,0:T(8,128)S(1)}, u32[]{:S(2)}, u32[]{:S(2)}) %collective-permute-start.17) | collective-permute-done | bytes 73760 | tf_op jit(solution)/shard_map/ppermute | solution.py:566
  64.2 1.9 %collective-permute-start.20 = (f32[72,256]{1,0:T(8,128)S(1)}, f32[72,256]{1,0:T(8,128)S(1)}, u32[]{:S(2)}, u32[]{:S(2)}) collective-permute-start(f32[72,256]{1,0:T(8,128)S(1)} %add.69), channel_id=1, source_target_pairs={{0,17},{1,16},{2,19},{3,18},{4,21},{5,20},{6,23},{7,22},{8,25},{9,... | collective-permute-start | bytes 221192 | tf_op jit(solution)/shard_map/ppermute | solution.py:566
  67.9 1.6 %collective-permute-done.20 = f32[72,256]{1,0:T(8,128)S(1)} collective-permute-done((f32[72,256]{1,0:T(8,128)S(1)}, f32[72,256]{1,0:T(8,128)S(1)}, u32[]{:S(2)}, u32[]{:S(2)}) %collective-permute-start.20) | collective-permute-done | bytes 73760 | tf_op jit(solution)/shard_map/ppermute | solution.py:566
  (78 shorter events, 13.5 us)
Async XLA Ops:
  4.8 5.3 %collective-permute-start = (f32[136,128]{1,0:T(8,128)S(1)}, f32[136,128]{1,0:T(8,128)S(1)}, u32[]{:S(2)}, u32[]{:S(2)}) collective-permute-start(f32[136,128]{1,0:T(8,128)S(1)} %get-tuple-element.47), channel_id=1, source_target_pairs={{0,1},{1,0},{2,3},{3,2},{4,5},{5,4},{6,7},{7,6},{8,9},{9,8},{10,11... | collective-permute-start | bytes 208904 | tf_op jit(solution)/shard_map/ppermute | solution.py:566
  10.1 6.7 %collective-permute-start.3 = (f32[136,128]{1,0:T(8,128)S(1)}, f32[136,128]{1,0:T(8,128)S(1)}, u32[]{:S(2)}, u32[]{:S(2)}) collective-permute-start(f32[136,128]{1,0:T(8,128)S(1)} %add.54), channel_id=1, source_target_pairs={{0,6},{1,7},{2,4},{3,5},{4,2},{5,3},{6,0},{7,1},{8,14},{9,15},{10,... | collective-permute-start | bytes 208904 | tf_op jit(solution)/shard_map/ppermute | solution.py:566
  14.3 5.4 %collective-permute-start.2 = (f32[136,128]{1,0:T(8,128)S(1)}, f32[136,128]{1,0:T(8,128)S(1)}, u32[]{:S(2)}, u32[]{:S(2)}) collective-permute-start(f32[136,128]{1,0:T(8,128)S(1)} %add.54), channel_id=1, source_target_pairs={{0,4},{1,5},{2,6},{3,7},{4,0},{5,1},{6,2},{7,3},{8,12},{9,13},{10,... | collective-permute-start | bytes 208904 | tf_op jit(solution)/shard_map/ppermute | solution.py:566
  14.3 5.4 %collective-permute-start.1 = (f32[136,128]{1,0:T(8,128)S(1)}, f32[136,128]{1,0:T(8,128)S(1)}, u32[]{:S(2)}, u32[]{:S(2)}) collective-permute-start(f32[136,128]{1,0:T(8,128)S(1)} %add.54), channel_id=1, source_target_pairs={{0,2},{1,3},{2,0},{3,1},{4,6},{5,7},{6,4},{7,5},{8,10},{9,11},{10,... | collective-permute-start | bytes 208904 | tf_op jit(solution)/shard_map/ppermute | solution.py:566
  24.4 4.5 %collective-permute-start.8 = (f32[384,256]{1,0:T(8,128)S(1)}, f32[384,256]{1,0:T(8,128)S(1)}, u32[]{:S(2)}, u32[]{:S(2)}) collective-permute-start(f32[384,256]{1,0:T(8,128)S(1)} %get-tuple-element.60), channel_id=1, source_target_pairs={{0,8},{1,9},{2,10},{3,11},{4,12},{5,13},{6,14},{7,15},{8,0},{9,1},... | collective-permute-start | bytes 1179656 | tf_op jit(solution)/shard_map/ppermute | solution.py:566
  24.4 7.6 %collective-permute-start.6 = (f32[32,512]{1,0:T(8,128)S(1)}, f32[32,512]{1,0:T(8,128)S(1)}, u32[]{:S(2)}, u32[]{:S(2)}) collective-permute-start(f32[32,512]{1,0:T(8,128)S(1)} %get-tuple-element.57), channel_id=1, source_target_pairs={{0,6},{1,7},{2,4},{3,5},{4,2},{5,3},{6,0},{7,1},{8,14},{9,15},{10,... | collective-permute-start | bytes 196616 | tf_op jit(solution)/shard_map/ppermute | solution.py:566
  26.7 7.1 %collective-permute-start.5 = (f32[32,512]{1,0:T(8,128)S(1)}, f32[32,512]{1,0:T(8,128)S(1)}, u32[]{:S(2)}, u32[]{:S(2)}) collective-permute-start(f32[32,512]{1,0:T(8,128)S(1)} %get-tuple-element.57), channel_id=1, source_target_pairs={{0,4},{1,5},{2,6},{3,7},{4,0},{5,1},{6,2},{7,3},{8,12},{9,13},{10,... | collective-permute-start | bytes 196616 | tf_op jit(solution)/shard_map/ppermute | solution.py:566
  26.7 7.1 %collective-permute-start.4 = (f32[32,512]{1,0:T(8,128)S(1)}, f32[32,512]{1,0:T(8,128)S(1)}, u32[]{:S(2)}, u32[]{:S(2)}) collective-permute-start(f32[32,512]{1,0:T(8,128)S(1)} %get-tuple-element.57), channel_id=1, source_target_pairs={{0,2},{1,3},{2,0},{3,1},{4,6},{5,7},{6,4},{7,5},{8,10},{9,11},{10,... | collective-permute-start | bytes 196616 | tf_op jit(solution)/shard_map/ppermute | solution.py:566
  28.9 9.6 %collective-permute-start.9 = (f32[96,256]{1,0:T(8,128)S(1)}, f32[96,256]{1,0:T(8,128)S(1)}, u32[]{:S(2)}, u32[]{:S(2)}) collective-permute-start(f32[96,256]{1,0:T(8,128)S(1)} %get-tuple-element.62), channel_id=1, source_target_pairs={{0,16},{1,17},{2,18},{3,19},{4,20},{5,21},{6,22},{7,23},{8,24},{9,... | collective-permute-start | bytes 294920 | tf_op jit(solution)/shard_map/ppermute | solution.py:566
  30.5 8.0 %collective-permute-start.10 = (f32[96,256]{1,0:T(8,128)S(1)}, f32[96,256]{1,0:T(8,128)S(1)}, u32[]{:S(2)}, u32[]{:S(2)}) collective-permute-start(f32[96,256]{1,0:T(8,128)S(1)} %get-tuple-element.63), channel_id=1, source_target_pairs={{0,1},{1,0},{2,3},{3,2},{4,5},{5,4},{6,7},{7,6},{8,9},{9,8},{10,11... | collective-permute-start | bytes 294920 | tf_op jit(solution)/shard_map/ppermute | solution.py:566
  32.0 6.5 %collective-permute-start.11 = (f32[96,256]{1,0:T(8,128)S(1)}, f32[96,256]{1,0:T(8,128)S(1)}, u32[]{:S(2)}, u32[]{:S(2)}) collective-permute-start(f32[96,256]{1,0:T(8,128)S(1)} %get-tuple-element.64), channel_id=1, source_target_pairs={{0,17},{1,16},{2,19},{3,18},{4,21},{5,20},{6,23},{7,22},{8,25},{9,... | collective-permute-start | bytes 294920 | tf_op jit(solution)/shard_map/ppermute | solution.py:566
  33.8 4.8 %collective-permute-start.7 = (f32[32,512]{1,0:T(8,128)S(1)}, f32[32,512]{1,0:T(8,128)S(1)}, u32[]{:S(2)}, u32[]{:S(2)}) collective-permute-start(f32[32,512]{1,0:T(8,128)S(1)} %add_add_fusion.3), channel_id=1, source_target_pairs={{0,1},{1,0},{2,3},{3,2},{4,5},{5,4},{6,7},{7,6},{8,9},{9,8},{10,11... | collective-permute-start | bytes 196616 | tf_op jit(solution)/shard_map/ppermute | solution.py:566
  42.6 5.3 %collective-permute-start.22 = (f32[96,256]{1,0:T(8,128)S(1)}, f32[96,256]{1,0:T(8,128)S(1)}, u32[]{:S(2)}, u32[]{:S(2)}) collective-permute-start(f32[96,256]{1,0:T(8,128)S(1)} %add_add_fusion), channel_id=1, source_target_pairs={{0,2},{1,3},{2,0},{3,1},{4,6},{5,7},{6,4},{7,5},{8,12},{9,13},{10,... | collective-permute-start | bytes 294920 | tf_op jit(solution)/shard_map/ppermute | solution.py:566
  44.3 6.4 %collective-permute-start.13 = (f32[72,256]{1,0:T(8,128)S(1)}, f32[72,256]{1,0:T(8,128)S(1)}, u32[]{:S(2)}, u32[]{:S(2)}) collective-permute-start(f32[72,256]{1,0:T(8,128)S(1)} %get-tuple-element.78), channel_id=1, source_target_pairs={{0,16},{1,17},{2,18},{3,19},{4,20},{5,21},{6,22},{7,23},{8,24},{9,... | collective-permute-start | bytes 221192 | tf_op jit(solution)/shard_map/ppermute | solution.py:566
  45.7 5.0 %collective-permute-start.14 = (f32[72,256]{1,0:T(8,128)S(1)}, f32[72,256]{1,0:T(8,128)S(1)}, u32[]{:S(2)}, u32[]{:S(2)}) collective-permute-start(f32[72,256]{1,0:T(8,128)S(1)} %get-tuple-element.79), channel_id=1, source_target_pairs={{0,1},{1,0},{2,3},{3,2},{4,5},{5,4},{6,7},{7,6},{8,9},{9,8},{10,11... | collective-permute-start | bytes 221192 | tf_op jit(solution)/shard_map/ppermute | solution.py:566
  47.2 5.4 %collective-permute-start.15 = (f32[72,256]{1,0:T(8,128)S(1)}, f32[72,256]{1,0:T(8,128)S(1)}, u32[]{:S(2)}, u32[]{:S(2)}) collective-permute-start(f32[72,256]{1,0:T(8,128)S(1)} %get-tuple-element.80), channel_id=1, source_target_pairs={{0,17},{1,16},{2,19},{3,18},{4,21},{5,20},{6,23},{7,22},{8,25},{9,... | collective-permute-start | bytes 221192 | tf_op jit(solution)/shard_map/ppermute | solution.py:566
  47.9 6.6 %collective-permute-start.23 = (f32[96,256]{1,0:T(8,128)S(1)}, f32[96,256]{1,0:T(8,128)S(1)}, u32[]{:S(2)}, u32[]{:S(2)}) collective-permute-start(f32[96,256]{1,0:T(8,128)S(1)} %add.70), channel_id=1, source_target_pairs={{0,4},{1,5},{2,6},{3,7},{4,0},{5,1},{6,2},{7,3},{8,10},{9,11},{10,... | collective-permute-start | bytes 294920 | tf_op jit(solution)/shard_map/ppermute | solution.py:566
  52.6 5.5 %collective-permute-start.16 = (f32[72,256]{1,0:T(8,128)S(1)}, f32[72,256]{1,0:T(8,128)S(1)}, u32[]{:S(2)}, u32[]{:S(2)}) collective-permute-start(f32[72,256]{1,0:T(8,128)S(1)} %add_add_fusion.1), channel_id=1, source_target_pairs={{0,2},{1,3},{2,0},{3,1},{4,6},{5,7},{6,4},{7,5},{8,12},{9,13},{10,... | collective-permute-start | bytes 221192 | tf_op jit(solution)/shard_map/ppermute | solution.py:566
  54.5 12.2 %collective-permute-start.26 = (f32[96,256]{1,0:T(8,128)S(1)}, f32[96,256]{1,0:T(8,128)S(1)}, u32[]{:S(2)}, u32[]{:S(2)}) collective-permute-start(f32[96,256]{1,0:T(8,128)S(1)} %add.71), channel_id=1, source_target_pairs={{0,17},{1,16},{2,19},{3,18},{4,21},{5,20},{6,23},{7,22},{8,25},{9,... | collective-permute-start | bytes 294920 | tf_op jit(solution)/shard_map/ppermute | solution.py:566
  56.4 11.3 %collective-permute-start.25 = (f32[96,256]{1,0:T(8,128)S(1)}, f32[96,256]{1,0:T(8,128)S(1)}, u32[]{:S(2)}, u32[]{:S(2)}) collective-permute-start(f32[96,256]{1,0:T(8,128)S(1)} %add.71), channel_id=1, source_target_pairs={{0,1},{1,0},{2,3},{3,2},{4,5},{5,4},{6,7},{7,6},{8,9},{9,8},{10,11... | collective-permute-start | bytes 294920 | tf_op jit(solution)/shard_map/ppermute | solution.py:566
  57.0 10.8 %collective-permute-start.24 = (f32[96,256]{1,0:T(8,128)S(1)}, f32[96,256]{1,0:T(8,128)S(1)}, u32[]{:S(2)}, u32[]{:S(2)}) collective-permute-start(f32[96,256]{1,0:T(8,128)S(1)} %add.71), channel_id=1, source_target_pairs={{0,16},{1,17},{2,18},{3,19},{4,20},{5,21},{6,22},{7,23},{8,24},{9,... | collective-permute-start | bytes 294920 | tf_op jit(solution)/shard_map/ppermute | solution.py:566
  58.1 6.1 %collective-permute-start.17 = (f32[72,256]{1,0:T(8,128)S(1)}, f32[72,256]{1,0:T(8,128)S(1)}, u32[]{:S(2)}, u32[]{:S(2)}) collective-permute-start(f32[72,256]{1,0:T(8,128)S(1)} %add.68), channel_id=1, source_target_pairs={{0,4},{1,5},{2,6},{3,7},{4,0},{5,1},{6,2},{7,3},{8,10},{9,11},{10,... | collective-permute-start | bytes 221192 | tf_op jit(solution)/shard_map/ppermute | solution.py:566
  64.2 5.3 %collective-permute-start.20 = (f32[72,256]{1,0:T(8,128)S(1)}, f32[72,256]{1,0:T(8,128)S(1)}, u32[]{:S(2)}, u32[]{:S(2)}) collective-permute-start(f32[72,256]{1,0:T(8,128)S(1)} %add.69), channel_id=1, source_target_pairs={{0,17},{1,16},{2,19},{3,18},{4,21},{5,20},{6,23},{7,22},{8,25},{9,... | collective-permute-start | bytes 221192 | tf_op jit(solution)/shard_map/ppermute | solution.py:566
  66.7 4.4 %collective-permute-start.18 = (f32[72,256]{1,0:T(8,128)S(1)}, f32[72,256]{1,0:T(8,128)S(1)}, u32[]{:S(2)}, u32[]{:S(2)}) collective-permute-start(f32[72,256]{1,0:T(8,128)S(1)} %add.69), channel_id=1, source_target_pairs={{0,16},{1,17},{2,18},{3,19},{4,20},{5,21},{6,22},{7,23},{8,24},{9,... | collective-permute-start | bytes 221192 | tf_op jit(solution)/shard_map/ppermute | solution.py:566
  (16 other events, 194.3 us)

commit v6 on v5

--- a/solution.py
+++ b/solution.py
@@ -592,10 +592,12 @@
     return list(zip(axes, turned))
 
 
-def point_steps(sizes):
-    masks = bits(sizes[1])
-    groups = [[bit] for bit in masks[:-2]]
-    groups.append([masks[-2], masks[-1], masks[-2] | masks[-1]] if len(masks) > 1 else masks)
+def direct_steps(masks, sizes):
+    groups = [[mask] for mask in masks[:-2]]
+    if len(masks) > 1:
+        groups.append([masks[-2], masks[-1], masks[-2] | masks[-1]])
+    elif masks:
+        groups.append([masks[-1]])
 
     def step(group):
         def run(value):
@@ -608,13 +610,17 @@
     return [step(group) for group in groups]
 
 
+def point_steps(sizes):
+    return direct_steps(bits(sizes[1]), sizes)
+
+
 def all_axes(sizes):
     return paired(
         [(1, 1)] + [(0, b) for b in bits(sizes[0])[1:]] + [(1, b) for b in bits(sizes[1])[1:]]
     )
 
 
-def quarter_steps(sizes):
+def quarter_steps(sizes, direct):
     group = [lambda d, p: (d ^ 2, p), lambda d, p: (d, p ^ 1), lambda d, p: (d ^ 2, p ^ 1)]
     others = paired([(0, b) for b in bits(sizes[0])[2:]] + [(1, b) for b in bits(sizes[1])[1:]])
 
@@ -639,12 +645,17 @@
     def last(value):
         return value, swap(value, flips(CORES), sizes)
 
-    return [cores, scatter] + [add(axes) for axes in others] + [gather, last]
-
-
-def all_steps(sizes, scatters):
+    if direct:
+        sums = [add(axes) for axes in paired([(0, b) for b in bits(sizes[0])[2:]])]
+        sums += direct_steps(bits(sizes[1])[1:], sizes)
+    else:
+        sums = [add(axes) for axes in others]
+    return [cores, scatter] + sums + [gather, last]
+
+
+def all_steps(sizes, scatters, direct=False):
     if scatters == 0:
-        return quarter_steps(sizes)
+        return quarter_steps(sizes, direct)
     steps_axes = all_axes(sizes)
 
     def add_halve(i, mine, received):
@@ -769,7 +780,7 @@
         rows_kernel, "rows", [VMEM] * 4, VMEM, shape(1, points, width),
         (front, front_wide, back_wide, end), 2 * dense,
     )
-    steps = all_steps(sizes, LATE)
+    steps = all_steps(sizes, LATE, True)
     for i, step in enumerate(steps):
         late = step(late)
         if i == 0:

time: 74 us -> 72.2 us (0.976)
  waiting for transfers between devices: 19.5 us -> 16.9 us
  starting transfers between devices: 36.1 us -> 36.9 us
    ppermute x28 -> x29, waiting for transfers between devices: 19.5 us -> 16.9 us  [swap(): return lax.ppermute(value, ('dp', 'point'), pairs)]
    ppermute x28 -> x29, starting transfers between devices: 36.1 us -> 36.9 us  [swap(): return lax.ppermute(value, ('dp', 'point'), pairs)]
  transfers between devices with their start and end apart: 28 -> 29, of which waited for: 10 -> 10; matrix products, arithmetic and copies ran while one was open for 0% -> 0% of each run, Pallas kernels for 5% -> 5%
where the time goes in v6:
time: 72.2 us; the launch traced here: 72 us
  starting transfers between devices  36.9 us (51%)
  Pallas kernels  17 us (24%)
  waiting for transfers between devices  16.9 us (23%)
  between operations  0.96 us (1%)
    ppermute x29, starting transfers between devices, swap(): return lax.ppermute(value, ('dp', 'point'), pairs)  36.9 us
    pallas_call x10, Pallas kernels, call(): pl.pallas_call(body, name=name, in_specs=in_specs, out_specs=out_specs, o...  17 us
    ppermute x29, waiting for transfers between devices, swap(): return lax.ppermute(value, ('dp', 'point'), pairs)  16.9 us
  transfers between devices with their start and end apart: 29, of which 10 were waited for; matrix products, arithmetic and copies ran while one was open for 0% of the time, Pallas kernels for 5%

profile of v6, /device:TPU:0, one launch (start us, length us, event | category | flops | bytes accessed | tf_op | source)
XLA Modules:
  0.0 72.0 jit_solution(14043647429505182958)
XLA Ops:
  0.7 4.0 %front.1 = (bf16[3072,512]{1,0:T(8,128)(2,1)S(1)}, f32[272,512]{1,0:T(8,128)S(1)}, f32[136,128]{1,0:T(8,128)S(1)}) custom-call(f32[1,512,256]{2,1,0:T(8,128)} %x_hbm.1, f32[1,256]{1,0:T(1,128)} %bitcast.4, f32[256,256]{1,0:T(8,128)} %fx_weight.1, f32[256,256]{1,0:T(8,128)} %x_weight.1, f32[32,64]{1,0:T(8,128)} %logit_weight.1, f32[8]{0:T(128)} %temper_hbm.1), custom_call_target="tpu_custom_call" | custom-call | flops 805306368 | bytes 1048576 | tf_op jit(solution)/shard_map/front/pallas_call | solution.py:546
  4.8 3.0 %collective-permute-start = (f32[136,128]{1,0:T(8,128)S(1)}, f32[136,128]{1,0:T(8,128)S(1)}, u32[]{:S(2)}, u32[]{:S(2)}) collective-permute-start(f32[136,128]{1,0:T(8,128)S(1)} %get-tuple-element.47), channel_id=1, source_target_pairs={{0,1},{1,0},{2,3},{3,2},{4,5},{5,4},{6,7},{7,6},{8,9},{9,8},{10,11... | collective-permute-start | bytes 208904 | tf_op jit(solution)/shard_map/ppermute | solution.py:566
  7.8 2.3 %collective-permute-done = f32[136,128]{1,0:T(8,128)S(1)} collective-permute-done((f32[136,128]{1,0:T(8,128)S(1)}, f32[136,128]{1,0:T(8,128)S(1)}, u32[]{:S(2)}, u32[]{:S(2)}) %collective-permute-start) | collective-permute-done | bytes 69664 | tf_op jit(solution)/shard_map/ppermute | solution.py:566
  10.1 4.2 %collective-permute-start.3 = (f32[136,128]{1,0:T(8,128)S(1)}, f32[136,128]{1,0:T(8,128)S(1)}, u32[]{:S(2)}, u32[]{:S(2)}) collective-permute-start(f32[136,128]{1,0:T(8,128)S(1)} %add.57), channel_id=1, source_target_pairs={{0,6},{1,7},{2,4},{3,5},{4,2},{5,3},{6,0},{7,1},{8,14},{9,15},{10,... | collective-permute-start | bytes 208904 | tf_op jit(solution)/shard_map/ppermute | solution.py:566
  16.8 2.9 %collective-permute-done.2 = f32[136,128]{1,0:T(8,128)S(1)} collective-permute-done((f32[136,128]{1,0:T(8,128)S(1)}, f32[136,128]{1,0:T(8,128)S(1)}, u32[]{:S(2)}, u32[]{:S(2)}) %collective-permute-start.2) | collective-permute-done | bytes 69664 | tf_op jit(solution)/shard_map/ppermute | solution.py:566
  19.7 3.8 %back.1 = (f32[32,512]{1,0:T(8,128)S(1)}, bf16[3072,512]{1,0:T(8,128)(2,1)S(1)}, f32[680,512]{1,0:T(8,128)S(1)}) custom-call(f32[136,128]{1,0:T(8,128)S(1)} %add_add_fusion.3.sums, bf16[3072,512]{1,0:T(8,128)(2,1)S(1)} %get-tuple-element.48.front, f32[272,512]{1,0:T(8,128)S(1)} %get-tuple-element.49.front_wide, ...), custom_call_target="tpu_custom_call" | custom-call | flops 1207959552 | bytes 1048576 | tf_op jit(solution)/shard_map/back/pallas_call | solution.py:546
  24.4 2.2 %collective-permute-start.6 = (f32[32,512]{1,0:T(8,128)S(1)}, f32[32,512]{1,0:T(8,128)S(1)}, u32[]{:S(2)}, u32[]{:S(2)}) collective-permute-start(f32[32,512]{1,0:T(8,128)S(1)} %get-tuple-element.57), channel_id=1, source_target_pairs={{0,6},{1,7},{2,4},{3,5},{4,2},{5,3},{6,0},{7,1},{8,14},{9,15},{10,... | collective-permute-start | bytes 196616 | tf_op jit(solution)/shard_map/ppermute | solution.py:566
  26.7 2.2 %collective-permute-start.4 = (f32[32,512]{1,0:T(8,128)S(1)}, f32[32,512]{1,0:T(8,128)S(1)}, u32[]{:S(2)}, u32[]{:S(2)}) collective-permute-start(f32[32,512]{1,0:T(8,128)S(1)} %get-tuple-element.57), channel_id=1, source_target_pairs={{0,2},{1,3},{2,0},{3,1},{4,6},{5,7},{6,4},{7,5},{8,10},{9,11},{10,... | collective-permute-start | bytes 196616 | tf_op jit(solution)/shard_map/ppermute | solution.py:566
  28.9 1.6 %collective-permute-start.9 = (f32[96,256]{1,0:T(8,128)S(1)}, f32[96,256]{1,0:T(8,128)S(1)}, u32[]{:S(2)}, u32[]{:S(2)}) collective-permute-start(f32[96,256]{1,0:T(8,128)S(1)} %get-tuple-element.62), channel_id=1, source_target_pairs={{0,16},{1,17},{2,18},{3,19},{4,20},{5,21},{6,22},{7,23},{8,24},{9,... | collective-permute-start | bytes 294920 | tf_op jit(solution)/shard_map/ppermute | solution.py:566
  30.5 1.5 %collective-permute-start.10 = (f32[96,256]{1,0:T(8,128)S(1)}, f32[96,256]{1,0:T(8,128)S(1)}, u32[]{:S(2)}, u32[]{:S(2)}) collective-permute-start(f32[96,256]{1,0:T(8,128)S(1)} %get-tuple-element.63), channel_id=1, source_target_pairs={{0,1},{1,0},{2,3},{3,2},{4,5},{5,4},{6,7},{7,6},{8,9},{9,8},{10,11... | collective-permute-start | bytes 294920 | tf_op jit(solution)/shard_map/ppermute | solution.py:566
  32.0 1.7 %collective-permute-start.11 = (f32[96,256]{1,0:T(8,128)S(1)}, f32[96,256]{1,0:T(8,128)S(1)}, u32[]{:S(2)}, u32[]{:S(2)}) collective-permute-start(f32[96,256]{1,0:T(8,128)S(1)} %get-tuple-element.64), channel_id=1, source_target_pairs={{0,17},{1,16},{2,19},{3,18},{4,21},{5,20},{6,23},{7,22},{8,25},{9,... | collective-permute-start | bytes 294920 | tf_op jit(solution)/shard_map/ppermute | solution.py:566
  33.8 1.4 %collective-permute-start.7 = (f32[32,512]{1,0:T(8,128)S(1)}, f32[32,512]{1,0:T(8,128)S(1)}, u32[]{:S(2)}, u32[]{:S(2)}) collective-permute-start(f32[32,512]{1,0:T(8,128)S(1)} %add_add_fusion.4), channel_id=1, source_target_pairs={{0,1},{1,0},{2,3},{3,2},{4,5},{5,4},{6,7},{7,6},{8,9},{9,8},{10,11... | collective-permute-start | bytes 196616 | tf_op jit(solution)/shard_map/ppermute | solution.py:566
  35.1 3.4 %collective-permute-done.7 = f32[32,512]{1,0:T(8,128)S(1)} collective-permute-done((f32[32,512]{1,0:T(8,128)S(1)}, f32[32,512]{1,0:T(8,128)S(1)}, u32[]{:S(2)}, u32[]{:S(2)}) %collective-permute-start.7) | collective-permute-done | bytes 65568 | tf_op jit(solution)/shard_map/ppermute | solution.py:566
  38.6 3.9 %end.1 = (f32[288,256]{1,0:T(8,128)S(1)}, f32[288,256]{1,0:T(8,128)S(1)}, bf16[1024,512]{1,0:T(8,128)(2,1)S(1)}) custom-call(f32[32,512]{1,0:T(8,128)S(1)} %add.64.out_sum, bf16[3072,512]{1,0:T(8,128)(2,1)S(1)} %get-tuple-element.48.front, f32[272,512]{1,0:T(8,128)S(1)} %get-tuple-element.49.front_wide, bf16[2560,256]{1,0:T(8,128)(2,1)S(1)} %get-tuple-element.56.map_packed, ...), custom_call_target="tpu_custom_call" | custom-call | flops 1610612736 | bytes 1048576 | tf_op jit(solution)/shard_map/end/pallas_call | solution.py:546
  42.6 1.6 %rows.1 = f32[1,512,256]{2,1,0:T(8,128)} custom-call(bf16[3072,512]{1,0:T(8,128)(2,1)S(1)} %get-tuple-element.48.front, f32[272,512]{1,0:T(8,128)S(1)} %get-tuple-element.49.front_wide, f32[680,512]{1,0:T(8,128)S(1)} %get-tuple-element.66.back_wide, bf16[1024,512]{1,0:T(8,128)(2,1)S(1)} %get-tuple-element.75.end), custom_call_target="tpu_custom_call" | custom-call | flops 402653184 | bytes 1048576 | tf_op jit(solution)/shard_map/rows/pallas_call | solution.py:546
  44.3 1.4 %collective-permute-start.13 = (f32[72,256]{1,0:T(8,128)S(1)}, f32[72,256]{1,0:T(8,128)S(1)}, u32[]{:S(2)}, u32[]{:S(2)}) collective-permute-start(f32[72,256]{1,0:T(8,128)S(1)} %get-tuple-element.78), channel_id=1, source_target_pairs={{0,16},{1,17},{2,18},{3,19},{4,20},{5,21},{6,22},{7,23},{8,24},{9,... | collective-permute-start | bytes 221192 | tf_op jit(solution)/shard_map/ppermute | solution.py:566
  45.7 1.5 %collective-permute-start.14 = (f32[72,256]{1,0:T(8,128)S(1)}, f32[72,256]{1,0:T(8,128)S(1)}, u32[]{:S(2)}, u32[]{:S(2)}) collective-permute-start(f32[72,256]{1,0:T(8,128)S(1)} %get-tuple-element.79), channel_id=1, source_target_pairs={{0,1},{1,0},{2,3},{3,2},{4,5},{5,4},{6,7},{7,6},{8,9},{9,8},{10,11... | collective-permute-start | bytes 221192 | tf_op jit(solution)/shard_map/ppermute | solution.py:566
  47.9 2.8 %collective-permute-start.24 = (f32[96,256]{1,0:T(8,128)S(1)}, f32[96,256]{1,0:T(8,128)S(1)}, u32[]{:S(2)}, u32[]{:S(2)}) collective-permute-start(f32[96,256]{1,0:T(8,128)S(1)} %add.74), channel_id=1, source_target_pairs={{0,4},{1,5},{2,6},{3,7},{4,0},{5,1},{6,2},{7,3},{8,10},{9,11},{10,... | collective-permute-start | bytes 294920 | tf_op jit(solution)/shard_map/ppermute | solution.py:566
  50.7 1.9 %collective-permute-done.15 = f32[72,256]{1,0:T(8,128)S(1)} collective-permute-done((f32[72,256]{1,0:T(8,128)S(1)}, f32[72,256]{1,0:T(8,128)S(1)}, u32[]{:S(2)}, u32[]{:S(2)}) %collective-permute-start.15) | collective-permute-done | bytes 73760 | tf_op jit(solution)/shard_map/ppermute | solution.py:566
  52.6 2.5 %collective-permute-start.18 = (f32[72,256]{1,0:T(8,128)S(1)}, f32[72,256]{1,0:T(8,128)S(1)}, u32[]{:S(2)}, u32[]{:S(2)}) collective-permute-start(f32[72,256]{1,0:T(8,128)S(1)} %add_add_fusion.2), channel_id=1, source_target_pairs={{0,6},{1,7},{2,4},{3,5},{4,2},{5,3},{6,0},{7,1},{8,14},{9,15},{10,... | collective-permute-start | bytes 221192 | tf_op jit(solution)/shard_map/ppermute | solution.py:566
  57.1 1.8 %collective-permute-start.27 = (f32[96,256]{1,0:T(8,128)S(1)}, f32[96,256]{1,0:T(8,128)S(1)}, u32[]{:S(2)}, u32[]{:S(2)}) collective-permute-start(f32[96,256]{1,0:T(8,128)S(1)} %add.75), channel_id=1, source_target_pairs={{0,17},{1,16},{2,19},{3,18},{4,21},{5,20},{6,23},{7,22},{8,25},{9,... | collective-permute-start | bytes 294920 | tf_op jit(solution)/shard_map/ppermute | solution.py:566
  60.8 1.7 %collective-permute-done.17 = f32[72,256]{1,0:T(8,128)S(1)} collective-permute-done((f32[72,256]{1,0:T(8,128)S(1)}, f32[72,256]{1,0:T(8,128)S(1)}, u32[]{:S(2)}, u32[]{:S(2)}) %collective-permute-start.17) | collective-permute-done | bytes 73760 | tf_op jit(solution)/shard_map/ppermute | solution.py:566
  62.5 2.1 %collective-permute-start.21 = (f32[72,256]{1,0:T(8,128)S(1)}, f32[72,256]{1,0:T(8,128)S(1)}, u32[]{:S(2)}, u32[]{:S(2)}) collective-permute-start(f32[72,256]{1,0:T(8,128)S(1)} %add_add_fusion.1), channel_id=1, source_target_pairs={{0,17},{1,16},{2,19},{3,18},{4,21},{5,20},{6,23},{7,22},{8,25},{9,... | collective-permute-start | bytes 221192 | tf_op jit(solution)/shard_map/ppermute | solution.py:566
  66.2 2.1 %collective-permute-done.21 = f32[72,256]{1,0:T(8,128)S(1)} collective-permute-done((f32[72,256]{1,0:T(8,128)S(1)}, f32[72,256]{1,0:T(8,128)S(1)}, u32[]{:S(2)}, u32[]{:S(2)}) %collective-permute-start.21) | collective-permute-done | bytes 73760 | tf_op jit(solution)/shard_map/ppermute | solution.py:566
  (79 shorter events, 13.6 us)
Async XLA Ops:
  4.8 5.3 %collective-permute-start = (f32[136,128]{1,0:T(8,128)S(1)}, f32[136,128]{1,0:T(8,128)S(1)}, u32[]{:S(2)}, u32[]{:S(2)}) collective-permute-start(f32[136,128]{1,0:T(8,128)S(1)} %get-tuple-element.47), channel_id=1, source_target_pairs={{0,1},{1,0},{2,3},{3,2},{4,5},{5,4},{6,7},{7,6},{8,9},{9,8},{10,11... | collective-permute-start | bytes 208904 | tf_op jit(solution)/shard_map/ppermute | solution.py:566
  10.1 6.7 %collective-permute-start.3 = (f32[136,128]{1,0:T(8,128)S(1)}, f32[136,128]{1,0:T(8,128)S(1)}, u32[]{:S(2)}, u32[]{:S(2)}) collective-permute-start(f32[136,128]{1,0:T(8,128)S(1)} %add.57), channel_id=1, source_target_pairs={{0,6},{1,7},{2,4},{3,5},{4,2},{5,3},{6,0},{7,1},{8,14},{9,15},{10,... | collective-permute-start | bytes 208904 | tf_op jit(solution)/shard_map/ppermute | solution.py:566
  14.3 5.4 %collective-permute-start.2 = (f32[136,128]{1,0:T(8,128)S(1)}, f32[136,128]{1,0:T(8,128)S(1)}, u32[]{:S(2)}, u32[]{:S(2)}) collective-permute-start(f32[136,128]{1,0:T(8,128)S(1)} %add.57), channel_id=1, source_target_pairs={{0,4},{1,5},{2,6},{3,7},{4,0},{5,1},{6,2},{7,3},{8,12},{9,13},{10,... | collective-permute-start | bytes 208904 | tf_op jit(solution)/shard_map/ppermute | solution.py:566
  14.3 5.4 %collective-permute-start.1 = (f32[136,128]{1,0:T(8,128)S(1)}, f32[136,128]{1,0:T(8,128)S(1)}, u32[]{:S(2)}, u32[]{:S(2)}) collective-permute-start(f32[136,128]{1,0:T(8,128)S(1)} %add.57), channel_id=1, source_target_pairs={{0,2},{1,3},{2,0},{3,1},{4,6},{5,7},{6,4},{7,5},{8,10},{9,11},{10,... | collective-permute-start | bytes 208904 | tf_op jit(solution)/shard_map/ppermute | solution.py:566
  24.4 4.5 %collective-permute-start.8 = (f32[384,256]{1,0:T(8,128)S(1)}, f32[384,256]{1,0:T(8,128)S(1)}, u32[]{:S(2)}, u32[]{:S(2)}) collective-permute-start(f32[384,256]{1,0:T(8,128)S(1)} %get-tuple-element.60), channel_id=1, source_target_pairs={{0,8},{1,9},{2,10},{3,11},{4,12},{5,13},{6,14},{7,15},{8,0},{9,1},... | collective-permute-start | bytes 1179656 | tf_op jit(solution)/shard_map/ppermute | solution.py:566
  24.4 7.6 %collective-permute-start.6 = (f32[32,512]{1,0:T(8,128)S(1)}, f32[32,512]{1,0:T(8,128)S(1)}, u32[]{:S(2)}, u32[]{:S(2)}) collective-permute-start(f32[32,512]{1,0:T(8,128)S(1)} %get-tuple-element.57), channel_id=1, source_target_pairs={{0,6},{1,7},{2,4},{3,5},{4,2},{5,3},{6,0},{7,1},{8,14},{9,15},{10,... | collective-permute-start | bytes 196616 | tf_op jit(solution)/shard_map/ppermute | solution.py:566
  26.7 7.1 %collective-permute-start.5 = (f32[32,512]{1,0:T(8,128)S(1)}, f32[32,512]{1,0:T(8,128)S(1)}, u32[]{:S(2)}, u32[]{:S(2)}) collective-permute-start(f32[32,512]{1,0:T(8,128)S(1)} %get-tuple-element.57), channel_id=1, source_target_pairs={{0,4},{1,5},{2,6},{3,7},{4,0},{5,1},{6,2},{7,3},{8,12},{9,13},{10,... | collective-permute-start | bytes 196616 | tf_op jit(solution)/shard_map/ppermute | solution.py:566
  26.7 7.1 %collective-permute-start.4 = (f32[32,512]{1,0:T(8,128)S(1)}, f32[32,512]{1,0:T(8,128)S(1)}, u32[]{:S(2)}, u32[]{:S(2)}) collective-permute-start(f32[32,512]{1,0:T(8,128)S(1)} %get-tuple-element.57), channel_id=1, source_target_pairs={{0,2},{1,3},{2,0},{3,1},{4,6},{5,7},{6,4},{7,5},{8,10},{9,11},{10,... | collective-permute-start | bytes 196616 | tf_op jit(solution)/shard_map/ppermute | solution.py:566
  28.9 9.6 %collective-permute-start.9 = (f32[96,256]{1,0:T(8,128)S(1)}, f32[96,256]{1,0:T(8,128)S(1)}, u32[]{:S(2)}, u32[]{:S(2)}) collective-permute-start(f32[96,256]{1,0:T(8,128)S(1)} %get-tuple-element.62), channel_id=1, source_target_pairs={{0,16},{1,17},{2,18},{3,19},{4,20},{5,21},{6,22},{7,23},{8,24},{9,... | collective-permute-start | bytes 294920 | tf_op jit(solution)/shard_map/ppermute | solution.py:566
  30.5 8.0 %collective-permute-start.10 = (f32[96,256]{1,0:T(8,128)S(1)}, f32[96,256]{1,0:T(8,128)S(1)}, u32[]{:S(2)}, u32[]{:S(2)}) collective-permute-start(f32[96,256]{1,0:T(8,128)S(1)} %get-tuple-element.63), channel_id=1, source_target_pairs={{0,1},{1,0},{2,3},{3,2},{4,5},{5,4},{6,7},{7,6},{8,9},{9,8},{10,11... | collective-permute-start | bytes 294920 | tf_op jit(solution)/shard_map/ppermute | solution.py:566
  32.0 6.5 %collective-permute-start.11 = (f32[96,256]{1,0:T(8,128)S(1)}, f32[96,256]{1,0:T(8,128)S(1)}, u32[]{:S(2)}, u32[]{:S(2)}) collective-permute-start(f32[96,256]{1,0:T(8,128)S(1)} %get-tuple-element.64), channel_id=1, source_target_pairs={{0,17},{1,16},{2,19},{3,18},{4,21},{5,20},{6,23},{7,22},{8,25},{9,... | collective-permute-start | bytes 294920 | tf_op jit(solution)/shard_map/ppermute | solution.py:566
  33.8 4.8 %collective-permute-start.7 = (f32[32,512]{1,0:T(8,128)S(1)}, f32[32,512]{1,0:T(8,128)S(1)}, u32[]{:S(2)}, u32[]{:S(2)}) collective-permute-start(f32[32,512]{1,0:T(8,128)S(1)} %add_add_fusion.4), channel_id=1, source_target_pairs={{0,1},{1,0},{2,3},{3,2},{4,5},{5,4},{6,7},{7,6},{8,9},{9,8},{10,11... | collective-permute-start | bytes 196616 | tf_op jit(solution)/shard_map/ppermute | solution.py:566
  42.6 5.3 %collective-permute-start.23 = (f32[96,256]{1,0:T(8,128)S(1)}, f32[96,256]{1,0:T(8,128)S(1)}, u32[]{:S(2)}, u32[]{:S(2)}) collective-permute-start(f32[96,256]{1,0:T(8,128)S(1)} %add_add_fusion), channel_id=1, source_target_pairs={{0,2},{1,3},{2,0},{3,1},{4,6},{5,7},{6,4},{7,5},{8,12},{9,13},{10,... | collective-permute-start | bytes 294920 | tf_op jit(solution)/shard_map/ppermute | solution.py:566
  44.3 6.4 %collective-permute-start.13 = (f32[72,256]{1,0:T(8,128)S(1)}, f32[72,256]{1,0:T(8,128)S(1)}, u32[]{:S(2)}, u32[]{:S(2)}) collective-permute-start(f32[72,256]{1,0:T(8,128)S(1)} %get-tuple-element.78), channel_id=1, source_target_pairs={{0,16},{1,17},{2,18},{3,19},{4,20},{5,21},{6,22},{7,23},{8,24},{9,... | collective-permute-start | bytes 221192 | tf_op jit(solution)/shard_map/ppermute | solution.py:566
  45.7 5.0 %collective-permute-start.14 = (f32[72,256]{1,0:T(8,128)S(1)}, f32[72,256]{1,0:T(8,128)S(1)}, u32[]{:S(2)}, u32[]{:S(2)}) collective-permute-start(f32[72,256]{1,0:T(8,128)S(1)} %get-tuple-element.79), channel_id=1, source_target_pairs={{0,1},{1,0},{2,3},{3,2},{4,5},{5,4},{6,7},{7,6},{8,9},{9,8},{10,11... | collective-permute-start | bytes 221192 | tf_op jit(solution)/shard_map/ppermute | solution.py:566
  47.2 5.4 %collective-permute-start.15 = (f32[72,256]{1,0:T(8,128)S(1)}, f32[72,256]{1,0:T(8,128)S(1)}, u32[]{:S(2)}, u32[]{:S(2)}) collective-permute-start(f32[72,256]{1,0:T(8,128)S(1)} %get-tuple-element.80), channel_id=1, source_target_pairs={{0,17},{1,16},{2,19},{3,18},{4,21},{5,20},{6,23},{7,22},{8,25},{9,... | collective-permute-start | bytes 221192 | tf_op jit(solution)/shard_map/ppermute | solution.py:566
  47.9 9.2 %collective-permute-start.24 = (f32[96,256]{1,0:T(8,128)S(1)}, f32[96,256]{1,0:T(8,128)S(1)}, u32[]{:S(2)}, u32[]{:S(2)}) collective-permute-start(f32[96,256]{1,0:T(8,128)S(1)} %add.74), channel_id=1, source_target_pairs={{0,4},{1,5},{2,6},{3,7},{4,0},{5,1},{6,2},{7,3},{8,10},{9,11},{10,... | collective-permute-start | bytes 294920 | tf_op jit(solution)/shard_map/ppermute | solution.py:566
  52.6 7.2 %collective-permute-start.18 = (f32[72,256]{1,0:T(8,128)S(1)}, f32[72,256]{1,0:T(8,128)S(1)}, u32[]{:S(2)}, u32[]{:S(2)}) collective-permute-start(f32[72,256]{1,0:T(8,128)S(1)} %add_add_fusion.2), channel_id=1, source_target_pairs={{0,6},{1,7},{2,4},{3,5},{4,2},{5,3},{6,0},{7,1},{8,14},{9,15},{10,... | collective-permute-start | bytes 221192 | tf_op jit(solution)/shard_map/ppermute | solution.py:566
  55.0 7.5 %collective-permute-start.17 = (f32[72,256]{1,0:T(8,128)S(1)}, f32[72,256]{1,0:T(8,128)S(1)}, u32[]{:S(2)}, u32[]{:S(2)}) collective-permute-start(f32[72,256]{1,0:T(8,128)S(1)} %add_add_fusion.2), channel_id=1, source_target_pairs={{0,4},{1,5},{2,6},{3,7},{4,0},{5,1},{6,2},{7,3},{8,12},{9,13},{10,... | collective-permute-start | bytes 221192 | tf_op jit(solution)/shard_map/ppermute | solution.py:566
  55.9 6.6 %collective-permute-start.16 = (f32[72,256]{1,0:T(8,128)S(1)}, f32[72,256]{1,0:T(8,128)S(1)}, u32[]{:S(2)}, u32[]{:S(2)}) collective-permute-start(f32[72,256]{1,0:T(8,128)S(1)} %add_add_fusion.2), channel_id=1, source_target_pairs={{0,2},{1,3},{2,0},{3,1},{4,6},{5,7},{6,4},{7,5},{8,10},{9,11},{10,... | collective-permute-start | bytes 221192 | tf_op jit(solution)/shard_map/ppermute | solution.py:566
  57.1 7.8 %collective-permute-start.27 = (f32[96,256]{1,0:T(8,128)S(1)}, f32[96,256]{1,0:T(8,128)S(1)}, u32[]{:S(2)}, u32[]{:S(2)}) collective-permute-start(f32[96,256]{1,0:T(8,128)S(1)} %add.75), channel_id=1, source_target_pairs={{0,17},{1,16},{2,19},{3,18},{4,21},{5,20},{6,23},{7,22},{8,25},{9,... | collective-permute-start | bytes 294920 | tf_op jit(solution)/shard_map/ppermute | solution.py:566
  58.9 7.2 %collective-permute-start.26 = (f32[96,256]{1,0:T(8,128)S(1)}, f32[96,256]{1,0:T(8,128)S(1)}, u32[]{:S(2)}, u32[]{:S(2)}) collective-permute-start(f32[96,256]{1,0:T(8,128)S(1)} %add.75), channel_id=1, source_target_pairs={{0,1},{1,0},{2,3},{3,2},{4,5},{5,4},{6,7},{7,6},{8,9},{9,8},{10,11... | collective-permute-start | bytes 294920 | tf_op jit(solution)/shard_map/ppermute | solution.py:566
  59.8 6.3 %collective-permute-start.25 = (f32[96,256]{1,0:T(8,128)S(1)}, f32[96,256]{1,0:T(8,128)S(1)}, u32[]{:S(2)}, u32[]{:S(2)}) collective-permute-start(f32[96,256]{1,0:T(8,128)S(1)} %add.75), channel_id=1, source_target_pairs={{0,16},{1,17},{2,18},{3,19},{4,20},{5,21},{6,22},{7,23},{8,24},{9,... | collective-permute-start | bytes 294920 | tf_op jit(solution)/shard_map/ppermute | solution.py:566
  62.5 5.7 %collective-permute-start.21 = (f32[72,256]{1,0:T(8,128)S(1)}, f32[72,256]{1,0:T(8,128)S(1)}, u32[]{:S(2)}, u32[]{:S(2)}) collective-permute-start(f32[72,256]{1,0:T(8,128)S(1)} %add_add_fusion.1), channel_id=1, source_target_pairs={{0,17},{1,16},{2,19},{3,18},{4,21},{5,20},{6,23},{7,22},{8,25},{9,... | collective-permute-start | bytes 221192 | tf_op jit(solution)/shard_map/ppermute | solution.py:566
  (17 other events, 185.3 us)

commit v7 on v6

--- a/solution.py
+++ b/solution.py
@@ -622,7 +622,7 @@
 
 def quarter_steps(sizes, direct):
     group = [lambda d, p: (d ^ 2, p), lambda d, p: (d, p ^ 1), lambda d, p: (d ^ 2, p ^ 1)]
-    others = paired([(0, b) for b in bits(sizes[0])[2:]] + [(1, b) for b in bits(sizes[1])[1:]])
+    others = paired(([(0, b) for b in bits(sizes[0])[2:]] + [(1, b) for b in bits(sizes[1])[1:]])[::-1])
 
     def cores(value):
         received = swap(value[1], flips(CORES), sizes)

time: 72.2 us -> 71.6 us (level)
  transfers between devices with their start and end apart: 29 -> 29, of which waited for: 10 -> 12; matrix products, arithmetic and copies ran while one was open for 0% -> 0% of each run, Pallas kernels for 5% -> 5%
where the time goes in v7:
time: 71.6 us; the launch traced here: 71.4 us
  starting transfers between devices  36.8 us (51%)
  Pallas kernels  17 us (24%)
  waiting for transfers between devices  16.4 us (23%)
  between operations  0.96 us (1%)
    ppermute x29, starting transfers between devices, swap(): return lax.ppermute(value, ('dp', 'point'), pairs)  36.8 us
    pallas_call x10, Pallas kernels, call(): pl.pallas_call(body, name=name, in_specs=in_specs, out_specs=out_specs, o...  17 us
    ppermute x29, waiting for transfers between devices, swap(): return lax.ppermute(value, ('dp', 'point'), pairs)  16.4 us
  transfers between devices with their start and end apart: 29, of which 12 were waited for; matrix products, arithmetic and copies ran while one was open for 0% of the time, Pallas kernels for 5%

profile of v7, /device:TPU:0, one launch (start us, length us, event | category | flops | bytes accessed | tf_op | source)
XLA Modules:
  0.0 71.4 jit_solution(2774240834622841638)
XLA Ops:
  0.7 4.0 %front.1 = (bf16[3072,512]{1,0:T(8,128)(2,1)S(1)}, f32[272,512]{1,0:T(8,128)S(1)}, f32[136,128]{1,0:T(8,128)S(1)}) custom-call(f32[1,512,256]{2,1,0:T(8,128)} %x_hbm.1, f32[1,256]{1,0:T(1,128)} %bitcast.4, f32[256,256]{1,0:T(8,128)} %fx_weight.1, f32[256,256]{1,0:T(8,128)} %x_weight.1, f32[32,64]{1,0:T(8,128)} %logit_weight.1, f32[8]{0:T(128)} %temper_hbm.1), custom_call_target="tpu_custom_call" | custom-call | flops 805306368 | bytes 1048576 | tf_op jit(solution)/shard_map/front/pallas_call | solution.py:546
  4.8 3.0 %collective-permute-start = (f32[136,128]{1,0:T(8,128)S(1)}, f32[136,128]{1,0:T(8,128)S(1)}, u32[]{:S(2)}, u32[]{:S(2)}) collective-permute-start(f32[136,128]{1,0:T(8,128)S(1)} %get-tuple-element.47), channel_id=1, source_target_pairs={{0,1},{1,0},{2,3},{3,2},{4,5},{5,4},{6,7},{7,6},{8,9},{9,8},{10,11... | collective-permute-start | bytes 208904 | tf_op jit(solution)/shard_map/ppermute | solution.py:566
  7.8 2.3 %collective-permute-done = f32[136,128]{1,0:T(8,128)S(1)} collective-permute-done((f32[136,128]{1,0:T(8,128)S(1)}, f32[136,128]{1,0:T(8,128)S(1)}, u32[]{:S(2)}, u32[]{:S(2)}) %collective-permute-start) | collective-permute-done | bytes 69664 | tf_op jit(solution)/shard_map/ppermute | solution.py:566
  10.1 4.2 %collective-permute-start.3 = (f32[136,128]{1,0:T(8,128)S(1)}, f32[136,128]{1,0:T(8,128)S(1)}, u32[]{:S(2)}, u32[]{:S(2)}) collective-permute-start(f32[136,128]{1,0:T(8,128)S(1)} %add.57), channel_id=1, source_target_pairs={{0,6},{1,7},{2,4},{3,5},{4,2},{5,3},{6,0},{7,1},{8,14},{9,15},{10,... | collective-permute-start | bytes 208904 | tf_op jit(solution)/shard_map/ppermute | solution.py:566
  16.8 2.9 %collective-permute-done.2 = f32[136,128]{1,0:T(8,128)S(1)} collective-permute-done((f32[136,128]{1,0:T(8,128)S(1)}, f32[136,128]{1,0:T(8,128)S(1)}, u32[]{:S(2)}, u32[]{:S(2)}) %collective-permute-start.2) | collective-permute-done | bytes 69664 | tf_op jit(solution)/shard_map/ppermute | solution.py:566
  19.7 3.8 %back.1 = (f32[32,512]{1,0:T(8,128)S(1)}, bf16[3072,512]{1,0:T(8,128)(2,1)S(1)}, f32[680,512]{1,0:T(8,128)S(1)}) custom-call(f32[136,128]{1,0:T(8,128)S(1)} %add_add_fusion.3.sums, bf16[3072,512]{1,0:T(8,128)(2,1)S(1)} %get-tuple-element.48.front, f32[272,512]{1,0:T(8,128)S(1)} %get-tuple-element.49.front_wide, ...), custom_call_target="tpu_custom_call" | custom-call | flops 1207959552 | bytes 1048576 | tf_op jit(solution)/shard_map/back/pallas_call | solution.py:546
  24.4 2.2 %collective-permute-start.6 = (f32[32,512]{1,0:T(8,128)S(1)}, f32[32,512]{1,0:T(8,128)S(1)}, u32[]{:S(2)}, u32[]{:S(2)}) collective-permute-start(f32[32,512]{1,0:T(8,128)S(1)} %get-tuple-element.57), channel_id=1, source_target_pairs={{0,6},{1,7},{2,4},{3,5},{4,2},{5,3},{6,0},{7,1},{8,14},{9,15},{10,... | collective-permute-start | bytes 196616 | tf_op jit(solution)/shard_map/ppermute | solution.py:566
  26.7 2.2 %collective-permute-start.4 = (f32[32,512]{1,0:T(8,128)S(1)}, f32[32,512]{1,0:T(8,128)S(1)}, u32[]{:S(2)}, u32[]{:S(2)}) collective-permute-start(f32[32,512]{1,0:T(8,128)S(1)} %get-tuple-element.57), channel_id=1, source_target_pairs={{0,2},{1,3},{2,0},{3,1},{4,6},{5,7},{6,4},{7,5},{8,10},{9,11},{10,... | collective-permute-start | bytes 196616 | tf_op jit(solution)/shard_map/ppermute | solution.py:566
  28.9 1.6 %collective-permute-start.9 = (f32[96,256]{1,0:T(8,128)S(1)}, f32[96,256]{1,0:T(8,128)S(1)}, u32[]{:S(2)}, u32[]{:S(2)}) collective-permute-start(f32[96,256]{1,0:T(8,128)S(1)} %get-tuple-element.62), channel_id=1, source_target_pairs={{0,16},{1,17},{2,18},{3,19},{4,20},{5,21},{6,22},{7,23},{8,24},{9,... | collective-permute-start | bytes 294920 | tf_op jit(solution)/shard_map/ppermute | solution.py:566
  30.5 1.5 %collective-permute-start.10 = (f32[96,256]{1,0:T(8,128)S(1)}, f32[96,256]{1,0:T(8,128)S(1)}, u32[]{:S(2)}, u32[]{:S(2)}) collective-permute-start(f32[96,256]{1,0:T(8,128)S(1)} %get-tuple-element.63), channel_id=1, source_target_pairs={{0,1},{1,0},{2,3},{3,2},{4,5},{5,4},{6,7},{7,6},{8,9},{9,8},{10,11... | collective-permute-start | bytes 294920 | tf_op jit(solution)/shard_map/ppermute | solution.py:566
  32.0 1.7 %collective-permute-start.11 = (f32[96,256]{1,0:T(8,128)S(1)}, f32[96,256]{1,0:T(8,128)S(1)}, u32[]{:S(2)}, u32[]{:S(2)}) collective-permute-start(f32[96,256]{1,0:T(8,128)S(1)} %get-tuple-element.64), channel_id=1, source_target_pairs={{0,17},{1,16},{2,19},{3,18},{4,21},{5,20},{6,23},{7,22},{8,25},{9,... | collective-permute-start | bytes 294920 | tf_op jit(solution)/shard_map/ppermute | solution.py:566
  33.8 1.4 %collective-permute-start.7 = (f32[32,512]{1,0:T(8,128)S(1)}, f32[32,512]{1,0:T(8,128)S(1)}, u32[]{:S(2)}, u32[]{:S(2)}) collective-permute-start(f32[32,512]{1,0:T(8,128)S(1)} %add_add_fusion.4), channel_id=1, source_target_pairs={{0,1},{1,0},{2,3},{3,2},{4,5},{5,4},{6,7},{7,6},{8,9},{9,8},{10,11... | collective-permute-start | bytes 196616 | tf_op jit(solution)/shard_map/ppermute | solution.py:566
  35.1 3.4 %collective-permute-done.7 = f32[32,512]{1,0:T(8,128)S(1)} collective-permute-done((f32[32,512]{1,0:T(8,128)S(1)}, f32[32,512]{1,0:T(8,128)S(1)}, u32[]{:S(2)}, u32[]{:S(2)}) %collective-permute-start.7) | collective-permute-done | bytes 65568 | tf_op jit(solution)/shard_map/ppermute | solution.py:566
  38.6 3.9 %end.1 = (f32[288,256]{1,0:T(8,128)S(1)}, f32[288,256]{1,0:T(8,128)S(1)}, bf16[1024,512]{1,0:T(8,128)(2,1)S(1)}) custom-call(f32[32,512]{1,0:T(8,128)S(1)} %add.64.out_sum, bf16[3072,512]{1,0:T(8,128)(2,1)S(1)} %get-tuple-element.48.front, f32[272,512]{1,0:T(8,128)S(1)} %get-tuple-element.49.front_wide, bf16[2560,256]{1,0:T(8,128)(2,1)S(1)} %get-tuple-element.56.map_packed, ...), custom_call_target="tpu_custom_call" | custom-call | flops 1610612736 | bytes 1048576 | tf_op jit(solution)/shard_map/end/pallas_call | solution.py:546
  42.6 1.8 %collective-permute-start.23 = (f32[96,256]{1,0:T(8,128)S(1)}, f32[96,256]{1,0:T(8,128)S(1)}, u32[]{:S(2)}, u32[]{:S(2)}) collective-permute-start(f32[96,256]{1,0:T(8,128)S(1)} %add_add_fusion), channel_id=1, source_target_pairs={{0,4},{1,5},{2,6},{3,7},{4,0},{5,1},{6,2},{7,3},{8,10},{9,11},{10,... | collective-permute-start | bytes 294920 | tf_op jit(solution)/shard_map/ppermute | solution.py:566
  44.4 1.6 %rows.1 = f32[1,512,256]{2,1,0:T(8,128)} custom-call(bf16[3072,512]{1,0:T(8,128)(2,1)S(1)} %get-tuple-element.48.front, f32[272,512]{1,0:T(8,128)S(1)} %get-tuple-element.49.front_wide, f32[680,512]{1,0:T(8,128)S(1)} %get-tuple-element.66.back_wide, bf16[1024,512]{1,0:T(8,128)(2,1)S(1)} %get-tuple-element.75.end), custom_call_target="tpu_custom_call" | custom-call | flops 402653184 | bytes 1048576 | tf_op jit(solution)/shard_map/rows/pallas_call | solution.py:546
  47.8 1.8 %collective-permute-start.15 = (f32[72,256]{1,0:T(8,128)S(1)}, f32[72,256]{1,0:T(8,128)S(1)}, u32[]{:S(2)}, u32[]{:S(2)}) collective-permute-start(f32[72,256]{1,0:T(8,128)S(1)} %get-tuple-element.80), channel_id=1, source_target_pairs={{0,17},{1,16},{2,19},{3,18},{4,21},{5,20},{6,23},{7,22},{8,25},{9,... | collective-permute-start | bytes 221192 | tf_op jit(solution)/shard_map/ppermute | solution.py:566
  51.4 1.6 %collective-permute-done.15 = f32[72,256]{1,0:T(8,128)S(1)} collective-permute-done((f32[72,256]{1,0:T(8,128)S(1)}, f32[72,256]{1,0:T(8,128)S(1)}, u32[]{:S(2)}, u32[]{:S(2)}) %collective-permute-start.15) | collective-permute-done | bytes 73760 | tf_op jit(solution)/shard_map/ppermute | solution.py:566
  53.0 1.9 %collective-permute-start.18 = (f32[72,256]{1,0:T(8,128)S(1)}, f32[72,256]{1,0:T(8,128)S(1)}, u32[]{:S(2)}, u32[]{:S(2)}) collective-permute-start(f32[72,256]{1,0:T(8,128)S(1)} %add_add_fusion.2), channel_id=1, source_target_pairs={{0,6},{1,7},{2,4},{3,5},{4,2},{5,3},{6,0},{7,1},{8,14},{9,15},{10,... | collective-permute-start | bytes 221192 | tf_op jit(solution)/shard_map/ppermute | solution.py:566
  54.9 1.6 %collective-permute-start.17 = (f32[72,256]{1,0:T(8,128)S(1)}, f32[72,256]{1,0:T(8,128)S(1)}, u32[]{:S(2)}, u32[]{:S(2)}) collective-permute-start(f32[72,256]{1,0:T(8,128)S(1)} %add_add_fusion.2), channel_id=1, source_target_pairs={{0,4},{1,5},{2,6},{3,7},{4,0},{5,1},{6,2},{7,3},{8,12},{9,13},{10,... | collective-permute-start | bytes 221192 | tf_op jit(solution)/shard_map/ppermute | solution.py:566
  57.5 1.9 %collective-permute-start.27 = (f32[96,256]{1,0:T(8,128)S(1)}, f32[96,256]{1,0:T(8,128)S(1)}, u32[]{:S(2)}, u32[]{:S(2)}) collective-permute-start(f32[96,256]{1,0:T(8,128)S(1)} %add.75), channel_id=1, source_target_pairs={{0,17},{1,16},{2,19},{3,18},{4,21},{5,20},{6,23},{7,22},{8,25},{9,... | collective-permute-start | bytes 294920 | tf_op jit(solution)/shard_map/ppermute | solution.py:566
  61.7 1.3 %collective-permute-start.21 = (f32[72,256]{1,0:T(8,128)S(1)}, f32[72,256]{1,0:T(8,128)S(1)}, u32[]{:S(2)}, u32[]{:S(2)}) collective-permute-start(f32[72,256]{1,0:T(8,128)S(1)} %add_add_fusion.1), channel_id=1, source_target_pairs={{0,17},{1,16},{2,19},{3,18},{4,21},{5,20},{6,23},{7,22},{8,25},{9,... | collective-permute-start | bytes 221192 | tf_op jit(solution)/shard_map/ppermute | solution.py:566
  63.1 1.2 %collective-permute-start.20 = (f32[72,256]{1,0:T(8,128)S(1)}, f32[72,256]{1,0:T(8,128)S(1)}, u32[]{:S(2)}, u32[]{:S(2)}) collective-permute-start(f32[72,256]{1,0:T(8,128)S(1)} %add_add_fusion.1), channel_id=1, source_target_pairs={{0,1},{1,0},{2,3},{3,2},{4,5},{5,4},{6,7},{7,6},{8,9},{9,8},{10,11... | collective-permute-start | bytes 221192 | tf_op jit(solution)/shard_map/ppermute | solution.py:566
  65.3 2.0 %collective-permute-done.25 = f32[96,256]{1,0:T(8,128)S(1)} collective-permute-done((f32[96,256]{1,0:T(8,128)S(1)}, f32[96,256]{1,0:T(8,128)S(1)}, u32[]{:S(2)}, u32[]{:S(2)}) %collective-permute-start.25) | collective-permute-done | bytes 98336 | tf_op jit(solution)/shard_map/ppermute | solution.py:566
  (79 shorter events, 15.6 us)
Async XLA Ops:
  4.8 5.3 %collective-permute-start = (f32[136,128]{1,0:T(8,128)S(1)}, f32[136,128]{1,0:T(8,128)S(1)}, u32[]{:S(2)}, u32[]{:S(2)}) collective-permute-start(f32[136,128]{1,0:T(8,128)S(1)} %get-tuple-element.47), channel_id=1, source_target_pairs={{0,1},{1,0},{2,3},{3,2},{4,5},{5,4},{6,7},{7,6},{8,9},{9,8},{10,11... | collective-permute-start | bytes 208904 | tf_op jit(solution)/shard_map/ppermute | solution.py:566
  10.1 6.7 %collective-permute-start.3 = (f32[136,128]{1,0:T(8,128)S(1)}, f32[136,128]{1,0:T(8,128)S(1)}, u32[]{:S(2)}, u32[]{:S(2)}) collective-permute-start(f32[136,128]{1,0:T(8,128)S(1)} %add.57), channel_id=1, source_target_pairs={{0,6},{1,7},{2,4},{3,5},{4,2},{5,3},{6,0},{7,1},{8,14},{9,15},{10,... | collective-permute-start | bytes 208904 | tf_op jit(solution)/shard_map/ppermute | solution.py:566
  14.3 5.4 %collective-permute-start.2 = (f32[136,128]{1,0:T(8,128)S(1)}, f32[136,128]{1,0:T(8,128)S(1)}, u32[]{:S(2)}, u32[]{:S(2)}) collective-permute-start(f32[136,128]{1,0:T(8,128)S(1)} %add.57), channel_id=1, source_target_pairs={{0,4},{1,5},{2,6},{3,7},{4,0},{5,1},{6,2},{7,3},{8,12},{9,13},{10,... | collective-permute-start | bytes 208904 | tf_op jit(solution)/shard_map/ppermute | solution.py:566
  14.3 5.4 %collective-permute-start.1 = (f32[136,128]{1,0:T(8,128)S(1)}, f32[136,128]{1,0:T(8,128)S(1)}, u32[]{:S(2)}, u32[]{:S(2)}) collective-permute-start(f32[136,128]{1,0:T(8,128)S(1)} %add.57), channel_id=1, source_target_pairs={{0,2},{1,3},{2,0},{3,1},{4,6},{5,7},{6,4},{7,5},{8,10},{9,11},{10,... | collective-permute-start | bytes 208904 | tf_op jit(solution)/shard_map/ppermute | solution.py:566
  24.4 4.5 %collective-permute-start.8 = (f32[384,256]{1,0:T(8,128)S(1)}, f32[384,256]{1,0:T(8,128)S(1)}, u32[]{:S(2)}, u32[]{:S(2)}) collective-permute-start(f32[384,256]{1,0:T(8,128)S(1)} %get-tuple-element.60), channel_id=1, source_target_pairs={{0,8},{1,9},{2,10},{3,11},{4,12},{5,13},{6,14},{7,15},{8,0},{9,1},... | collective-permute-start | bytes 1179656 | tf_op jit(solution)/shard_map/ppermute | solution.py:566
  24.4 7.6 %collective-permute-start.6 = (f32[32,512]{1,0:T(8,128)S(1)}, f32[32,512]{1,0:T(8,128)S(1)}, u32[]{:S(2)}, u32[]{:S(2)}) collective-permute-start(f32[32,512]{1,0:T(8,128)S(1)} %get-tuple-element.57), channel_id=1, source_target_pairs={{0,6},{1,7},{2,4},{3,5},{4,2},{5,3},{6,0},{7,1},{8,14},{9,15},{10,... | collective-permute-start | bytes 196616 | tf_op jit(solution)/shard_map/ppermute | solution.py:566
  26.7 7.1 %collective-permute-start.5 = (f32[32,512]{1,0:T(8,128)S(1)}, f32[32,512]{1,0:T(8,128)S(1)}, u32[]{:S(2)}, u32[]{:S(2)}) collective-permute-start(f32[32,512]{1,0:T(8,128)S(1)} %get-tuple-element.57), channel_id=1, source_target_pairs={{0,4},{1,5},{2,6},{3,7},{4,0},{5,1},{6,2},{7,3},{8,12},{9,13},{10,... | collective-permute-start | bytes 196616 | tf_op jit(solution)/shard_map/ppermute | solution.py:566
  26.7 7.1 %collective-permute-start.4 = (f32[32,512]{1,0:T(8,128)S(1)}, f32[32,512]{1,0:T(8,128)S(1)}, u32[]{:S(2)}, u32[]{:S(2)}) collective-permute-start(f32[32,512]{1,0:T(8,128)S(1)} %get-tuple-element.57), channel_id=1, source_target_pairs={{0,2},{1,3},{2,0},{3,1},{4,6},{5,7},{6,4},{7,5},{8,10},{9,11},{10,... | collective-permute-start | bytes 196616 | tf_op jit(solution)/shard_map/ppermute | solution.py:566
  28.9 9.6 %collective-permute-start.9 = (f32[96,256]{1,0:T(8,128)S(1)}, f32[96,256]{1,0:T(8,128)S(1)}, u32[]{:S(2)}, u32[]{:S(2)}) collective-permute-start(f32[96,256]{1,0:T(8,128)S(1)} %get-tuple-element.62), channel_id=1, source_target_pairs={{0,16},{1,17},{2,18},{3,19},{4,20},{5,21},{6,22},{7,23},{8,24},{9,... | collective-permute-start | bytes 294920 | tf_op jit(solution)/shard_map/ppermute | solution.py:566
  30.5 8.0 %collective-permute-start.10 = (f32[96,256]{1,0:T(8,128)S(1)}, f32[96,256]{1,0:T(8,128)S(1)}, u32[]{:S(2)}, u32[]{:S(2)}) collective-permute-start(f32[96,256]{1,0:T(8,128)S(1)} %get-tuple-element.63), channel_id=1, source_target_pairs={{0,1},{1,0},{2,3},{3,2},{4,5},{5,4},{6,7},{7,6},{8,9},{9,8},{10,11... | collective-permute-start | bytes 294920 | tf_op jit(solution)/shard_map/ppermute | solution.py:566
  32.0 6.5 %collective-permute-start.11 = (f32[96,256]{1,0:T(8,128)S(1)}, f32[96,256]{1,0:T(8,128)S(1)}, u32[]{:S(2)}, u32[]{:S(2)}) collective-permute-start(f32[96,256]{1,0:T(8,128)S(1)} %get-tuple-element.64), channel_id=1, source_target_pairs={{0,17},{1,16},{2,19},{3,18},{4,21},{5,20},{6,23},{7,22},{8,25},{9,... | collective-permute-start | bytes 294920 | tf_op jit(solution)/shard_map/ppermute | solution.py:566
  33.8 4.8 %collective-permute-start.7 = (f32[32,512]{1,0:T(8,128)S(1)}, f32[32,512]{1,0:T(8,128)S(1)}, u32[]{:S(2)}, u32[]{:S(2)}) collective-permute-start(f32[32,512]{1,0:T(8,128)S(1)} %add_add_fusion.4), channel_id=1, source_target_pairs={{0,1},{1,0},{2,3},{3,2},{4,5},{5,4},{6,7},{7,6},{8,9},{9,8},{10,11... | collective-permute-start | bytes 196616 | tf_op jit(solution)/shard_map/ppermute | solution.py:566
  42.6 7.0 %collective-permute-start.23 = (f32[96,256]{1,0:T(8,128)S(1)}, f32[96,256]{1,0:T(8,128)S(1)}, u32[]{:S(2)}, u32[]{:S(2)}) collective-permute-start(f32[96,256]{1,0:T(8,128)S(1)} %add_add_fusion), channel_id=1, source_target_pairs={{0,4},{1,5},{2,6},{3,7},{4,0},{5,1},{6,2},{7,3},{8,10},{9,11},{10,... | collective-permute-start | bytes 294920 | tf_op jit(solution)/shard_map/ppermute | solution.py:566
  46.0 5.2 %collective-permute-start.13 = (f32[72,256]{1,0:T(8,128)S(1)}, f32[72,256]{1,0:T(8,128)S(1)}, u32[]{:S(2)}, u32[]{:S(2)}) collective-permute-start(f32[72,256]{1,0:T(8,128)S(1)} %get-tuple-element.78), channel_id=1, source_target_pairs={{0,16},{1,17},{2,18},{3,19},{4,20},{5,21},{6,22},{7,23},{8,24},{9,... | collective-permute-start | bytes 221192 | tf_op jit(solution)/shard_map/ppermute | solution.py:566
  46.6 4.8 %collective-permute-start.14 = (f32[72,256]{1,0:T(8,128)S(1)}, f32[72,256]{1,0:T(8,128)S(1)}, u32[]{:S(2)}, u32[]{:S(2)}) collective-permute-start(f32[72,256]{1,0:T(8,128)S(1)} %get-tuple-element.79), channel_id=1, source_target_pairs={{0,1},{1,0},{2,3},{3,2},{4,5},{5,4},{6,7},{7,6},{8,9},{9,8},{10,11... | collective-permute-start | bytes 221192 | tf_op jit(solution)/shard_map/ppermute | solution.py:566
  47.8 5.3 %collective-permute-start.15 = (f32[72,256]{1,0:T(8,128)S(1)}, f32[72,256]{1,0:T(8,128)S(1)}, u32[]{:S(2)}, u32[]{:S(2)}) collective-permute-start(f32[72,256]{1,0:T(8,128)S(1)} %get-tuple-element.80), channel_id=1, source_target_pairs={{0,17},{1,16},{2,19},{3,18},{4,21},{5,20},{6,23},{7,22},{8,25},{9,... | collective-permute-start | bytes 221192 | tf_op jit(solution)/shard_map/ppermute | solution.py:566
  49.6 7.9 %collective-permute-start.24 = (f32[96,256]{1,0:T(8,128)S(1)}, f32[96,256]{1,0:T(8,128)S(1)}, u32[]{:S(2)}, u32[]{:S(2)}) collective-permute-start(f32[96,256]{1,0:T(8,128)S(1)} %add.74), channel_id=1, source_target_pairs={{0,2},{1,3},{2,0},{3,1},{4,6},{5,7},{6,4},{7,5},{8,12},{9,13},{10,... | collective-permute-start | bytes 294920 | tf_op jit(solution)/shard_map/ppermute | solution.py:566
  53.0 7.4 %collective-permute-start.18 = (f32[72,256]{1,0:T(8,128)S(1)}, f32[72,256]{1,0:T(8,128)S(1)}, u32[]{:S(2)}, u32[]{:S(2)}) collective-permute-start(f32[72,256]{1,0:T(8,128)S(1)} %add_add_fusion.2), channel_id=1, source_target_pairs={{0,6},{1,7},{2,4},{3,5},{4,2},{5,3},{6,0},{7,1},{8,14},{9,15},{10,... | collective-permute-start | bytes 221192 | tf_op jit(solution)/shard_map/ppermute | solution.py:566
  54.9 6.8 %collective-permute-start.17 = (f32[72,256]{1,0:T(8,128)S(1)}, f32[72,256]{1,0:T(8,128)S(1)}, u32[]{:S(2)}, u32[]{:S(2)}) collective-permute-start(f32[72,256]{1,0:T(8,128)S(1)} %add_add_fusion.2), channel_id=1, source_target_pairs={{0,4},{1,5},{2,6},{3,7},{4,0},{5,1},{6,2},{7,3},{8,12},{9,13},{10,... | collective-permute-start | bytes 221192 | tf_op jit(solution)/shard_map/ppermute | solution.py:566
  56.5 5.2 %collective-permute-start.16 = (f32[72,256]{1,0:T(8,128)S(1)}, f32[72,256]{1,0:T(8,128)S(1)}, u32[]{:S(2)}, u32[]{:S(2)}) collective-permute-start(f32[72,256]{1,0:T(8,128)S(1)} %add_add_fusion.2), channel_id=1, source_target_pairs={{0,2},{1,3},{2,0},{3,1},{4,6},{5,7},{6,4},{7,5},{8,10},{9,11},{10,... | collective-permute-start | bytes 221192 | tf_op jit(solution)/shard_map/ppermute | solution.py:566
  57.5 6.8 %collective-permute-start.27 = (f32[96,256]{1,0:T(8,128)S(1)}, f32[96,256]{1,0:T(8,128)S(1)}, u32[]{:S(2)}, u32[]{:S(2)}) collective-permute-start(f32[96,256]{1,0:T(8,128)S(1)} %add.75), channel_id=1, source_target_pairs={{0,17},{1,16},{2,19},{3,18},{4,21},{5,20},{6,23},{7,22},{8,25},{9,... | collective-permute-start | bytes 294920 | tf_op jit(solution)/shard_map/ppermute | solution.py:566
  59.4 5.9 %collective-permute-start.26 = (f32[96,256]{1,0:T(8,128)S(1)}, f32[96,256]{1,0:T(8,128)S(1)}, u32[]{:S(2)}, u32[]{:S(2)}) collective-permute-start(f32[96,256]{1,0:T(8,128)S(1)} %add.75), channel_id=1, source_target_pairs={{0,1},{1,0},{2,3},{3,2},{4,5},{5,4},{6,7},{7,6},{8,9},{9,8},{10,11... | collective-permute-start | bytes 294920 | tf_op jit(solution)/shard_map/ppermute | solution.py:566
  60.4 6.9 %collective-permute-start.25 = (f32[96,256]{1,0:T(8,128)S(1)}, f32[96,256]{1,0:T(8,128)S(1)}, u32[]{:S(2)}, u32[]{:S(2)}) collective-permute-start(f32[96,256]{1,0:T(8,128)S(1)} %add.75), channel_id=1, source_target_pairs={{0,16},{1,17},{2,18},{3,19},{4,20},{5,21},{6,22},{7,23},{8,24},{9,... | collective-permute-start | bytes 294920 | tf_op jit(solution)/shard_map/ppermute | solution.py:566
  61.7 5.7 %collective-permute-start.21 = (f32[72,256]{1,0:T(8,128)S(1)}, f32[72,256]{1,0:T(8,128)S(1)}, u32[]{:S(2)}, u32[]{:S(2)}) collective-permute-start(f32[72,256]{1,0:T(8,128)S(1)} %add_add_fusion.1), channel_id=1, source_target_pairs={{0,17},{1,16},{2,19},{3,18},{4,21},{5,20},{6,23},{7,22},{8,25},{9,... | collective-permute-start | bytes 221192 | tf_op jit(solution)/shard_map/ppermute | solution.py:566
  (17 other events, 182.6 us)

commit v8 on v7

--- a/solution.py
+++ b/solution.py
@@ -159,10 +159,10 @@
             head = g * GROUP + i
             scale = jnp.full((1, points), temper[head], F32)
             temper_rows[head : head + 1] = scale
-            scaled = logits[i * slices : (i + 1) * slices] / scale
+            scaled = logits[i * slices : (i + 1) * slices] * (1.0 / scale)
             scaled = scaled - jnp.max(scaled, axis=0, keepdims=True)
             grown = jnp.exp(scaled)
-            parts.append(grown / jnp.sum(grown, axis=0, keepdims=True))
+            parts.append(grown * (1.0 / jnp.sum(grown, axis=0, keepdims=True)))
         weights = split(jnp.concatenate(parts, axis=0))
         span = slice(g * GROUP * slices, (g + 1) * GROUP * slices)
         weight_h[span], weight_l[span] = weights
@@ -262,7 +262,7 @@
         scores = jnp.where(same, scores, -1e30)
         scores = scores - jnp.max(scores, axis=0, keepdims=True)
         grown = jnp.where(same, jnp.exp(scores), 0.0)
-        probs = grown / jnp.sum(grown, axis=0, keepdims=True)
+        probs = grown * (1.0 / jnp.sum(grown, axis=0, keepdims=True))
         attn[:, span] = probs
         results.append(product(v, split(probs), 1, 0))
     result = jnp.concatenate(results, axis=1)
@@ -451,7 +451,7 @@
             w = weights[0][block].astype(F32) + weights[1][block].astype(F32)
             weighted = w * weight_grad[block]
             total = jnp.sum(weighted, axis=0, keepdims=True)
-            grads.append((weighted - w * total) / scale)
+            grads.append((weighted - w * total) * (1.0 / scale))
         grads = split(jnp.concatenate(grads, axis=0))
         assign_grads.append(product(logit_blocks, grads, 1, 0))
         full = product((assign_h[piece], assign_l[piece]), grads, 1, 1)
@@ -514,10 +514,7 @@
     width = gain.shape[1]
     head_size, slices = logit.shape
     base = 2 * width
-    for i in range(3):
-        maps[i] = late[base : base + head_size, i * head_size : (i + 1) * head_size]
-    logit[...] = late[base : base + head_size, 128 : 128 + slices]
-    copies = fetch((maps, logit), (maps_out, logit_out), sems)
+    copies = []
     gain_column = column(gain[...])
     total = jnp.zeros((1, width), F32)
     for i, weight in enumerate((fx_weight, x_weight)):
@@ -525,6 +522,10 @@
         copy = pltpu.make_async_copy(scaled.at[i], matrices.at[i], sems.at[2 + i])
         copy.start()
         copies.append(copy)
+    for i in range(3):
+        maps[i] = late[base : base + head_size, i * head_size : (i + 1) * head_size]
+    logit[...] = late[base : base + head_size, 128 : 128 + slices]
+    copies += fetch((maps, logit), (maps_out, logit_out), sems)
     for i, weight in enumerate((fx_weight, x_weight)):
         total = total + row_total(late[i * width : (i + 1) * width], weight[...])
     gains[...] = jnp.concatenate([total, gain_row[...]], axis=0)

time: 71.6 us -> 71.6 us (level)
  no operation moved by 1% of the time
where the time goes in v8:
time: 71.6 us; the launch traced here: 71.5 us
  starting transfers between devices  36.8 us (51%)
  Pallas kernels  17.1 us (24%)
  waiting for transfers between devices  16.4 us (23%)
  between operations  0.96 us (1%)
    ppermute x29, starting transfers between devices, swap(): return lax.ppermute(value, ('dp', 'point'), pairs)  36.8 us
    pallas_call x10, Pallas kernels, call(): pl.pallas_call(body, name=name, in_specs=in_specs, out_specs=out_specs, o...  17.1 us
    ppermute x29, waiting for transfers between devices, swap(): return lax.ppermute(value, ('dp', 'point'), pairs)  16.4 us
  transfers between devices with their start and end apart: 29, of which 12 were waited for; matrix products, arithmetic and copies ran while one was open for 0% of the time, Pallas kernels for 5%

profile of v8, /device:TPU:0, one launch (start us, length us, event | category | flops | bytes accessed | tf_op | source)
XLA Modules:
  0.0 71.5 jit_solution(4114715074735116829)
XLA Ops:
  0.7 4.0 %front.1 = (bf16[3072,512]{1,0:T(8,128)(2,1)S(1)}, f32[272,512]{1,0:T(8,128)S(1)}, f32[136,128]{1,0:T(8,128)S(1)}) custom-call(f32[1,512,256]{2,1,0:T(8,128)} %x_hbm.1, f32[1,256]{1,0:T(1,128)} %bitcast.4, f32[256,256]{1,0:T(8,128)} %fx_weight.1, f32[256,256]{1,0:T(8,128)} %x_weight.1, f32[32,64]{1,0:T(8,128)} %logit_weight.1, f32[8]{0:T(128)} %temper_hbm.1), custom_call_target="tpu_custom_call" | custom-call | flops 805306368 | bytes 1048576 | tf_op jit(solution)/shard_map/front/pallas_call | solution.py:547
  4.8 3.0 %collective-permute-start = (f32[136,128]{1,0:T(8,128)S(1)}, f32[136,128]{1,0:T(8,128)S(1)}, u32[]{:S(2)}, u32[]{:S(2)}) collective-permute-start(f32[136,128]{1,0:T(8,128)S(1)} %get-tuple-element.47), channel_id=1, source_target_pairs={{0,1},{1,0},{2,3},{3,2},{4,5},{5,4},{6,7},{7,6},{8,9},{9,8},{10,11... | collective-permute-start | bytes 208904 | tf_op jit(solution)/shard_map/ppermute | solution.py:567
  7.8 2.3 %collective-permute-done = f32[136,128]{1,0:T(8,128)S(1)} collective-permute-done((f32[136,128]{1,0:T(8,128)S(1)}, f32[136,128]{1,0:T(8,128)S(1)}, u32[]{:S(2)}, u32[]{:S(2)}) %collective-permute-start) | collective-permute-done | bytes 69664 | tf_op jit(solution)/shard_map/ppermute | solution.py:567
  10.1 4.2 %collective-permute-start.3 = (f32[136,128]{1,0:T(8,128)S(1)}, f32[136,128]{1,0:T(8,128)S(1)}, u32[]{:S(2)}, u32[]{:S(2)}) collective-permute-start(f32[136,128]{1,0:T(8,128)S(1)} %add.57), channel_id=1, source_target_pairs={{0,6},{1,7},{2,4},{3,5},{4,2},{5,3},{6,0},{7,1},{8,14},{9,15},{10,... | collective-permute-start | bytes 208904 | tf_op jit(solution)/shard_map/ppermute | solution.py:567
  16.8 2.9 %collective-permute-done.2 = f32[136,128]{1,0:T(8,128)S(1)} collective-permute-done((f32[136,128]{1,0:T(8,128)S(1)}, f32[136,128]{1,0:T(8,128)S(1)}, u32[]{:S(2)}, u32[]{:S(2)}) %collective-permute-start.2) | collective-permute-done | bytes 69664 | tf_op jit(solution)/shard_map/ppermute | solution.py:567
  19.7 3.8 %back.1 = (f32[32,512]{1,0:T(8,128)S(1)}, bf16[3072,512]{1,0:T(8,128)(2,1)S(1)}, f32[680,512]{1,0:T(8,128)S(1)}) custom-call(f32[136,128]{1,0:T(8,128)S(1)} %add_add_fusion.3.sums, bf16[3072,512]{1,0:T(8,128)(2,1)S(1)} %get-tuple-element.48.front, f32[272,512]{1,0:T(8,128)S(1)} %get-tuple-element.49.front_wide, ...), custom_call_target="tpu_custom_call" | custom-call | flops 1207959552 | bytes 1048576 | tf_op jit(solution)/shard_map/back/pallas_call | solution.py:547
  24.4 2.2 %collective-permute-start.6 = (f32[32,512]{1,0:T(8,128)S(1)}, f32[32,512]{1,0:T(8,128)S(1)}, u32[]{:S(2)}, u32[]{:S(2)}) collective-permute-start(f32[32,512]{1,0:T(8,128)S(1)} %get-tuple-element.57), channel_id=1, source_target_pairs={{0,6},{1,7},{2,4},{3,5},{4,2},{5,3},{6,0},{7,1},{8,14},{9,15},{10,... | collective-permute-start | bytes 196616 | tf_op jit(solution)/shard_map/ppermute | solution.py:567
  26.7 2.2 %collective-permute-start.4 = (f32[32,512]{1,0:T(8,128)S(1)}, f32[32,512]{1,0:T(8,128)S(1)}, u32[]{:S(2)}, u32[]{:S(2)}) collective-permute-start(f32[32,512]{1,0:T(8,128)S(1)} %get-tuple-element.57), channel_id=1, source_target_pairs={{0,2},{1,3},{2,0},{3,1},{4,6},{5,7},{6,4},{7,5},{8,10},{9,11},{10,... | collective-permute-start | bytes 196616 | tf_op jit(solution)/shard_map/ppermute | solution.py:567
  28.9 1.6 %collective-permute-start.9 = (f32[96,256]{1,0:T(8,128)S(1)}, f32[96,256]{1,0:T(8,128)S(1)}, u32[]{:S(2)}, u32[]{:S(2)}) collective-permute-start(f32[96,256]{1,0:T(8,128)S(1)} %get-tuple-element.62), channel_id=1, source_target_pairs={{0,16},{1,17},{2,18},{3,19},{4,20},{5,21},{6,22},{7,23},{8,24},{9,... | collective-permute-start | bytes 294920 | tf_op jit(solution)/shard_map/ppermute | solution.py:567
  30.5 1.5 %collective-permute-start.10 = (f32[96,256]{1,0:T(8,128)S(1)}, f32[96,256]{1,0:T(8,128)S(1)}, u32[]{:S(2)}, u32[]{:S(2)}) collective-permute-start(f32[96,256]{1,0:T(8,128)S(1)} %get-tuple-element.63), channel_id=1, source_target_pairs={{0,1},{1,0},{2,3},{3,2},{4,5},{5,4},{6,7},{7,6},{8,9},{9,8},{10,11... | collective-permute-start | bytes 294920 | tf_op jit(solution)/shard_map/ppermute | solution.py:567
  32.0 1.7 %collective-permute-start.11 = (f32[96,256]{1,0:T(8,128)S(1)}, f32[96,256]{1,0:T(8,128)S(1)}, u32[]{:S(2)}, u32[]{:S(2)}) collective-permute-start(f32[96,256]{1,0:T(8,128)S(1)} %get-tuple-element.64), channel_id=1, source_target_pairs={{0,17},{1,16},{2,19},{3,18},{4,21},{5,20},{6,23},{7,22},{8,25},{9,... | collective-permute-start | bytes 294920 | tf_op jit(solution)/shard_map/ppermute | solution.py:567
  33.8 1.4 %collective-permute-start.7 = (f32[32,512]{1,0:T(8,128)S(1)}, f32[32,512]{1,0:T(8,128)S(1)}, u32[]{:S(2)}, u32[]{:S(2)}) collective-permute-start(f32[32,512]{1,0:T(8,128)S(1)} %add_add_fusion.4), channel_id=1, source_target_pairs={{0,1},{1,0},{2,3},{3,2},{4,5},{5,4},{6,7},{7,6},{8,9},{9,8},{10,11... | collective-permute-start | bytes 196616 | tf_op jit(solution)/shard_map/ppermute | solution.py:567
  35.1 3.4 %collective-permute-done.7 = f32[32,512]{1,0:T(8,128)S(1)} collective-permute-done((f32[32,512]{1,0:T(8,128)S(1)}, f32[32,512]{1,0:T(8,128)S(1)}, u32[]{:S(2)}, u32[]{:S(2)}) %collective-permute-start.7) | collective-permute-done | bytes 65568 | tf_op jit(solution)/shard_map/ppermute | solution.py:567
  38.6 3.9 %end.1 = (f32[288,256]{1,0:T(8,128)S(1)}, f32[288,256]{1,0:T(8,128)S(1)}, bf16[1024,512]{1,0:T(8,128)(2,1)S(1)}) custom-call(f32[32,512]{1,0:T(8,128)S(1)} %add.64.out_sum, bf16[3072,512]{1,0:T(8,128)(2,1)S(1)} %get-tuple-element.48.front, f32[272,512]{1,0:T(8,128)S(1)} %get-tuple-element.49.front_wide, bf16[2560,256]{1,0:T(8,128)(2,1)S(1)} %get-tuple-element.56.map_packed, ...), custom_call_target="tpu_custom_call" | custom-call | flops 1610612736 | bytes 1048576 | tf_op jit(solution)/shard_map/end/pallas_call | solution.py:547
  42.6 1.8 %collective-permute-start.23 = (f32[96,256]{1,0:T(8,128)S(1)}, f32[96,256]{1,0:T(8,128)S(1)}, u32[]{:S(2)}, u32[]{:S(2)}) collective-permute-start(f32[96,256]{1,0:T(8,128)S(1)} %add_add_fusion), channel_id=1, source_target_pairs={{0,4},{1,5},{2,6},{3,7},{4,0},{5,1},{6,2},{7,3},{8,10},{9,11},{10,... | collective-permute-start | bytes 294920 | tf_op jit(solution)/shard_map/ppermute | solution.py:567
  44.4 1.6 %rows.1 = f32[1,512,256]{2,1,0:T(8,128)} custom-call(bf16[3072,512]{1,0:T(8,128)(2,1)S(1)} %get-tuple-element.48.front, f32[272,512]{1,0:T(8,128)S(1)} %get-tuple-element.49.front_wide, f32[680,512]{1,0:T(8,128)S(1)} %get-tuple-element.66.back_wide, bf16[1024,512]{1,0:T(8,128)(2,1)S(1)} %get-tuple-element.75.end), custom_call_target="tpu_custom_call" | custom-call | flops 402653184 | bytes 1048576 | tf_op jit(solution)/shard_map/rows/pallas_call | solution.py:547
  47.8 1.8 %collective-permute-start.15 = (f32[72,256]{1,0:T(8,128)S(1)}, f32[72,256]{1,0:T(8,128)S(1)}, u32[]{:S(2)}, u32[]{:S(2)}) collective-permute-start(f32[72,256]{1,0:T(8,128)S(1)} %get-tuple-element.80), channel_id=1, source_target_pairs={{0,17},{1,16},{2,19},{3,18},{4,21},{5,20},{6,23},{7,22},{8,25},{9,... | collective-permute-start | bytes 221192 | tf_op jit(solution)/shard_map/ppermute | solution.py:567
  51.4 1.6 %collective-permute-done.15 = f32[72,256]{1,0:T(8,128)S(1)} collective-permute-done((f32[72,256]{1,0:T(8,128)S(1)}, f32[72,256]{1,0:T(8,128)S(1)}, u32[]{:S(2)}, u32[]{:S(2)}) %collective-permute-start.15) | collective-permute-done | bytes 73760 | tf_op jit(solution)/shard_map/ppermute | solution.py:567
  53.0 1.9 %collective-permute-start.18 = (f32[72,256]{1,0:T(8,128)S(1)}, f32[72,256]{1,0:T(8,128)S(1)}, u32[]{:S(2)}, u32[]{:S(2)}) collective-permute-start(f32[72,256]{1,0:T(8,128)S(1)} %add_add_fusion.2), channel_id=1, source_target_pairs={{0,6},{1,7},{2,4},{3,5},{4,2},{5,3},{6,0},{7,1},{8,14},{9,15},{10,... | collective-permute-start | bytes 221192 | tf_op jit(solution)/shard_map/ppermute | solution.py:567
  54.9 1.6 %collective-permute-start.17 = (f32[72,256]{1,0:T(8,128)S(1)}, f32[72,256]{1,0:T(8,128)S(1)}, u32[]{:S(2)}, u32[]{:S(2)}) collective-permute-start(f32[72,256]{1,0:T(8,128)S(1)} %add_add_fusion.2), channel_id=1, source_target_pairs={{0,4},{1,5},{2,6},{3,7},{4,0},{5,1},{6,2},{7,3},{8,12},{9,13},{10,... | collective-permute-start | bytes 221192 | tf_op jit(solution)/shard_map/ppermute | solution.py:567
  57.5 1.9 %collective-permute-start.27 = (f32[96,256]{1,0:T(8,128)S(1)}, f32[96,256]{1,0:T(8,128)S(1)}, u32[]{:S(2)}, u32[]{:S(2)}) collective-permute-start(f32[96,256]{1,0:T(8,128)S(1)} %add.75), channel_id=1, source_target_pairs={{0,17},{1,16},{2,19},{3,18},{4,21},{5,20},{6,23},{7,22},{8,25},{9,... | collective-permute-start | bytes 294920 | tf_op jit(solution)/shard_map/ppermute | solution.py:567
  61.7 1.3 %collective-permute-start.21 = (f32[72,256]{1,0:T(8,128)S(1)}, f32[72,256]{1,0:T(8,128)S(1)}, u32[]{:S(2)}, u32[]{:S(2)}) collective-permute-start(f32[72,256]{1,0:T(8,128)S(1)} %add_add_fusion.1), channel_id=1, source_target_pairs={{0,17},{1,16},{2,19},{3,18},{4,21},{5,20},{6,23},{7,22},{8,25},{9,... | collective-permute-start | bytes 221192 | tf_op jit(solution)/shard_map/ppermute | solution.py:567
  63.1 1.2 %collective-permute-start.20 = (f32[72,256]{1,0:T(8,128)S(1)}, f32[72,256]{1,0:T(8,128)S(1)}, u32[]{:S(2)}, u32[]{:S(2)}) collective-permute-start(f32[72,256]{1,0:T(8,128)S(1)} %add_add_fusion.1), channel_id=1, source_target_pairs={{0,1},{1,0},{2,3},{3,2},{4,5},{5,4},{6,7},{7,6},{8,9},{9,8},{10,11... | collective-permute-start | bytes 221192 | tf_op jit(solution)/shard_map/ppermute | solution.py:567
  65.3 2.0 %collective-permute-done.25 = f32[96,256]{1,0:T(8,128)S(1)} collective-permute-done((f32[96,256]{1,0:T(8,128)S(1)}, f32[96,256]{1,0:T(8,128)S(1)}, u32[]{:S(2)}, u32[]{:S(2)}) %collective-permute-start.25) | collective-permute-done | bytes 98336 | tf_op jit(solution)/shard_map/ppermute | solution.py:567
  (79 shorter events, 15.6 us)
Async XLA Ops:
  4.8 5.3 %collective-permute-start = (f32[136,128]{1,0:T(8,128)S(1)}, f32[136,128]{1,0:T(8,128)S(1)}, u32[]{:S(2)}, u32[]{:S(2)}) collective-permute-start(f32[136,128]{1,0:T(8,128)S(1)} %get-tuple-element.47), channel_id=1, source_target_pairs={{0,1},{1,0},{2,3},{3,2},{4,5},{5,4},{6,7},{7,6},{8,9},{9,8},{10,11... | collective-permute-start | bytes 208904 | tf_op jit(solution)/shard_map/ppermute | solution.py:567
  10.1 6.7 %collective-permute-start.3 = (f32[136,128]{1,0:T(8,128)S(1)}, f32[136,128]{1,0:T(8,128)S(1)}, u32[]{:S(2)}, u32[]{:S(2)}) collective-permute-start(f32[136,128]{1,0:T(8,128)S(1)} %add.57), channel_id=1, source_target_pairs={{0,6},{1,7},{2,4},{3,5},{4,2},{5,3},{6,0},{7,1},{8,14},{9,15},{10,... | collective-permute-start | bytes 208904 | tf_op jit(solution)/shard_map/ppermute | solution.py:567
  14.3 5.4 %collective-permute-start.2 = (f32[136,128]{1,0:T(8,128)S(1)}, f32[136,128]{1,0:T(8,128)S(1)}, u32[]{:S(2)}, u32[]{:S(2)}) collective-permute-start(f32[136,128]{1,0:T(8,128)S(1)} %add.57), channel_id=1, source_target_pairs={{0,4},{1,5},{2,6},{3,7},{4,0},{5,1},{6,2},{7,3},{8,12},{9,13},{10,... | collective-permute-start | bytes 208904 | tf_op jit(solution)/shard_map/ppermute | solution.py:567
  14.3 5.4 %collective-permute-start.1 = (f32[136,128]{1,0:T(8,128)S(1)}, f32[136,128]{1,0:T(8,128)S(1)}, u32[]{:S(2)}, u32[]{:S(2)}) collective-permute-start(f32[136,128]{1,0:T(8,128)S(1)} %add.57), channel_id=1, source_target_pairs={{0,2},{1,3},{2,0},{3,1},{4,6},{5,7},{6,4},{7,5},{8,10},{9,11},{10,... | collective-permute-start | bytes 208904 | tf_op jit(solution)/shard_map/ppermute | solution.py:567
  24.4 4.5 %collective-permute-start.8 = (f32[384,256]{1,0:T(8,128)S(1)}, f32[384,256]{1,0:T(8,128)S(1)}, u32[]{:S(2)}, u32[]{:S(2)}) collective-permute-start(f32[384,256]{1,0:T(8,128)S(1)} %get-tuple-element.60), channel_id=1, source_target_pairs={{0,8},{1,9},{2,10},{3,11},{4,12},{5,13},{6,14},{7,15},{8,0},{9,1},... | collective-permute-start | bytes 1179656 | tf_op jit(solution)/shard_map/ppermute | solution.py:567
  24.4 7.6 %collective-permute-start.6 = (f32[32,512]{1,0:T(8,128)S(1)}, f32[32,512]{1,0:T(8,128)S(1)}, u32[]{:S(2)}, u32[]{:S(2)}) collective-permute-start(f32[32,512]{1,0:T(8,128)S(1)} %get-tuple-element.57), channel_id=1, source_target_pairs={{0,6},{1,7},{2,4},{3,5},{4,2},{5,3},{6,0},{7,1},{8,14},{9,15},{10,... | collective-permute-start | bytes 196616 | tf_op jit(solution)/shard_map/ppermute | solution.py:567
  26.7 7.1 %collective-permute-start.5 = (f32[32,512]{1,0:T(8,128)S(1)}, f32[32,512]{1,0:T(8,128)S(1)}, u32[]{:S(2)}, u32[]{:S(2)}) collective-permute-start(f32[32,512]{1,0:T(8,128)S(1)} %get-tuple-element.57), channel_id=1, source_target_pairs={{0,4},{1,5},{2,6},{3,7},{4,0},{5,1},{6,2},{7,3},{8,12},{9,13},{10,... | collective-permute-start | bytes 196616 | tf_op jit(solution)/shard_map/ppermute | solution.py:567
  26.7 7.1 %collective-permute-start.4 = (f32[32,512]{1,0:T(8,128)S(1)}, f32[32,512]{1,0:T(8,128)S(1)}, u32[]{:S(2)}, u32[]{:S(2)}) collective-permute-start(f32[32,512]{1,0:T(8,128)S(1)} %get-tuple-element.57), channel_id=1, source_target_pairs={{0,2},{1,3},{2,0},{3,1},{4,6},{5,7},{6,4},{7,5},{8,10},{9,11},{10,... | collective-permute-start | bytes 196616 | tf_op jit(solution)/shard_map/ppermute | solution.py:567
  28.9 9.6 %collective-permute-start.9 = (f32[96,256]{1,0:T(8,128)S(1)}, f32[96,256]{1,0:T(8,128)S(1)}, u32[]{:S(2)}, u32[]{:S(2)}) collective-permute-start(f32[96,256]{1,0:T(8,128)S(1)} %get-tuple-element.62), channel_id=1, source_target_pairs={{0,16},{1,17},{2,18},{3,19},{4,20},{5,21},{6,22},{7,23},{8,24},{9,... | collective-permute-start | bytes 294920 | tf_op jit(solution)/shard_map/ppermute | solution.py:567
  30.5 8.0 %collective-permute-start.10 = (f32[96,256]{1,0:T(8,128)S(1)}, f32[96,256]{1,0:T(8,128)S(1)}, u32[]{:S(2)}, u32[]{:S(2)}) collective-permute-start(f32[96,256]{1,0:T(8,128)S(1)} %get-tuple-element.63), channel_id=1, source_target_pairs={{0,1},{1,0},{2,3},{3,2},{4,5},{5,4},{6,7},{7,6},{8,9},{9,8},{10,11... | collective-permute-start | bytes 294920 | tf_op jit(solution)/shard_map/ppermute | solution.py:567
  32.0 6.5 %collective-permute-start.11 = (f32[96,256]{1,0:T(8,128)S(1)}, f32[96,256]{1,0:T(8,128)S(1)}, u32[]{:S(2)}, u32[]{:S(2)}) collective-permute-start(f32[96,256]{1,0:T(8,128)S(1)} %get-tuple-element.64), channel_id=1, source_target_pairs={{0,17},{1,16},{2,19},{3,18},{4,21},{5,20},{6,23},{7,22},{8,25},{9,... | collective-permute-start | bytes 294920 | tf_op jit(solution)/shard_map/ppermute | solution.py:567
  33.8 4.8 %collective-permute-start.7 = (f32[32,512]{1,0:T(8,128)S(1)}, f32[32,512]{1,0:T(8,128)S(1)}, u32[]{:S(2)}, u32[]{:S(2)}) collective-permute-start(f32[32,512]{1,0:T(8,128)S(1)} %add_add_fusion.4), channel_id=1, source_target_pairs={{0,1},{1,0},{2,3},{3,2},{4,5},{5,4},{6,7},{7,6},{8,9},{9,8},{10,11... | collective-permute-start | bytes 196616 | tf_op jit(solution)/shard_map/ppermute | solution.py:567
  42.6 7.0 %collective-permute-start.23 = (f32[96,256]{1,0:T(8,128)S(1)}, f32[96,256]{1,0:T(8,128)S(1)}, u32[]{:S(2)}, u32[]{:S(2)}) collective-permute-start(f32[96,256]{1,0:T(8,128)S(1)} %add_add_fusion), channel_id=1, source_target_pairs={{0,4},{1,5},{2,6},{3,7},{4,0},{5,1},{6,2},{7,3},{8,10},{9,11},{10,... | collective-permute-start | bytes 294920 | tf_op jit(solution)/shard_map/ppermute | solution.py:567
  46.0 5.2 %collective-permute-start.13 = (f32[72,256]{1,0:T(8,128)S(1)}, f32[72,256]{1,0:T(8,128)S(1)}, u32[]{:S(2)}, u32[]{:S(2)}) collective-permute-start(f32[72,256]{1,0:T(8,128)S(1)} %get-tuple-element.78), channel_id=1, source_target_pairs={{0,16},{1,17},{2,18},{3,19},{4,20},{5,21},{6,22},{7,23},{8,24},{9,... | collective-permute-start | bytes 221192 | tf_op jit(solution)/shard_map/ppermute | solution.py:567
  46.6 4.8 %collective-permute-start.14 = (f32[72,256]{1,0:T(8,128)S(1)}, f32[72,256]{1,0:T(8,128)S(1)}, u32[]{:S(2)}, u32[]{:S(2)}) collective-permute-start(f32[72,256]{1,0:T(8,128)S(1)} %get-tuple-element.79), channel_id=1, source_target_pairs={{0,1},{1,0},{2,3},{3,2},{4,5},{5,4},{6,7},{7,6},{8,9},{9,8},{10,11... | collective-permute-start | bytes 221192 | tf_op jit(solution)/shard_map/ppermute | solution.py:567
  47.8 5.3 %collective-permute-start.15 = (f32[72,256]{1,0:T(8,128)S(1)}, f32[72,256]{1,0:T(8,128)S(1)}, u32[]{:S(2)}, u32[]{:S(2)}) collective-permute-start(f32[72,256]{1,0:T(8,128)S(1)} %get-tuple-element.80), channel_id=1, source_target_pairs={{0,17},{1,16},{2,19},{3,18},{4,21},{5,20},{6,23},{7,22},{8,25},{9,... | collective-permute-start | bytes 221192 | tf_op jit(solution)/shard_map/ppermute | solution.py:567
  49.6 7.9 %collective-permute-start.24 = (f32[96,256]{1,0:T(8,128)S(1)}, f32[96,256]{1,0:T(8,128)S(1)}, u32[]{:S(2)}, u32[]{:S(2)}) collective-permute-start(f32[96,256]{1,0:T(8,128)S(1)} %add.74), channel_id=1, source_target_pairs={{0,2},{1,3},{2,0},{3,1},{4,6},{5,7},{6,4},{7,5},{8,12},{9,13},{10,... | collective-permute-start | bytes 294920 | tf_op jit(solution)/shard_map/ppermute | solution.py:567
  53.0 7.4 %collective-permute-start.18 = (f32[72,256]{1,0:T(8,128)S(1)}, f32[72,256]{1,0:T(8,128)S(1)}, u32[]{:S(2)}, u32[]{:S(2)}) collective-permute-start(f32[72,256]{1,0:T(8,128)S(1)} %add_add_fusion.2), channel_id=1, source_target_pairs={{0,6},{1,7},{2,4},{3,5},{4,2},{5,3},{6,0},{7,1},{8,14},{9,15},{10,... | collective-permute-start | bytes 221192 | tf_op jit(solution)/shard_map/ppermute | solution.py:567
  54.9 6.8 %collective-permute-start.17 = (f32[72,256]{1,0:T(8,128)S(1)}, f32[72,256]{1,0:T(8,128)S(1)}, u32[]{:S(2)}, u32[]{:S(2)}) collective-permute-start(f32[72,256]{1,0:T(8,128)S(1)} %add_add_fusion.2), channel_id=1, source_target_pairs={{0,4},{1,5},{2,6},{3,7},{4,0},{5,1},{6,2},{7,3},{8,12},{9,13},{10,... | collective-permute-start | bytes 221192 | tf_op jit(solution)/shard_map/ppermute | solution.py:567
  56.5 5.2 %collective-permute-start.16 = (f32[72,256]{1,0:T(8,128)S(1)}, f32[72,256]{1,0:T(8,128)S(1)}, u32[]{:S(2)}, u32[]{:S(2)}) collective-permute-start(f32[72,256]{1,0:T(8,128)S(1)} %add_add_fusion.2), channel_id=1, source_target_pairs={{0,2},{1,3},{2,0},{3,1},{4,6},{5,7},{6,4},{7,5},{8,10},{9,11},{10,... | collective-permute-start | bytes 221192 | tf_op jit(solution)/shard_map/ppermute | solution.py:567
  57.5 6.8 %collective-permute-start.27 = (f32[96,256]{1,0:T(8,128)S(1)}, f32[96,256]{1,0:T(8,128)S(1)}, u32[]{:S(2)}, u32[]{:S(2)}) collective-permute-start(f32[96,256]{1,0:T(8,128)S(1)} %add.75), channel_id=1, source_target_pairs={{0,17},{1,16},{2,19},{3,18},{4,21},{5,20},{6,23},{7,22},{8,25},{9,... | collective-permute-start | bytes 294920 | tf_op jit(solution)/shard_map/ppermute | solution.py:567
  59.4 5.9 %collective-permute-start.26 = (f32[96,256]{1,0:T(8,128)S(1)}, f32[96,256]{1,0:T(8,128)S(1)}, u32[]{:S(2)}, u32[]{:S(2)}) collective-permute-start(f32[96,256]{1,0:T(8,128)S(1)} %add.75), channel_id=1, source_target_pairs={{0,1},{1,0},{2,3},{3,2},{4,5},{5,4},{6,7},{7,6},{8,9},{9,8},{10,11... | collective-permute-start | bytes 294920 | tf_op jit(solution)/shard_map/ppermute | solution.py:567
  60.4 6.9 %collective-permute-start.25 = (f32[96,256]{1,0:T(8,128)S(1)}, f32[96,256]{1,0:T(8,128)S(1)}, u32[]{:S(2)}, u32[]{:S(2)}) collective-permute-start(f32[96,256]{1,0:T(8,128)S(1)} %add.75), channel_id=1, source_target_pairs={{0,16},{1,17},{2,18},{3,19},{4,20},{5,21},{6,22},{7,23},{8,24},{9,... | collective-permute-start | bytes 294920 | tf_op jit(solution)/shard_map/ppermute | solution.py:567
  61.7 5.7 %collective-permute-start.21 = (f32[72,256]{1,0:T(8,128)S(1)}, f32[72,256]{1,0:T(8,128)S(1)}, u32[]{:S(2)}, u32[]{:S(2)}) collective-permute-start(f32[72,256]{1,0:T(8,128)S(1)} %add_add_fusion.1), channel_id=1, source_target_pairs={{0,17},{1,16},{2,19},{3,18},{4,21},{5,20},{6,23},{7,22},{8,25},{9,... | collective-permute-start | bytes 221192 | tf_op jit(solution)/shard_map/ppermute | solution.py:567
  (17 other events, 182.6 us)
